TPU v7x, 32 devices: a whole 2x2x4 slice. The times are simulated.
32 devices in a mesh: enc: 2 (over x), row: 4 (over y, core), col: 4 (over z).
Axes of the slice: x: 2, y: 2, z: 4, core: 2. Of those that a mesh axis runs over, the one named last changes fastest.
Arguments:
- queries: bfloat16 [2560, 3072], P(('row', 'col'), 'enc'), may hold values from -150 to 150
- self_keys: bfloat16 [2560, 3072], P(('row', 'col'), 'enc'), may hold values from -150 to 150
- self_values: bfloat16 [2560, 3072], P(('row', 'col'), 'enc'), may hold values from -6 to 6
- positions: int32 [2560, 3], P(('row', 'col')), may hold values from 0 to 31, as said below
- query_gain: float32 [3072], P('enc'), may hold values from 1.3 to 2
- key_gain: float32 [3072], P('enc'), may hold values from 1.3 to 2
- context_keys: bfloat16 [32, 3072], P(('enc', 'row')), may hold values from -150 to 150
- context_values: bfloat16 [32, 3072], P(('enc', 'row')), may hold values from -6 to 6
- context_gain: float32 [3072], replicated, may hold values from 0.1 to 1.9
- image_cotangent: bfloat16 [2560, 3072], P(('row', 'col'), 'enc'), may hold values from -6 to 6
Outputs:
- self_mixed: bfloat16 [2560, 3072], P(('row', 'col'), 'enc')
- image_mixed: bfloat16 [2560, 3072], P(('row', 'col'), 'enc')
- grad_context_keys: float32 [32, 3072], P(('enc', 'row'))
- grad_context_values: float32 [32, 3072], P(('enc', 'row'))
Inputs may be any that keep to these rules, and one draw needn't show every extreme that they name: `positions`: each (frame, patch row, patch column) of the 5 x 32 x 16 grid appears once; the tokens of one device form one tile of 8 x 4 patches in every frame, in order of frame, row, column; which tile lies on which device is drawn.
All inputs are finite; a program needn't handle non-finite values.
Results may differ from a plain program's by a relative error of at most 0.002.
The roundings to bfloat16 on the way count: a program that leaves them out, or rounds other values in their place, can miss the bound.
Values may be sent and summed in bfloat16 or wider, within the bound.
No kernel may reach another device: no remote copies, remote signals or barrier semaphores. Data moves between devices by JAX's collectives and lax.ppermute only.
A program may use at most 128 MiB of HBM per device.

v0:
```python
import jax
import jax.numpy as jnp
from jax import lax
from jax.sharding import PartitionSpec as P

HEAD_DIM = 128


eps = 1e-06


def rope_angles(positions):
    half = HEAD_DIM // 2
    part_side = HEAD_DIM // 6
    part_time = half - 2 * part_side
    freq_time = 1.0 / 10000.0 ** (jnp.arange(part_time, dtype=jnp.float32) * 2.0 / (2 * part_time))
    freq_side = 1.0 / 10000.0 ** (jnp.arange(part_side, dtype=jnp.float32) * 2.0 / (2 * part_side))
    zeros_side = jnp.zeros((part_side,), jnp.float32)
    zeros_time = jnp.zeros((part_time,), jnp.float32)
    time_row = jnp.concatenate([freq_time, zeros_side, zeros_side])
    height_row = jnp.concatenate([zeros_time, freq_side, zeros_side])
    width_row = jnp.concatenate([zeros_time, zeros_side, freq_side])
    coords = positions.astype(jnp.float32)
    return coords[:, 0:1] * time_row + coords[:, 1:2] * height_row + coords[:, 2:3] * width_row


def pair_turn():
    indices = jnp.arange(HEAD_DIM)
    rows_index = indices[:, None]
    cols_index = indices[None, :]
    plus_entry = (cols_index == rows_index + 1) & (rows_index % 2 == 0)
    minus_entry = (rows_index == cols_index + 1) & (cols_index % 2 == 0)
    return jnp.where(plus_entry, 1.0, jnp.where(minus_entry, -1.0, 0.0)).astype(jnp.float32)


def rotate(normed, angles):
    row_count = normed.shape[0]
    heads_here = normed.shape[1] // HEAD_DIM
    turned = jnp.dot(
        normed.reshape(row_count * heads_here, HEAD_DIM),
        pair_turn(),
        precision=lax.Precision.HIGHEST,
    )
    turned = turned.reshape(row_count, heads_here, HEAD_DIM)
    cosine = jnp.repeat(jnp.cos(angles), 2, axis=1)[:, None, :]
    sine = jnp.repeat(jnp.sin(angles), 2, axis=1)[:, None, :]
    return normed.reshape(row_count, heads_here, HEAD_DIM) * cosine + turned * sine


def per_device(
    queries,
    self_keys,
    self_values,
    positions,
    query_gain,
    key_gain,
    context_keys,
    context_values,
    context_gain,
    image_cotangent,
):
    rows_here = queries.shape[0]
    local_width = queries.shape[1]
    heads_here = local_width // HEAD_DIM
    score_scale = HEAD_DIM ** (-0.5)
    query_wide = queries.astype(jnp.float32)
    key_wide = self_keys.astype(jnp.float32)
    query_total, key_total = lax.psum(
        (jnp.sum(query_wide * query_wide, axis=1), jnp.sum(key_wide * key_wide, axis=1)), "enc"
    )
    full_width = local_width * lax.axis_size("enc")
    query_normed = query_wide * lax.rsqrt(query_total[:, None] / full_width + eps) * query_gain
    key_normed = key_wide * lax.rsqrt(key_total[:, None] / full_width + eps) * key_gain
    angles = rope_angles(positions)
    query_turned = rotate(query_normed, angles).astype(jnp.bfloat16)
    key_turned = rotate(key_normed, angles).astype(jnp.bfloat16).reshape(rows_here, local_width)
    peak_now = jnp.full((heads_here, rows_here), -1e30, jnp.float32)
    accumulated = jnp.zeros((rows_here, heads_here, HEAD_DIM), jnp.float32)
    key_piece = lax.all_gather(key_turned, ("row", "col"), axis=0, tiled=True)
    value_piece = lax.all_gather(self_values, ("row", "col"), axis=0, tiled=True)
    key_count = key_piece.shape[0]
    key_heads = key_piece.reshape(key_count, heads_here, HEAD_DIM)
    value_heads = value_piece.reshape(key_count, heads_here, HEAD_DIM)
    scores = (
        jnp.einsum("qhd,khd->hqk", query_turned, key_heads, preferred_element_type=jnp.float32)
        * score_scale
    )
    newest = jnp.maximum(peak_now, jnp.max(scores, axis=2))
    shrink = jnp.exp(peak_now - newest)
    weights = jnp.exp(scores - newest[:, :, None])
    weight_sum = jnp.sum(weights, axis=2)
    update = jnp.einsum(
        "hqk,khd->qhd",
        weights.astype(jnp.bfloat16),
        value_heads,
        preferred_element_type=jnp.float32,
    )
    accumulated = accumulated * shrink.T[:, :, None] + update
    peak_now, weight_sum, accumulated = (newest, weight_sum, accumulated)
    self_out = (
        (accumulated / weight_sum.T[:, :, None])
        .astype(jnp.bfloat16)
        .reshape(rows_here, local_width)
    )
    query_plain = query_normed.astype(jnp.bfloat16).reshape(rows_here, heads_here, HEAD_DIM)
    context_wide = context_keys.astype(jnp.float32)
    context_recip = lax.rsqrt(jnp.mean(context_wide * context_wide, axis=1, keepdims=True) + eps)
    context_normed = (context_wide * context_recip * context_gain).astype(jnp.bfloat16)
    relayed_keys, relayed_values = (
        lax.all_to_all(context_normed, "enc", split_axis=1, concat_axis=0, tiled=True),
        lax.all_to_all(context_values, "enc", split_axis=1, concat_axis=0, tiled=True),
    )
    cross_keys, cross_values = (
        lax.all_gather(relayed_keys, "row", axis=0, tiled=True),
        lax.all_gather(relayed_values, "row", axis=0, tiled=True),
    )
    context_count = cross_keys.shape[0]
    cross_key_heads = cross_keys.reshape(context_count, heads_here, HEAD_DIM)
    cross_value_heads = cross_values.reshape(context_count, heads_here, HEAD_DIM)
    image_scores = (
        jnp.einsum("qhd,chd->hqc", query_plain, cross_key_heads, preferred_element_type=jnp.float32)
        * score_scale
    )
    image_peak = jnp.max(image_scores, axis=2, keepdims=True)
    image_weights = jnp.exp(image_scores - image_peak)
    probs = image_weights / jnp.sum(image_weights, axis=2, keepdims=True)
    probs_low = probs.astype(jnp.bfloat16)
    image_out = jnp.einsum(
        "hqc,chd->qhd", probs_low, cross_value_heads, preferred_element_type=jnp.float32
    )
    image_out = image_out.astype(jnp.bfloat16).reshape(rows_here, local_width)
    cotangent = image_cotangent.reshape(rows_here, heads_here, HEAD_DIM)
    grad_values = jnp.einsum(
        "hqc,qhd->chd", probs_low, cotangent, preferred_element_type=jnp.float32
    ).reshape(context_count, local_width)
    grad_probs = jnp.einsum(
        "qhd,chd->hqc", cotangent, cross_value_heads, preferred_element_type=jnp.float32
    )
    inner = jnp.sum(probs * grad_probs, axis=2, keepdims=True)
    grad_scores = (probs * (grad_probs - inner)).astype(jnp.bfloat16)
    grad_keys = (
        jnp.einsum("hqc,qhd->chd", grad_scores, query_plain, preferred_element_type=jnp.float32)
        * score_scale
    )
    grad_keys = grad_keys.reshape(context_count, local_width)
    part_keys, part_values = (
        lax.psum_scatter(grad_keys, "row", scatter_dimension=0, tiled=True),
        lax.psum_scatter(grad_values, "row", scatter_dimension=0, tiled=True),
    )
    summed_keys, summed_values = lax.psum((part_keys, part_values), "col")
    back_keys, back_values = (
        lax.all_to_all(summed_keys, "enc", split_axis=0, concat_axis=1, tiled=True),
        lax.all_to_all(summed_values, "enc", split_axis=0, concat_axis=1, tiled=True),
    )
    scaled_grad = context_gain * back_keys
    grad_keys_in = context_recip * scaled_grad - context_wide * context_recip**3 * jnp.mean(
        context_wide * scaled_grad, axis=1, keepdims=True
    )
    return (self_out, image_out, grad_keys_in, back_values)


def solution(mesh):
    return jax.shard_map(
        per_device,
        mesh=mesh,
        in_specs=(
            P(("row", "col"), "enc"),
            P(("row", "col"), "enc"),
            P(("row", "col"), "enc"),
            P(("row", "col"), None),
            P("enc"),
            P("enc"),
            P(("enc", "row"), None),
            P(("enc", "row"), None),
            P(),
            P(("row", "col"), "enc"),
        ),
        out_specs=(
            P(("row", "col"), "enc"),
            P(("row", "col"), "enc"),
            P(("enc", "row"), None),
            P(("enc", "row"), None),
        ),
        check_vma=False,
    )
```

profile of v0, /device:TPU:0, one launch (start us, length us, event | category | flops | bytes accessed | tf_op | source)
XLA Modules:
  0.0 264.3 jit_solution(4261165534219029951)
XLA Ops:
  8.0 0.9 fusion.67
  9.0 1.4 fusion.69
  10.4 4.2 %all-to-all-start = ((bf16[4,2,1536]{2,0,1:T(4,128)(2,1)}), bf16[4,2,1536]{2,0,1:T(4,128)(2,1)S(1)}, u32[]{:S(2)}, u32[]{:S(2)}) async-start(bf16[4,2,1536]{2,0,1:T(4,128)(2,1)} %bitcast.9), calls=%async_computation | async-start | bytes 49152 | tf_op jit(solution)/shard_map/all_to_all | solution.py:110
  14.6 1.2 fusion.22
  15.8 1.2 fusion.26
  17.1 4.9 %all-reduce.2 = (f32[160]{0:T(256)S(1)}, f32[160]{0:T(256)S(1)}) all-reduce(f32[160]{0:T(256)S(1)} %fusion.22, f32[160]{0:T(256)S(1)} %fusion.26), channel_id=1, replica_groups=mesh['enc'=2,'row'=4,'col'=4] {'enc'}, use_global_device_ids=true, to_apply=%region_1.0 | all-reduce | flops 320 | bytes 2560 | tf_op jit(solution)/shard_map/psum | solution.py:68
  22.0 1.2 fusion.38
  23.3 0.7 convert_element_type.43
  24.0 3.3 %all-to-all-start.1 = ((bf16[4,2,1536]{2,0,1:T(4,128)(2,1)}), bf16[4,2,1536]{2,0,1:T(4,128)(2,1)S(1)}, u32[]{:S(2)}, u32[]{:S(2)}) async-start(bf16[4,2,1536]{2,0,1:T(4,128)(2,1)} %bitcast.143), calls=%async_computation.1 | async-start | bytes 49152 | tf_op jit(solution)/shard_map/all_to_all | solution.py:111
  27.4 5.4 %all_gather.14 = bf16[32,1536]{1,0:T(8,128)(2,1)S(1)} all-gather(bf16[8,1536]{1,0:T(8,128)(2,1)S(1)} %all_to_all.59), channel_id=1, replica_groups=mesh['enc'=2,'row'=4,'col'=4] {'row'}, dimensions={0}, use_global_device_ids=true | all-gather | bytes 122880 | tf_op jit(solution)/shard_map/all_gather | solution.py:114
  32.8 5.6 %all_gather.15 = bf16[32,1536]{1,0:T(8,128)(2,1)S(1)} all-gather(bf16[8,1536]{1,0:T(8,128)(2,1)S(1)} %all_to_all.63), channel_id=1, replica_groups=mesh['enc'=2,'row'=4,'col'=4] {'row'}, dimensions={0}, use_global_device_ids=true | all-gather | bytes 122880 | tf_op jit(solution)/shard_map/all_gather | solution.py:115
  38.4 0.5 fusion.98
  38.8 0.4 multiply_reduce_fusion.1
  39.3 0.3 fusion.21
  39.6 0.7 copy.131
  40.4 0.3 convolution_bitcast_fusion
  40.7 0.7 copy.130
  41.4 0.3 fusion.60
  41.8 0.1 mul.216
  41.9 0.1 copy.41
  42.1 0.1 mul.219
  42.2 0.1 copy.44
  42.3 19.9 %reduce-scatter.3.cloned.1.call-done = f32[8,1536]{1,0:T(8,128)} async-done(((f32[32,1536]{1,0:T(8,128)}), f32[8,1536]{1,0:T(8,128)}) %reduce-scatter.3.cloned.1.call-update) | async-done | bytes 49168 | tf_op jit(solution)/shard_map/reduce_scatter | solution.py:147
  62.2 1.4 all_to_all.64
  63.6 21.4 %reduce-scatter.5.cloned.1.call-done = f32[8,1536]{1,0:T(8,128)} async-done(((f32[32,1536]{1,0:T(8,128)}), f32[8,1536]{1,0:T(8,128)}) %reduce-scatter.5.cloned.1.call-update) | async-done | bytes 49168 | tf_op jit(solution)/shard_map/reduce_scatter | solution.py:148
  85.0 1.4 all_to_all.68
  86.5 2.3 fusion.19
  88.8 0.9 copy.129
  89.8 0.5 all-gather.5.cloned.1.call-update
  90.3 45.6 %all-reduce.5.cloned.1.call-done = (f32[2,4,1536]{2,1,0:T(4,128)}, f32[2,4,1536]{2,1,0:T(4,128)}) async-done(((f32[2,4,1536]{2,1,0:T(4,128)}, f32[2,4,1536]{2,1,0:T(4,128)}), (f32[2,4,1536]{2,1,0:T(4,128)}, f32[2,4,1536]{2,1,0:T(4,128)})) %all-reduce.5.cloned.1.call-update) | async-done | bytes 98320 | tf_op jit(solution)/shard_map/psum | solution.py:150
  135.9 3.3 %all-to-all-start.3 = ((f32[2,4,1536]{2,1,0:T(4,128)}), f32[2,4,1536]{2,1,0:T(4,128)S(1)}, u32[]{:S(2)}, u32[]{:S(2)}) async-start(f32[2,4,1536]{2,1,0:T(4,128)} %get-tuple-element.5), calls=%async_computation.5 | async-start | bytes 98304 | tf_op jit(solution)/shard_map/all_to_all | solution.py:153
  139.2 1.0 fusion.15
  140.3 3.0 %all-to-all-done.3 = f32[2,4,1536]{2,1,0:T(4,128)S(1)} async-done(((f32[2,4,1536]{2,1,0:T(4,128)}), f32[2,4,1536]{2,1,0:T(4,128)S(1)}, u32[]{:S(2)}, u32[]{:S(2)}) %all-to-all-start.3) | async-done | bytes 49184 | tf_op jit(solution)/shard_map/all_to_all | solution.py:153
  143.2 3.5 %all-to-all-start.2 = ((f32[2,4,1536]{2,1,0:T(4,128)}), f32[2,4,1536]{2,1,0:T(4,128)S(1)}, u32[]{:S(2)}, u32[]{:S(2)}) async-start(f32[2,4,1536]{2,1,0:T(4,128)} %get-tuple-element.4), calls=%async_computation.3 | async-start | bytes 98304 | tf_op jit(solution)/shard_map/all_to_all | solution.py:152
  146.7 0.4 fusion.18
  147.1 0.9 copy.127
  147.9 2.6 all-to-all-done.2
  150.6 0.1 fusion.72
  150.7 0.7 fusion.71
  151.4 10.0 %all-gather.3.cloned.1.call-done = bf16[2560,1536]{1,0:T(8,128)(2,1)} async-done(((bf16[160,1536]{1,0:T(8,128)(2,1)}), bf16[2560,1536]{1,0:T(8,128)(2,1)}) %all-gather.3.cloned.1.call-update) | async-done | bytes 7864336 | tf_op jit(solution)/shard_map/all_gather | solution.py:79
  161.4 10.8 %copy.48 = bf16[2560,1536]{0,1:T(8,128)(2,1)} copy(bf16[2560,1536]{1,0:T(8,128)(2,1)} %all-gather.3.cloned.1.call-done) | data formatting | bytes 15728640 | tf_op jit(solution)/shard_map/all_gather | solution.py:79
  172.3 12.6 %multiply_reduce_fusion = (f32[12,160]{1,0:T(8,128)S(1)}, f32[12,160,2560]{2,1,0:T(8,128)}) fusion(bf16[160,12,128]{2,0,1:T(8,128)(2,1)S(1)} %fusion.15, bf16[2560,12,128]{0,2,1:T(8,128)(2,1)} %bitcast.131), kind=kOutput, calls=%fused_computation.2 | convolution fusion | flops 1268119680 | bytes 28024320 | tf_op jit(solution)/shard_map/qhd,khd->hqk/dot_general | solution.py:85
  184.9 10.0 %fusion.1 = f32[12,160]{1,0:T(8,128)S(1)} fusion(f32[12,160,2560]{2,1,0:T(8,128)} %get-tuple-element.22, f32[12,160]{1,0:T(8,128)S(1)} %get-tuple-element.11), kind=kLoop, calls=%fused_computation.3 | loop fusion | flops 14743680 | bytes 19676160 | tf_op jit(solution)/shard_map/reduce_sum | solution.py:91
  194.9 38.4 %all-gather.5.cloned.1.call-done = bf16[2560,1536]{1,0:T(8,128)(2,1)} async-done(((bf16[160,1536]{1,0:T(8,128)(2,1)}), bf16[2560,1536]{1,0:T(8,128)(2,1)}) %all-gather.5.cloned.1.call-update) | async-done | bytes 7864336 | tf_op jit(solution)/shard_map/all_gather | solution.py:80
  233.3 10.8 %copy.50 = bf16[2560,1536]{0,1:T(8,128)(2,1)} copy(bf16[2560,1536]{1,0:T(8,128)(2,1)} %all-gather.5.cloned.1.call-done) | data formatting | bytes 15728640 | tf_op jit(solution)/shard_map/all_gather | solution.py:80
  244.1 11.6 %fusion.35 = bf16[12,20,8,128]{3,2,1,0:T(8,128)(2,1)S(1)} fusion(bf16[2560,12,128]{0,2,1:T(8,128)(2,1)} %bitcast.132, f32[12,160,2560]{2,1,0:T(8,128)} %get-tuple-element.22, f32[12,160]{1,0:T(8,128)S(1)} %get-tuple-element.11, f32[160,12]{0,1:T(8,128)S(1)} %bitcast.144, f32[160,12]{0,1:T(8,128)S(1)} %get-tuple-element.10), kind=kOutput, calls=%fused_computation.43 | convolution fusion | flops 1273774080 | bytes 28039680 | tf_op jit(solution)/shard_map/hqk,khd->qhd/dot_general | solution.py:92
  255.7 0.9 copy.128
  256.6 0.6 copy.135
  (34 shorter events, 0.5 us)
Async XLA Ops:
  8.0 30.8 %copy-start = (bf16[160,1536]{1,0:T(8,128)(2,1)S(1)}, bf16[160,1536]{1,0:T(8,128)(2,1)}, u32[]{:S(2)}) copy-start(bf16[160,1536]{1,0:T(8,128)(2,1)} %param.19) | copy-start | bytes 1474564
  8.0 142.5 %copy-start.1 = (bf16[4,3072]{1,0:T(4,128)(2,1)S(1)}, bf16[4,3072]{1,0:T(4,128)(2,1)}, u32[]{:S(2)}) copy-start(bf16[4,3072]{1,0:T(4,128)(2,1)} %param.16) | copy-start | bytes 73732
  8.0 142.5 %copy-start.2 = (f32[3072]{0:T(1024)S(1)}, f32[3072]{0:T(1024)}, u32[]{:S(2)}) copy-start(f32[3072]{0:T(1024)} %param.18) | copy-start | bytes 36868
  10.4 13.6 %all-to-all-start = ((bf16[4,2,1536]{2,0,1:T(4,128)(2,1)}), bf16[4,2,1536]{2,0,1:T(4,128)(2,1)S(1)}, u32[]{:S(2)}, u32[]{:S(2)}) async-start(bf16[4,2,1536]{2,0,1:T(4,128)(2,1)} %bitcast.9), calls=%async_computation | async-start | bytes 49152 | tf_op jit(solution)/shard_map/all_to_all | solution.py:110
  24.0 8.7 %all-to-all-start.1 = ((bf16[4,2,1536]{2,0,1:T(4,128)(2,1)}), bf16[4,2,1536]{2,0,1:T(4,128)(2,1)S(1)}, u32[]{:S(2)}, u32[]{:S(2)}) async-start(bf16[4,2,1536]{2,0,1:T(4,128)(2,1)} %bitcast.143), calls=%async_computation.1 | async-start | bytes 49152 | tf_op jit(solution)/shard_map/all_to_all | solution.py:111
  27.4 34.8 %reduce-scatter.3.cloned.1.call-start = ((), (), s32[]{:S(2)}) async-start(), calls=%async_computation.8 | async-start | bytes 245760 | tf_op jit(solution)/shard_map/reduce_scatter | solution.py:147
  40.3 44.7 %reduce-scatter.5.cloned.1.call-start = ((), (), s32[]{:S(2)}) async-start(), calls=%async_computation.9 | async-start | bytes 245760 | tf_op jit(solution)/shard_map/reduce_scatter | solution.py:148
  41.4 94.5 %all-reduce.5.cloned.1.call-start = ((), (), s32[]{:S(2)}) async-start(), calls=%async_computation.10 | async-start | bytes 196608 | tf_op jit(solution)/shard_map/psum | solution.py:150
  86.5 75.0 %all-gather.3.cloned.1.call-start = ((), (), s32[]{:S(2)}) async-start(), calls=%async_computation.6 | async-start | bytes 8355840 | tf_op jit(solution)/shard_map/all_gather | solution.py:79
  89.7 143.6 %all-gather.5.cloned.1.call-start = ((), (), s32[]{:S(2)}) async-start(), calls=%async_computation.7 | async-start | bytes 8355840 | tf_op jit(solution)/shard_map/all_gather | solution.py:80
  135.9 7.3 %all-to-all-start.3 = ((f32[2,4,1536]{2,1,0:T(4,128)}), f32[2,4,1536]{2,1,0:T(4,128)S(1)}, u32[]{:S(2)}, u32[]{:S(2)}) async-start(f32[2,4,1536]{2,1,0:T(4,128)} %get-tuple-element.5), calls=%async_computation.5 | async-start | bytes 98304 | tf_op jit(solution)/shard_map/all_to_all | solution.py:153
  143.2 7.3 %all-to-all-start.2 = ((f32[2,4,1536]{2,1,0:T(4,128)}), f32[2,4,1536]{2,1,0:T(4,128)S(1)}, u32[]{:S(2)}, u32[]{:S(2)}) async-start(f32[2,4,1536]{2,1,0:T(4,128)} %get-tuple-element.4), calls=%async_computation.3 | async-start | bytes 98304 | tf_op jit(solution)/shard_map/all_to_all | solution.py:152
Sparse Core Ops, SparseCore 0:
  40.4 21.7 reduce-scatter.2
  65.2 19.7 reduce-scatter.4
  87.9 47.9 all-reduce.4
Sparse Core Ops, SparseCore 1:
  89.8 71.6 all-gather.2
  163.6 69.6 all-gather.4
where the time goes:
time: 266 us; the launch traced here: 264 us
  waiting for transfers between devices  141 us (53%)
  local copies, waits for them, and re-layouts  29.6 us (11%)
  matrix products  29.4 us (11%)
  other arithmetic  18 us (7%)
  blocking collectives  15.9 us (6%)
  between operations  15.4 us (6%)
  starting transfers between devices  14.4 us (5%)
    psum x1, waiting for transfers between devices, per_device(): summed_keys, summed_values = lax.psum((part_keys, part_values), 'col')  45.6 us
    all_gather x1, waiting for transfers between devices, per_device(): lax.all_gather(self_values, ('row', 'col'), axis=0, tiled=True)  38.4 us
    reduce_scatter x1, waiting for transfers between devices, per_device(): lax.psum_scatter(grad_values, 'row', scatter_dimension=0, tiled=True)  21.4 us
    reduce_scatter x1, waiting for transfers between devices, per_device(): lax.psum_scatter(grad_keys, 'row', scatter_dimension=0, tiled=True)  19.9 us
    dot_general x1, matrix products, per_device(): jnp.einsum('qhd,khd->hqk', query_turned, key_heads, preferred_element_typ...  12.6 us
    dot_general x1, matrix products, per_device(): jnp.einsum('hqk,khd->qhd', weights.astype(jnp.bfloat16), value_heads, pre...  11.6 us
    all_gather x1, local copies, waits for them, and re-layouts, per_device(): key_piece = lax.all_gather(key_turned, ('row', 'col'), axis=0, tiled=True)  10.8 us
    all_gather x1, local copies, waits for them, and re-layouts, per_device(): lax.all_gather(self_values, ('row', 'col'), axis=0, tiled=True)  10.8 us
  transfers between devices with their start and end apart: 9, of which 7 were waited for; matrix products, arithmetic and copies ran while one was open for 17% of the time, Pallas kernels for 0%

commit v1 on v0

v1 whole, which is shorter than its diff:
```python
import functools

import jax
import jax.numpy as jnp
import numpy as np
from jax import lax
from jax.experimental import pallas as pl
from jax.experimental.pallas import tpu as pltpu
from jax.sharding import PartitionSpec as P

HEAD_DIM = 128
eps = 1e-06
LOG2E = 1.4426950408889634
NT = (((1,), (1,)), ((), ()))
TN = (((0,), (0,)), ((), ()))
VMEM_LIMIT = 48 * 1024 * 1024


def swap(x, axis, size, k):
    return lax.ppermute(x, axis, [(i, i ^ k) for i in range(size)])


def kernel_call(body, out_shape, cost=(0, 0, 0), **kw):
    return pl.pallas_call(
        body,
        out_shape=out_shape,
        compiler_params=pltpu.CompilerParams(vmem_limit_bytes=VMEM_LIMIT),
        cost_estimate=pl.CostEstimate(flops=cost[0], bytes_accessed=cost[1], transcendentals=cost[2]),
        **kw,
    )


def rope_tables(positions):
    half = HEAD_DIM // 2
    part_side = HEAD_DIM // 6
    part_time = half - 2 * part_side
    freq_time = 1.0 / 10000.0 ** (jnp.arange(part_time, dtype=jnp.float32) * 2.0 / (2 * part_time))
    freq_side = 1.0 / 10000.0 ** (jnp.arange(part_side, dtype=jnp.float32) * 2.0 / (2 * part_side))
    freq = jnp.repeat(jnp.concatenate([freq_time, freq_side, freq_side]), 2)
    pair = np.arange(HEAD_DIM) // 2
    coords = positions.astype(jnp.float32)
    coord = jnp.where(
        pair < part_time,
        coords[:, 0:1],
        jnp.where(pair < part_time + part_side, coords[:, 1:2], coords[:, 2:3]),
    )
    angles = coord * freq
    sign = np.where(np.arange(HEAD_DIM) % 2 == 0, -1.0, 1.0).astype(np.float32)
    return jnp.cos(angles), jnp.sin(angles) * sign


def columns_of(axis, k, width):
    start = (lax.axis_index(axis) ^ k) * width
    return pl.ds(pl.multiple_of(start, HEAD_DIM), width)


def split_columns(x, axis, parts):
    rows, width = x.shape
    piece = width // parts

    def body(x_ref, *outs):
        for k in range(parts):
            outs[k][...] = x_ref[:, columns_of(axis, k, piece)]

    return kernel_call(
        body,
        [jax.ShapeDtypeStruct((rows, piece), x.dtype)] * parts,
        (0, 4 * rows * width, 0),
    )(x)


def join_columns(pieces, axis):
    rows, piece = pieces[0].shape
    parts = len(pieces)

    def body(*refs):
        for k in range(parts):
            refs[parts][:, columns_of(axis, k, piece)] = refs[k][...]

    return kernel_call(
        body,
        jax.ShapeDtypeStruct((rows, piece * parts), pieces[0].dtype),
        (0, 4 * rows * piece * parts, 0),
    )(*pieces)


def square_sums(queries, keys):
    rows, width = queries.shape

    def body(q_ref, k_ref, out_ref):
        for i, ref in enumerate((q_ref, k_ref)):
            wide = ref[...].astype(jnp.float32)
            out_ref[:, i : i + 1] = jnp.sum(wide * wide, axis=1, keepdims=True)

    return kernel_call(
        body, jax.ShapeDtypeStruct((rows, 2), jnp.float32), (4 * rows * width, 4 * rows * width, 0)
    )(queries, keys)


def normed_turned(x, which, totals, gain, cosine, sine, full_width, axis, parts, plain):
    rows, width = x.shape
    piece = width // parts
    n_totals = len(totals)

    def body(*refs):
        total_refs = refs[:n_totals]
        x_ref, gain_ref, cos_ref, sin_ref = refs[n_totals : n_totals + 4]
        outs = refs[n_totals + 4 :]
        total = total_refs[0][:, which : which + 1]
        for ref in total_refs[1:]:
            total = total + ref[:, which : which + 1]
        recip = lax.rsqrt(total / full_width + eps)
        cos = cos_ref[...]
        sin = sin_ref[...]
        even = lax.broadcasted_iota(jnp.int32, cos.shape, 1) % 2 == 0
        for k in range(parts):
            for h in range(piece // HEAD_DIM):
                start = (lax.axis_index(axis) ^ k) * piece + h * HEAD_DIM if parts > 1 else h * HEAD_DIM
                cols = pl.ds(pl.multiple_of(start, HEAD_DIM), HEAD_DIM)
                normed = x_ref[:, cols].astype(jnp.float32) * recip * gain_ref[:, cols]
                if plain:
                    outs[parts][:, cols] = normed.astype(jnp.bfloat16)
                other = jnp.where(
                    even, pltpu.roll(normed, HEAD_DIM - 1, 1), pltpu.roll(normed, 1, 1)
                )
                outs[k][:, h * HEAD_DIM : (h + 1) * HEAD_DIM] = (normed * cos + other * sin).astype(
                    jnp.bfloat16
                )

    shapes = [jax.ShapeDtypeStruct((rows, piece), jnp.bfloat16)] * parts
    if plain:
        shapes = shapes + [jax.ShapeDtypeStruct((rows, width), jnp.bfloat16)]
    return kernel_call(body, shapes, (10 * rows * width, 4 * rows * width, 0))(
        *totals, x, gain[None, :], cosine, sine
    )


def attention(query, keys, values):
    rows, width = query.shape
    heads = width // HEAD_DIM
    n = len(keys)
    total = sum(k.shape[0] for k in keys)
    factor = HEAD_DIM ** (-0.5) * LOG2E

    def body(q_ref, *refs):
        out_ref = refs[2 * n]
        q = q_ref[...]
        scores = [
            lax.dot_general(q, k[...], NT, preferred_element_type=jnp.float32) for k in refs[:n]
        ]
        peak = functools.reduce(
            jnp.maximum, [jnp.max(s, axis=1, keepdims=True) for s in scores]
        )
        weight_sum = 0.0
        mixed = 0.0
        for s, v in zip(scores, refs[n : 2 * n]):
            weights = jnp.exp2((s - peak) * factor)
            weight_sum = weight_sum + jnp.sum(weights, axis=1, keepdims=True)
            mixed = mixed + jnp.dot(
                weights.astype(jnp.bfloat16), v[...], preferred_element_type=jnp.float32
            )
        out_ref[...] = (mixed / weight_sum).astype(jnp.bfloat16)

    def spec(x):
        return pl.BlockSpec((x.shape[0], HEAD_DIM), lambda h: (0, h))

    return kernel_call(
        body,
        jax.ShapeDtypeStruct((rows, width), jnp.bfloat16),
        (4 * rows * total * width, 4 * total * width, rows * total * heads),
        grid=(heads,),
        in_specs=[spec(query)] + [spec(x) for x in keys] + [spec(x) for x in values],
        out_specs=spec(query),
    )(query, *keys, *values)


def image_attention(query_plain, context, cotangent):
    rows, width = query_plain.shape
    count = context.shape[1]
    heads = width // HEAD_DIM
    half = count // 2
    scale = HEAD_DIM ** (-0.5)

    def body(q_ref, c_ref, g_ref, out_ref, keep_ref, send_ref):
        for h in range(heads):
            cols = slice(h * HEAD_DIM, (h + 1) * HEAD_DIM)
            q = q_ref[:, cols]
            g = g_ref[:, cols]
            k = c_ref[0, :, cols]
            v = c_ref[1, :, cols]
            scores = lax.dot_general(k, q, NT, preferred_element_type=jnp.float32) * scale
            weights = jnp.exp(scores - jnp.max(scores, axis=0, keepdims=True))
            probs = weights / jnp.sum(weights, axis=0, keepdims=True)
            low = probs.astype(jnp.bfloat16)
            out_ref[:, cols] = lax.dot_general(
                low, v, TN, preferred_element_type=jnp.float32
            ).astype(jnp.bfloat16)
            grad_v = jnp.dot(low, g, preferred_element_type=jnp.float32)
            grad_p = lax.dot_general(v, g, NT, preferred_element_type=jnp.float32)
            inner = jnp.sum(probs * grad_p, axis=0, keepdims=True)
            grad_s = (probs * (grad_p - inner)).astype(jnp.bfloat16)
            grad_k = jnp.dot(grad_s, q, preferred_element_type=jnp.float32) * scale
            for i, grad in enumerate((grad_k, grad_v)):
                keep_ref[i, :, cols] = grad[:half]
                send_ref[i, :, cols] = grad[half:]

    return kernel_call(
        body,
        [
            jax.ShapeDtypeStruct((rows, width), jnp.bfloat16),
            jax.ShapeDtypeStruct((2, half, width), jnp.float32),
            jax.ShapeDtypeStruct((2, half, width), jnp.float32),
        ],
        (10 * rows * count * width, 8 * rows * width, rows * count * heads),
    )(query_plain, context, cotangent)


def per_device(
    sizes,
    queries,
    self_keys,
    self_values,
    positions,
    query_gain,
    key_gain,
    context_keys,
    context_values,
    context_gain,
    image_cotangent,
):
    n_enc, n_row, n_col = sizes
    rows, width = queries.shape
    heads = width // HEAD_DIM
    full_width = width * n_enc
    parts = n_col if heads % n_col == 0 else 1
    enc_index = lax.axis_index("enc")

    def exchange(pieces):
        return [pieces[0]] + [swap(pieces[k], "col", n_col, k) for k in range(1, parts)]

    def spread(pieces):
        if parts == 1:
            return [lax.all_gather(pieces[0], ("row", "col"), axis=0, tiled=True)]
        held = [jnp.concatenate(pieces, axis=0)]
        bit = n_row // 2
        while bit:
            held = held + [swap(x, "row", n_row, bit) for x in held]
            bit //= 2
        return held

    value_pieces = exchange(split_columns(self_values, "col", parts))

    sums = square_sums(queries, self_keys)
    totals = [sums]
    bit = 1
    while bit < n_enc:
        if len(totals) > 1:
            totals = [totals[0] + totals[1]]
        totals = [totals[0], swap(totals[0], "enc", n_enc, bit)]
        bit *= 2
    cosine, sine = rope_tables(positions)

    context_wide = context_keys.astype(jnp.float32)
    context_recip = lax.rsqrt(jnp.mean(context_wide * context_wide, axis=1, keepdims=True) + eps)
    context_normed = (context_wide * context_recip * context_gain).astype(jnp.bfloat16)
    own_count = context_keys.shape[0]
    context_both = jnp.stack([context_normed, context_values])
    context = []
    for k in range(n_enc):
        piece = lax.dynamic_slice_in_dim(context_both, (enc_index ^ k) * width, width, axis=2)
        context.append(swap(piece, "enc", n_enc, k) if k else piece)
    context = jnp.concatenate(context, axis=1)
    bit = n_row // 2
    while bit:
        context = jnp.concatenate([context, swap(context, "row", n_row, bit)], axis=1)
        bit //= 2

    key_pieces = normed_turned(
        self_keys, 1, totals, key_gain, cosine, sine, full_width, "col", parts, False
    )
    key_pieces = exchange(key_pieces)
    *query_pieces, query_plain = normed_turned(
        queries, 0, totals, query_gain, cosine, sine, full_width, "col", parts, True
    )
    query_pieces = exchange(query_pieces)

    image_out, grad, sent = image_attention(query_plain, context, image_cotangent)

    all_values = spread(value_pieces)
    all_keys = spread(key_pieces)

    bit = 1
    while bit < n_row:
        grad = grad + swap(sent, "row", n_row, bit)
        bit *= 2
        if bit < n_row:
            half = grad.shape[1] // 2
            grad, sent = grad[:, :half], grad[:, half:]
    bit = n_col // 2
    while bit:
        grad = grad + swap(grad, "col", n_col, bit)
        bit //= 2
    grad = grad.reshape(2, n_enc, own_count, width)
    grad = jnp.stack([grad[:, 0]] + [swap(grad[:, k], "enc", n_enc, k) for k in range(1, n_enc)])
    grad = jnp.concatenate(
        [lax.dynamic_index_in_dim(grad, enc_index ^ k, 0, False) for k in range(n_enc)], axis=2
    )
    scaled_grad = context_gain * grad[0]
    grad_keys_in = context_recip * scaled_grad - context_wide * context_recip**3 * jnp.mean(
        context_wide * scaled_grad, axis=1, keepdims=True
    )

    mixed = [None] * parts
    for k in reversed(range(parts)):
        piece = attention(query_pieces[k], all_keys, all_values)
        mixed[k] = swap(piece, "col", n_col, k) if k else piece
    self_out = join_columns(mixed, "col") if parts > 1 else mixed[0]

    return (self_out, image_out, grad_keys_in, grad[1])


def solution(mesh):
    sizes = tuple(mesh.shape[a] for a in ("enc", "row", "col"))
    return jax.shard_map(
        functools.partial(per_device, sizes),
        mesh=mesh,
        in_specs=(
            P(("row", "col"), "enc"),
            P(("row", "col"), "enc"),
            P(("row", "col"), "enc"),
            P(("row", "col"), None),
            P("enc"),
            P("enc"),
            P(("enc", "row"), None),
            P(("enc", "row"), None),
            P(),
            P(("row", "col"), "enc"),
        ),
        out_specs=(
            P(("row", "col"), "enc"),
            P(("row", "col"), "enc"),
            P(("enc", "row"), None),
            P(("enc", "row"), None),
        ),
        check_vma=False,
    )
```

time: 266 us -> 94.5 us (0.36)
  waiting for transfers between devices: 141 us -> 35.7 us
  matrix products: 29.4 us -> 0 us
  local copies, waits for them, and re-layouts: 29.6 us -> 3.23 us
  Pallas kernels: 0 us -> 21.7 us
  blocking collectives: 15.9 us -> 0 us
  starting transfers between devices: 14.4 us -> 30 us
  other arithmetic: 18 us -> 2.5 us
  between operations: 15.4 us -> 1.09 us
    all_gather x2 -> x0, waiting for transfers between devices: 48.4 us -> none  [the longest x1 38.4 us: per_device(): lax.all_gather(self_values, ('row', 'col'), axis=0, tiled=True)]
    psum x1 -> x0, waiting for transfers between devices: 45.6 us -> none  [per_device(): summed_keys, summed_values = lax.psum((part_keys, part_values), 'col')]
    reduce_scatter x2 -> x0, waiting for transfers between devices: 41.3 us -> none  [the longest x1 21.4 us: per_device(): lax.psum_scatter(grad_values, 'row', scatter_dimension=0, tiled=True)]
    ppermute x0 -> x27, waiting for transfers between devices: none -> 35.7 us  [swap(): return lax.ppermute(x, axis, [(i, i ^ k) for i in range(size)])]
    ppermute x0 -> x27, starting transfers between devices: none -> 30 us  [swap(): return lax.ppermute(x, axis, [(i, i ^ k) for i in range(size)])]
    dot_general x8 -> x0, matrix products: 29 us -> none  [the longest x1 12.6 us: per_device(): jnp.einsum('qhd,khd->hqk', query_turned, key_heads, preferred_element_typ...]
    pallas_call x0 -> x10, Pallas kernels: none -> 21.7 us  [the longest x4 14.5 us: attention(): kernel_call(body, jax.ShapeDtypeStruct((rows, width), jnp.bfloat16), (4 *...]
    all_gather x2 -> x0, local copies, waits for them, and re-layouts: 21.6 us -> none  [the longest x1 10.8 us: per_device(): key_piece = lax.all_gather(key_turned, ('row', 'col'), axis=0, tiled=True)]
  transfers between devices with their start and end apart: 9 -> 27, of which waited for: 7 -> 10; matrix products, arithmetic and copies ran while one was open for 17% -> 3% of each run, Pallas kernels for 0% -> 22%
where the time goes in v1:
time: 94.5 us; the launch traced here: 94.2 us
  waiting for transfers between devices  35.7 us (38%)
  starting transfers between devices  30 us (32%)
  Pallas kernels  21.7 us (23%)
  local copies, waits for them, and re-layouts  3.23 us (3%)
  other arithmetic  2.5 us (3%)
  between operations  1.09 us (1%)
    ppermute x27, waiting for transfers between devices, swap(): return lax.ppermute(x, axis, [(i, i ^ k) for i in range(size)])  35.7 us
    ppermute x27, starting transfers between devices, swap(): return lax.ppermute(x, axis, [(i, i ^ k) for i in range(size)])  30 us
    pallas_call x4, Pallas kernels, attention(): kernel_call(body, jax.ShapeDtypeStruct((rows, width), jnp.bfloat16), (4 *...  14.5 us
    pallas_call x1, Pallas kernels, image_attention(): kernel_call(body, [jax.ShapeDtypeStruct((rows, width), jnp.bfloat16), jax...  4.69 us
    unnamed x36, local copies, waits for them, and re-layouts  2.9 us
  transfers between devices with their start and end apart: 27, of which 10 were waited for; matrix products, arithmetic and copies ran while one was open for 3% of the time, Pallas kernels for 22%

profile of v1, /device:TPU:0, one launch (start us, length us, event | category | flops | bytes accessed | tf_op | source)
XLA Modules:
  0.0 94.2 jit_solution(13365003861429696864)
XLA Ops:
  0.6 1.0 %copy-done = bf16[160,1536]{1,0:T(8,128)(2,1)S(1)} copy-done((bf16[160,1536]{1,0:T(8,128)(2,1)S(1)}, bf16[160,1536]{1,0:T(8,128)(2,1)}, u32[]{:S(2)}) %copy-start) | copy-done | bytes 491544
  1.7 1.0 %copy-done.2 = bf16[160,1536]{1,0:T(8,128)(2,1)S(1)} copy-done((bf16[160,1536]{1,0:T(8,128)(2,1)S(1)}, bf16[160,1536]{1,0:T(8,128)(2,1)}, u32[]{:S(2)}) %copy-start.2) | copy-done | bytes 491544
  2.7 0.3 shard_map.156.refs_0_
  3.0 3.0 %collective-permute-start = (f32[160,2]{1,0:T(8,128)S(1)}, f32[160,2]{1,0:T(8,128)S(1)}, u32[]{:S(2)}, u32[]{:S(2)}) collective-permute-start(f32[160,2]{1,0:T(8,128)S(1)} %shard_map.156.refs_0_), channel_id=1, source_target_pairs={{0,16},{16,0},{1,17},{17,1},{2,18},{18,2},{3,19},{19,3},{4,20},{20... | collective-permute-start | bytes 3848 | tf_op jit(solution)/shard_map/ppermute | solution.py:20
  6.1 1.6 %collective-permute-start.7 = (bf16[160,384]{1,0:T(8,128)(2,1)S(1)}, bf16[160,384]{1,0:T(8,128)(2,1)S(1)}, u32[]{:S(2)}, u32[]{:S(2)}) collective-permute-start(bf16[160,384]{1,0:T(8,128)(2,1)S(1)} %get-tuple-element.26), channel_id=1, source_target_pairs={{0,1},{1,0},{2,3},{3,2},{4,5},{5,4},{6,7},{7,6},{8,9},{9,8},{10,11... | collective-permute-start | bytes 368648 | tf_op jit(solution)/shard_map/ppermute | solution.py:20
  7.7 2.6 %collective-permute-start.8 = (bf16[160,384]{1,0:T(8,128)(2,1)S(1)}, bf16[160,384]{1,0:T(8,128)(2,1)S(1)}, u32[]{:S(2)}, u32[]{:S(2)}) collective-permute-start(bf16[160,384]{1,0:T(8,128)(2,1)S(1)} %get-tuple-element.27), channel_id=1, source_target_pairs={{0,2},{1,3},{2,0},{3,1},{4,6},{5,7},{6,4},{7,5},{8,10},{9,11},{10,... | collective-permute-start | bytes 368648 | tf_op jit(solution)/shard_map/ppermute | solution.py:20
  10.3 0.2 collective-permute-start.9
  10.5 0.1 fusion.1
  10.8 0.8 collective-permute-start.19
  11.8 0.2 mul.76
  12.0 0.4 sine_multiply_fusion
  12.4 2.3 %collective-permute-done.19 = bf16[2,4,1536]{2,1,0:T(4,128)(2,1)S(1)} collective-permute-done((bf16[2,4,1536]{2,1,0:T(4,128)(2,1)S(1)}, bf16[2,4,1536]{2,1,0:T(4,128)(2,1)S(1)}, u32[]{:S(2)}, u32[]{:S(2)}) %collective-permute-start.19) | collective-permute-done | bytes 24608 | tf_op jit(solution)/shard_map/ppermute | solution.py:20
  14.8 1.6 %collective-permute-start.20 = (bf16[2,8,1536]{2,1,0:T(8,128)(2,1)S(1)}, bf16[2,8,1536]{2,1,0:T(8,128)(2,1)S(1)}, u32[]{:S(2)}, u32[]{:S(2)}) collective-permute-start(bf16[2,8,1536]{2,1,0:T(8,128)(2,1)S(1)} %pad_maximum_fusion.3), channel_id=1, source_target_pairs={{0,8},{4,12},{8,0},{12,4},{1,9},{5,13},{9,1},{13,5},{2,10},{6,14},... | collective-permute-start | bytes 147464 | tf_op jit(solution)/shard_map/ppermute | solution.py:20
  16.4 0.7 copy-done.9
  17.1 0.7 shard_map.158
  17.8 0.7 collective-permute-start.1
  18.5 0.7 shard_map.157
  19.4 1.3 %collective-permute-done.21 = bf16[2,16,1536]{2,1,0:T(8,128)(2,1)S(1)} collective-permute-done((bf16[2,16,1536]{2,1,0:T(8,128)(2,1)S(1)}, bf16[2,16,1536]{2,1,0:T(8,128)(2,1)S(1)}, u32[]{:S(2)}, u32[]{:S(2)}) %collective-permute-start.21) | collective-permute-done | bytes 98336 | tf_op jit(solution)/shard_map/ppermute | solution.py:20
  20.6 3.5 %collective-permute-start.2 = (bf16[160,384]{1,0:T(8,128)(2,1)S(1)}, bf16[160,384]{1,0:T(8,128)(2,1)S(1)}, u32[]{:S(2)}, u32[]{:S(2)}) collective-permute-start(bf16[160,384]{1,0:T(8,128)(2,1)S(1)} %get-tuple-element.23), channel_id=1, source_target_pairs={{0,2},{1,3},{2,0},{3,1},{4,6},{5,7},{6,4},{7,5},{8,10},{9,11},{10,... | collective-permute-start | bytes 368648 | tf_op jit(solution)/shard_map/ppermute | solution.py:20
  24.2 4.7 %shard_map.165 = (bf16[160,1536]{1,0:T(8,128)(2,1)}, f32[2,16,1536]{2,1,0:T(8,128)S(1)}, f32[2,16,1536]{2,1,0:T(8,128)S(1)}) custom-call(bf16[160,1536]{1,0:T(8,128)(2,1)S(1)} %get-tuple-element.32.q_ref, bf16[2,32,1536]{2,1,0:T(8,128)(2,1)S(1)} %pad_maximum_fusion.c_ref, bf16[160,1536]{1,0:T(8,128)(2,1)S(1)} %copy-done.4), custom_call_target="tpu_custom_call" | custom-call | flops 78643200 | bytes 1966080 | tf_op jit(solution)/shard_map/pallas_call | solution.py:207
  28.9 0.3 collective-permute-start.3
  29.2 1.1 %collective-permute-done.22 = f32[2,16,1536]{2,1,0:T(8,128)S(1)} collective-permute-done((f32[2,16,1536]{2,1,0:T(8,128)S(1)}, f32[2,16,1536]{2,1,0:T(8,128)S(1)}, u32[]{:S(2)}, u32[]{:S(2)}) %collective-permute-start.22) | collective-permute-done | bytes 196640 | tf_op jit(solution)/shard_map/ppermute | solution.py:20
  30.3 0.4 collective-permute-start.13
  30.8 1.6 %collective-permute-start.23 = (f32[2,8,1536]{2,1,0:T(8,128)S(1)}, f32[2,8,1536]{2,1,0:T(8,128)S(1)}, u32[]{:S(2)}, u32[]{:S(2)}) collective-permute-start(f32[2,8,1536]{2,1,0:T(8,128)S(1)} %slice.40), channel_id=1, source_target_pairs={{0,8},{4,12},{8,0},{12,4},{1,9},{5,13},{9,1},{13,5},{2,10},{6,14},... | collective-permute-start | bytes 294920 | tf_op jit(solution)/shard_map/ppermute | solution.py:20
  32.4 3.1 %collective-permute-done.23 = f32[2,8,1536]{2,1,0:T(8,128)S(1)} collective-permute-done((f32[2,8,1536]{2,1,0:T(8,128)S(1)}, f32[2,8,1536]{2,1,0:T(8,128)S(1)}, u32[]{:S(2)}, u32[]{:S(2)}) %collective-permute-start.23) | collective-permute-done | bytes 98336 | tf_op jit(solution)/shard_map/ppermute | solution.py:20
  35.4 2.8 %collective-permute-start.15 = (bf16[160,384]{1,0:T(8,128)(2,1)S(1)}, bf16[160,384]{1,0:T(8,128)(2,1)S(1)}, u32[]{:S(2)}, u32[]{:S(2)}) collective-permute-start(bf16[160,384]{1,0:T(8,128)(2,1)S(1)} %get-tuple-element.30), channel_id=1, source_target_pairs={{0,2},{1,3},{2,0},{3,1},{4,6},{5,7},{6,4},{7,5},{8,10},{9,11},{10,... | collective-permute-start | bytes 368648 | tf_op jit(solution)/shard_map/ppermute | solution.py:20
  38.3 0.2 collective-permute-start.24
  38.5 9.2 %collective-permute-done.24 = f32[2,8,1536]{2,1,0:T(8,128)S(1)} collective-permute-done((f32[2,8,1536]{2,1,0:T(8,128)S(1)}, f32[2,8,1536]{2,1,0:T(8,128)S(1)}, u32[]{:S(2)}, u32[]{:S(2)}) %collective-permute-start.24) | collective-permute-done | bytes 98336 | tf_op jit(solution)/shard_map/ppermute | solution.py:20
  47.7 1.3 %collective-permute-start.10 = (bf16[640,384]{1,0:T(8,128)(2,1)S(1)}, bf16[640,384]{1,0:T(8,128)(2,1)S(1)}, u32[]{:S(2)}, u32[]{:S(2)}) collective-permute-start(bf16[640,384]{1,0:T(8,128)(2,1)S(1)} %constant_dynamic-update-slice_fusion.4.refs_4_), channel_id=1, source_target_pairs={{0,8},{4,12},{8,0},{12,4},{1,9},{5,13},{9,1},{13,5},{2,10},{6,14},... | collective-permute-start | bytes 1474568 | tf_op jit(solution)/shard_map/ppermute | solution.py:20
  49.1 4.6 %collective-permute-done.25 = f32[2,8,1536]{2,1,0:T(8,128)S(1)} collective-permute-done((f32[2,8,1536]{2,1,0:T(8,128)S(1)}, f32[2,8,1536]{2,1,0:T(8,128)S(1)}, u32[]{:S(2)}, u32[]{:S(2)}) %collective-permute-start.25) | collective-permute-done | bytes 98336 | tf_op jit(solution)/shard_map/ppermute | solution.py:20
  53.7 0.8 collective-permute-start.26
  54.5 3.4 %collective-permute-done.26 = f32[2,4,1536]{2,1,0:T(4,128)S(1)} collective-permute-done((f32[2,4,1536]{2,1,0:T(4,128)S(1)}, f32[2,4,1536]{2,1,0:T(4,128)S(1)}, u32[]{:S(2)}, u32[]{:S(2)}) %collective-permute-start.26) | collective-permute-done | bytes 49184 | tf_op jit(solution)/shard_map/ppermute | solution.py:20
  57.9 0.8 collective-permute-start.4
  58.7 0.1 fusion.6
  58.9 2.8 %collective-permute-start.17 = (bf16[160,384]{1,0:T(8,128)(2,1)S(1)}, bf16[160,384]{1,0:T(8,128)(2,1)S(1)}, u32[]{:S(2)}, u32[]{:S(2)}) collective-permute-start(bf16[160,384]{1,0:T(8,128)(2,1)S(1)} %get-tuple-element.31), channel_id=1, source_target_pairs={{0,3},{1,2},{2,1},{3,0},{4,7},{5,6},{6,5},{7,4},{8,11},{9,10},{10,... | collective-permute-start | bytes 368648 | tf_op jit(solution)/shard_map/ppermute | solution.py:20
  61.7 0.5 collective-permute-start.12
  62.2 8.6 %collective-permute-done.4.refs_1_ = bf16[640,384]{1,0:T(8,128)(2,1)S(1)} collective-permute-done((bf16[640,384]{1,0:T(8,128)(2,1)S(1)}, bf16[640,384]{1,0:T(8,128)(2,1)S(1)}, u32[]{:S(2)}, u32[]{:S(2)}) %collective-permute-start.4) | collective-permute-done | bytes 491552 | tf_op jit(solution)/shard_map/ppermute | solution.py:20
  70.8 0.7 fusion.5
  71.5 1.1 %collective-permute-done.6.refs_3_ = bf16[640,384]{1,0:T(8,128)(2,1)S(1)} collective-permute-done((bf16[640,384]{1,0:T(8,128)(2,1)S(1)}, bf16[640,384]{1,0:T(8,128)(2,1)S(1)}, u32[]{:S(2)}, u32[]{:S(2)}) %collective-permute-start.6) | collective-permute-done | bytes 491552 | tf_op jit(solution)/shard_map/ppermute | solution.py:20
  72.7 3.6 %shard_map.161 = bf16[160,384]{1,0:T(8,128)(2,1)S(1)} custom-call(bf16[160,384]{1,0:T(8,128)(2,1)S(1)} %collective-permute-done.13.q_ref, bf16[640,384]{1,0:T(8,128)(2,1)S(1)} %constant_dynamic-update-slice_fusion.refs_0_, bf16[640,384]{1,0:T(8,128)(2,1)S(1)} %collective-permute-done.4.refs_1_, bf16[640,384]{1,0:T(8,128)(2,1)S(1)} %collective-permute-done.5.refs_2_, ...), custom_call_target="tpu_custom_call" | custom-call | flops 629145600 | bytes 3932160 | tf_op jit(solution)/shard_map/pallas_call | solution.py:167
  76.4 3.6 %shard_map.162 = bf16[160,384]{1,0:T(8,128)(2,1)S(1)} custom-call(bf16[160,384]{1,0:T(8,128)(2,1)S(1)} %collective-permute-done.15.q_ref, bf16[640,384]{1,0:T(8,128)(2,1)S(1)} %constant_dynamic-update-slice_fusion.refs_0_, bf16[640,384]{1,0:T(8,128)(2,1)S(1)} %collective-permute-done.4.refs_1_, bf16[640,384]{1,0:T(8,128)(2,1)S(1)} %collective-permute-done.5.refs_2_, ...), custom_call_target="tpu_custom_call" | custom-call | flops 629145600 | bytes 3932160 | tf_op jit(solution)/shard_map/pallas_call | solution.py:167
  80.0 2.9 %collective-permute-start.16 = (bf16[160,384]{1,0:T(8,128)(2,1)S(1)}, bf16[160,384]{1,0:T(8,128)(2,1)S(1)}, u32[]{:S(2)}, u32[]{:S(2)}) collective-permute-start(bf16[160,384]{1,0:T(8,128)(2,1)S(1)} %shard_map.162), channel_id=1, source_target_pairs={{0,2},{1,3},{2,0},{3,1},{4,6},{5,7},{6,4},{7,5},{8,10},{9,11},{10,... | collective-permute-start | bytes 368648 | tf_op jit(solution)/shard_map/ppermute | solution.py:20
  83.0 3.6 %shard_map.163 = bf16[160,384]{1,0:T(8,128)(2,1)S(1)} custom-call(bf16[160,384]{1,0:T(8,128)(2,1)S(1)} %collective-permute-done.17.q_ref, bf16[640,384]{1,0:T(8,128)(2,1)S(1)} %constant_dynamic-update-slice_fusion.refs_0_, bf16[640,384]{1,0:T(8,128)(2,1)S(1)} %collective-permute-done.4.refs_1_, bf16[640,384]{1,0:T(8,128)(2,1)S(1)} %collective-permute-done.5.refs_2_, ...), custom_call_target="tpu_custom_call" | custom-call | flops 629145600 | bytes 3932160 | tf_op jit(solution)/shard_map/pallas_call | solution.py:167
  86.6 1.6 %collective-permute-start.18 = (bf16[160,384]{1,0:T(8,128)(2,1)S(1)}, bf16[160,384]{1,0:T(8,128)(2,1)S(1)}, u32[]{:S(2)}, u32[]{:S(2)}) collective-permute-start(bf16[160,384]{1,0:T(8,128)(2,1)S(1)} %shard_map.163), channel_id=1, source_target_pairs={{0,3},{1,2},{2,1},{3,0},{4,7},{5,6},{6,5},{7,4},{8,11},{9,10},{10,... | collective-permute-start | bytes 368648 | tf_op jit(solution)/shard_map/ppermute | solution.py:20
  88.2 0.6 fusion.14
  88.8 3.6 %shard_map.160.refs_0_ = bf16[160,384]{1,0:T(8,128)(2,1)S(1)} custom-call(bf16[160,384]{1,0:T(8,128)(2,1)S(1)} %get-tuple-element.20.q_ref, bf16[640,384]{1,0:T(8,128)(2,1)S(1)} %constant_dynamic-update-slice_fusion.refs_0_, bf16[640,384]{1,0:T(8,128)(2,1)S(1)} %collective-permute-done.4.refs_1_, bf16[640,384]{1,0:T(8,128)(2,1)S(1)} %collective-permute-done.5.refs_2_, ...), custom_call_target="tpu_custom_call" | custom-call | flops 629145600 | bytes 3932160 | tf_op jit(solution)/shard_map/pallas_call | solution.py:167
  92.5 0.9 %collective-permute-done.18.refs_3_ = bf16[160,384]{1,0:T(8,128)(2,1)S(1)} collective-permute-done((bf16[160,384]{1,0:T(8,128)(2,1)S(1)}, bf16[160,384]{1,0:T(8,128)(2,1)S(1)}, u32[]{:S(2)}, u32[]{:S(2)}) %collective-permute-start.18) | collective-permute-done | bytes 122912 | tf_op jit(solution)/shard_map/ppermute | solution.py:20
  93.4 0.8 shard_map.164
  (83 shorter events, 1.2 us)
Async XLA Ops:
  0.6 1.0 %copy-start = (bf16[160,1536]{1,0:T(8,128)(2,1)S(1)}, bf16[160,1536]{1,0:T(8,128)(2,1)}, u32[]{:S(2)}) copy-start(bf16[160,1536]{1,0:T(8,128)(2,1)} %refs_2_.3) | copy-start | bytes 1474564
  1.7 1.0 %copy-start.2 = (bf16[160,1536]{1,0:T(8,128)(2,1)S(1)}, bf16[160,1536]{1,0:T(8,128)(2,1)}, u32[]{:S(2)}) copy-start(bf16[160,1536]{1,0:T(8,128)(2,1)} %refs_2_.2) | copy-start | bytes 1474564
  2.7 3.2 %copy-start.5 = (bf16[160,1536]{1,0:T(8,128)(2,1)S(1)}, bf16[160,1536]{1,0:T(8,128)(2,1)}, u32[]{:S(2)}) copy-start(bf16[160,1536]{1,0:T(8,128)(2,1)} %x_ref.1) | copy-start | bytes 1474564
  3.0 14.1 %collective-permute-start = (f32[160,2]{1,0:T(8,128)S(1)}, f32[160,2]{1,0:T(8,128)S(1)}, u32[]{:S(2)}, u32[]{:S(2)}) collective-permute-start(f32[160,2]{1,0:T(8,128)S(1)} %shard_map.156.refs_0_), channel_id=1, source_target_pairs={{0,16},{16,0},{1,17},{17,1},{2,18},{18,2},{3,19},{19,3},{4,20},{20... | collective-permute-start | bytes 3848 | tf_op jit(solution)/shard_map/ppermute | solution.py:20
  5.9 4.6 %copy-start.6 = (bf16[4,3072]{1,0:T(4,128)(2,1)S(1)}, bf16[4,3072]{1,0:T(4,128)(2,1)}, u32[]{:S(2)}) copy-start(bf16[4,3072]{1,0:T(4,128)(2,1)} %param.19) | copy-start | bytes 73732
  5.9 4.7 %copy-start.7 = (f32[3072]{0:T(1024)S(1)}, f32[3072]{0:T(1024)}, u32[]{:S(2)}) copy-start(f32[3072]{0:T(1024)} %param.21) | copy-start | bytes 36868
  5.9 4.8 %copy-start.8 = (bf16[4,3072]{1,0:T(4,128)(2,1)S(1)}, bf16[4,3072]{1,0:T(4,128)(2,1)}, u32[]{:S(2)}) copy-start(bf16[4,3072]{1,0:T(4,128)(2,1)} %param.20) | copy-start | bytes 73732
  6.0 6.0 %copy-start.11 = (s32[160,3]{0,1:T(4,128)S(1)}, s32[160,3]{0,1:T(4,128)}, u32[]{:S(2)}) copy-start(s32[160,3]{0,1:T(4,128)} %param.16) | copy-start | bytes 5764
  6.0 6.0 %copy-start.12 = (f32[128]{0:T(128)S(1)}, f32[128]{0:T(128)}, u32[]{:S(2)}) copy-start(f32[128]{0:T(128)} %constant.52.clone) | copy-start | bytes 1540
  6.0 6.0 %copy-start.13 = (pred[128]{0:T(512)(128)(4,1)S(1)}, pred[128]{0:T(512)(128)(4,1)}, u32[]{:S(2)}) copy-start(pred[128]{0:T(512)(128)(4,1)} %constant.50.clone) | copy-start | bytes 388
  6.0 6.0 %copy-start.14 = (pred[128]{0:T(512)(128)(4,1)S(1)}, pred[128]{0:T(512)(128)(4,1)}, u32[]{:S(2)}) copy-start(pred[128]{0:T(512)(128)(4,1)} %constant.51.clone) | copy-start | bytes 388
  6.1 11.0 %copy-start.1 = (bf16[160,1536]{1,0:T(8,128)(2,1)S(1)}, bf16[160,1536]{1,0:T(8,128)(2,1)}, u32[]{:S(2)}) copy-start(bf16[160,1536]{1,0:T(8,128)(2,1)} %refs_2_.3) | copy-start | bytes 1474564
  6.1 22.8 %collective-permute-start.7 = (bf16[160,384]{1,0:T(8,128)(2,1)S(1)}, bf16[160,384]{1,0:T(8,128)(2,1)S(1)}, u32[]{:S(2)}, u32[]{:S(2)}) collective-permute-start(bf16[160,384]{1,0:T(8,128)(2,1)S(1)} %get-tuple-element.26), channel_id=1, source_target_pairs={{0,1},{1,0},{2,3},{3,2},{4,5},{5,4},{6,7},{7,6},{8,9},{9,8},{10,11... | collective-permute-start | bytes 368648 | tf_op jit(solution)/shard_map/ppermute | solution.py:20
  7.7 21.2 %collective-permute-start.8 = (bf16[160,384]{1,0:T(8,128)(2,1)S(1)}, bf16[160,384]{1,0:T(8,128)(2,1)S(1)}, u32[]{:S(2)}, u32[]{:S(2)}) collective-permute-start(bf16[160,384]{1,0:T(8,128)(2,1)S(1)} %get-tuple-element.27), channel_id=1, source_target_pairs={{0,2},{1,3},{2,0},{3,1},{4,6},{5,7},{6,4},{7,5},{8,10},{9,11},{10,... | collective-permute-start | bytes 368648 | tf_op jit(solution)/shard_map/ppermute | solution.py:20
  10.3 20.4 %collective-permute-start.9 = (bf16[160,384]{1,0:T(8,128)(2,1)S(1)}, bf16[160,384]{1,0:T(8,128)(2,1)S(1)}, u32[]{:S(2)}, u32[]{:S(2)}) collective-permute-start(bf16[160,384]{1,0:T(8,128)(2,1)S(1)} %get-tuple-element.28), channel_id=1, source_target_pairs={{0,3},{1,2},{2,1},{3,0},{4,7},{5,6},{6,5},{7,4},{8,11},{9,10},{10,... | collective-permute-start | bytes 368648 | tf_op jit(solution)/shard_map/ppermute | solution.py:20
  10.8 3.9 %collective-permute-start.19 = (bf16[2,4,1536]{2,1,0:T(4,128)(2,1)S(1)}, bf16[2,4,1536]{2,1,0:T(4,128)(2,1)S(1)}, u32[]{:S(2)}, u32[]{:S(2)}) collective-permute-start(bf16[2,4,1536]{2,1,0:T(4,128)(2,1)S(1)} %get-tuple-element.41), channel_id=1, source_target_pairs={{0,16},{16,0},{1,17},{17,1},{2,18},{18,2},{3,19},{19,3},{4,20},{20... | collective-permute-start | bytes 73736 | tf_op jit(solution)/shard_map/ppermute | solution.py:20
  14.8 4.4 %collective-permute-start.20 = (bf16[2,8,1536]{2,1,0:T(8,128)(2,1)S(1)}, bf16[2,8,1536]{2,1,0:T(8,128)(2,1)S(1)}, u32[]{:S(2)}, u32[]{:S(2)}) collective-permute-start(bf16[2,8,1536]{2,1,0:T(8,128)(2,1)S(1)} %pad_maximum_fusion.3), channel_id=1, source_target_pairs={{0,8},{4,12},{8,0},{12,4},{1,9},{5,13},{9,1},{13,5},{2,10},{6,14},... | collective-permute-start | bytes 147464 | tf_op jit(solution)/shard_map/ppermute | solution.py:20
  16.3 0.7 copy-start.9
  16.3 0.7 copy-start.10
  16.4 2.1 %copy-start.3 = (bf16[160,1536]{1,0:T(8,128)(2,1)S(1)}, bf16[160,1536]{1,0:T(8,128)(2,1)}, u32[]{:S(2)}) copy-start(bf16[160,1536]{1,0:T(8,128)(2,1)} %refs_2_.2) | copy-start | bytes 1474564
  17.8 20.5 %collective-permute-start.1 = (bf16[160,384]{1,0:T(8,128)(2,1)S(1)}, bf16[160,384]{1,0:T(8,128)(2,1)S(1)}, u32[]{:S(2)}, u32[]{:S(2)}) collective-permute-start(bf16[160,384]{1,0:T(8,128)(2,1)S(1)} %get-tuple-element.22), channel_id=1, source_target_pairs={{0,1},{1,0},{2,3},{3,2},{4,5},{5,4},{6,7},{7,6},{8,9},{9,8},{10,11... | collective-permute-start | bytes 368648 | tf_op jit(solution)/shard_map/ppermute | solution.py:20
  19.2 5.0 %copy-start.4 = (bf16[160,1536]{1,0:T(8,128)(2,1)S(1)}, bf16[160,1536]{1,0:T(8,128)(2,1)}, u32[]{:S(2)}) copy-start(bf16[160,1536]{1,0:T(8,128)(2,1)} %g_ref.1) | copy-start | bytes 1474564
  19.3 1.4 %collective-permute-start.21 = (bf16[2,16,1536]{2,1,0:T(8,128)(2,1)S(1)}, bf16[2,16,1536]{2,1,0:T(8,128)(2,1)S(1)}, u32[]{:S(2)}, u32[]{:S(2)}) collective-permute-start(bf16[2,16,1536]{2,1,0:T(8,128)(2,1)S(1)} %pad_maximum_fusion.1), channel_id=1, source_target_pairs={{0,4},{4,0},{8,12},{12,8},{1,5},{5,1},{9,13},{13,9},{2,6},{6,2},{1... | collective-permute-start | bytes 294920 | tf_op jit(solution)/shard_map/ppermute | solution.py:20
  20.6 28.3 %collective-permute-start.2 = (bf16[160,384]{1,0:T(8,128)(2,1)S(1)}, bf16[160,384]{1,0:T(8,128)(2,1)S(1)}, u32[]{:S(2)}, u32[]{:S(2)}) collective-permute-start(bf16[160,384]{1,0:T(8,128)(2,1)S(1)} %get-tuple-element.23), channel_id=1, source_target_pairs={{0,2},{1,3},{2,0},{3,1},{4,6},{5,7},{6,4},{7,5},{8,10},{9,11},{10,... | collective-permute-start | bytes 368648 | tf_op jit(solution)/shard_map/ppermute | solution.py:20
  28.9 1.4 %collective-permute-start.22 = (f32[2,16,1536]{2,1,0:T(8,128)S(1)}, f32[2,16,1536]{2,1,0:T(8,128)S(1)}, u32[]{:S(2)}, u32[]{:S(2)}) collective-permute-start(f32[2,16,1536]{2,1,0:T(8,128)S(1)} %get-tuple-element.35), channel_id=1, source_target_pairs={{0,4},{4,0},{8,12},{12,8},{1,5},{5,1},{9,13},{13,9},{2,6},{6,2},{1... | collective-permute-start | bytes 589832 | tf_op jit(solution)/shard_map/ppermute | solution.py:20
  28.9 24.8 %collective-permute-start.3 = (bf16[160,384]{1,0:T(8,128)(2,1)S(1)}, bf16[160,384]{1,0:T(8,128)(2,1)S(1)}, u32[]{:S(2)}, u32[]{:S(2)}) collective-permute-start(bf16[160,384]{1,0:T(8,128)(2,1)S(1)} %get-tuple-element.24), channel_id=1, source_target_pairs={{0,3},{1,2},{2,1},{3,0},{4,7},{5,6},{6,5},{7,4},{8,11},{9,10},{10,... | collective-permute-start | bytes 368648 | tf_op jit(solution)/shard_map/ppermute | solution.py:20
  30.3 28.6 %collective-permute-start.13 = (bf16[160,384]{1,0:T(8,128)(2,1)S(1)}, bf16[160,384]{1,0:T(8,128)(2,1)S(1)}, u32[]{:S(2)}, u32[]{:S(2)}) collective-permute-start(bf16[160,384]{1,0:T(8,128)(2,1)S(1)} %get-tuple-element.29), channel_id=1, source_target_pairs={{0,1},{1,0},{2,3},{3,2},{4,5},{5,4},{6,7},{7,6},{8,9},{9,8},{10,11... | collective-permute-start | bytes 368648 | tf_op jit(solution)/shard_map/ppermute | solution.py:20
  30.8 4.7 %collective-permute-start.23 = (f32[2,8,1536]{2,1,0:T(8,128)S(1)}, f32[2,8,1536]{2,1,0:T(8,128)S(1)}, u32[]{:S(2)}, u32[]{:S(2)}) collective-permute-start(f32[2,8,1536]{2,1,0:T(8,128)S(1)} %slice.40), channel_id=1, source_target_pairs={{0,8},{4,12},{8,0},{12,4},{1,9},{5,13},{9,1},{13,5},{2,10},{6,14},... | collective-permute-start | bytes 294920 | tf_op jit(solution)/shard_map/ppermute | solution.py:20
  35.4 40.9 %collective-permute-start.15 = (bf16[160,384]{1,0:T(8,128)(2,1)S(1)}, bf16[160,384]{1,0:T(8,128)(2,1)S(1)}, u32[]{:S(2)}, u32[]{:S(2)}) collective-permute-start(bf16[160,384]{1,0:T(8,128)(2,1)S(1)} %get-tuple-element.30), channel_id=1, source_target_pairs={{0,2},{1,3},{2,0},{3,1},{4,6},{5,7},{6,4},{7,5},{8,10},{9,11},{10,... | collective-permute-start | bytes 368648 | tf_op jit(solution)/shard_map/ppermute | solution.py:20
  38.3 9.4 %collective-permute-start.24 = (f32[2,8,1536]{2,1,0:T(8,128)S(1)}, f32[2,8,1536]{2,1,0:T(8,128)S(1)}, u32[]{:S(2)}, u32[]{:S(2)}) collective-permute-start(f32[2,8,1536]{2,1,0:T(8,128)S(1)} %slice_add_fusion), channel_id=1, source_target_pairs={{0,2},{1,3},{2,0},{3,1},{4,6},{5,7},{6,4},{7,5},{8,10},{9,11},{10,... | collective-permute-start | bytes 294920 | tf_op jit(solution)/shard_map/ppermute | solution.py:20
  47.7 14.0 %collective-permute-start.10 = (bf16[640,384]{1,0:T(8,128)(2,1)S(1)}, bf16[640,384]{1,0:T(8,128)(2,1)S(1)}, u32[]{:S(2)}, u32[]{:S(2)}) collective-permute-start(bf16[640,384]{1,0:T(8,128)(2,1)S(1)} %constant_dynamic-update-slice_fusion.4.refs_4_), channel_id=1, source_target_pairs={{0,8},{4,12},{8,0},{12,4},{1,9},{5,13},{9,1},{13,5},{2,10},{6,14},... | collective-permute-start | bytes 1474568 | tf_op jit(solution)/shard_map/ppermute | solution.py:20
  49.0 4.7 %collective-permute-start.25 = (f32[2,8,1536]{2,1,0:T(8,128)S(1)}, f32[2,8,1536]{2,1,0:T(8,128)S(1)}, u32[]{:S(2)}, u32[]{:S(2)}) collective-permute-start(f32[2,8,1536]{2,1,0:T(8,128)S(1)} %add.41), channel_id=1, source_target_pairs={{0,1},{1,0},{2,3},{3,2},{4,5},{5,4},{6,7},{7,6},{8,9},{9,8},{10,11... | collective-permute-start | bytes 294920 | tf_op jit(solution)/shard_map/ppermute | solution.py:20
  53.6 8.0 %collective-permute-start.11 = (bf16[640,384]{1,0:T(8,128)(2,1)S(1)}, bf16[640,384]{1,0:T(8,128)(2,1)S(1)}, u32[]{:S(2)}, u32[]{:S(2)}) collective-permute-start(bf16[640,384]{1,0:T(8,128)(2,1)S(1)} %constant_dynamic-update-slice_fusion.4.refs_4_), channel_id=1, source_target_pairs={{0,4},{4,0},{8,12},{12,8},{1,5},{5,1},{9,13},{13,9},{2,6},{6,2},{1... | collective-permute-start | bytes 1474568 | tf_op jit(solution)/shard_map/ppermute | solution.py:20
  53.7 4.2 %collective-permute-start.26 = (f32[2,4,1536]{2,1,0:T(4,128)S(1)}, f32[2,4,1536]{2,1,0:T(4,128)S(1)}, u32[]{:S(2)}, u32[]{:S(2)}) collective-permute-start(f32[2,4,1536]{2,1,0:T(4,128)S(1)} %get-tuple-element.38), channel_id=1, source_target_pairs={{0,16},{16,0},{1,17},{17,1},{2,18},{18,2},{3,19},{19,3},{4,20},{20... | collective-permute-start | bytes 147464 | tf_op jit(solution)/shard_map/ppermute | solution.py:20
  57.9 12.9 %collective-permute-start.4 = (bf16[640,384]{1,0:T(8,128)(2,1)S(1)}, bf16[640,384]{1,0:T(8,128)(2,1)S(1)}, u32[]{:S(2)}, u32[]{:S(2)}) collective-permute-start(bf16[640,384]{1,0:T(8,128)(2,1)S(1)} %constant_dynamic-update-slice_fusion.refs_0_), channel_id=1, source_target_pairs={{0,8},{4,12},{8,0},{12,4},{1,9},{5,13},{9,1},{13,5},{2,10},{6,14},... | collective-permute-start | bytes 1474568 | tf_op jit(solution)/shard_map/ppermute | solution.py:20
  58.9 24.1 %collective-permute-start.17 = (bf16[160,384]{1,0:T(8,128)(2,1)S(1)}, bf16[160,384]{1,0:T(8,128)(2,1)S(1)}, u32[]{:S(2)}, u32[]{:S(2)}) collective-permute-start(bf16[160,384]{1,0:T(8,128)(2,1)S(1)} %get-tuple-element.31), channel_id=1, source_target_pairs={{0,3},{1,2},{2,1},{3,0},{4,7},{5,6},{6,5},{7,4},{8,11},{9,10},{10,... | collective-permute-start | bytes 368648 | tf_op jit(solution)/shard_map/ppermute | solution.py:20
  61.7 9.8 %collective-permute-start.5 = (bf16[640,384]{1,0:T(8,128)(2,1)S(1)}, bf16[640,384]{1,0:T(8,128)(2,1)S(1)}, u32[]{:S(2)}, u32[]{:S(2)}) collective-permute-start(bf16[640,384]{1,0:T(8,128)(2,1)S(1)} %constant_dynamic-update-slice_fusion.refs_0_), channel_id=1, source_target_pairs={{0,4},{4,0},{8,12},{12,8},{1,5},{5,1},{9,13},{13,9},{2,6},{6,2},{1... | collective-permute-start | bytes 1474568 | tf_op jit(solution)/shard_map/ppermute | solution.py:20
  61.7 9.8 %collective-permute-start.12 = (bf16[640,384]{1,0:T(8,128)(2,1)S(1)}, bf16[640,384]{1,0:T(8,128)(2,1)S(1)}, u32[]{:S(2)}, u32[]{:S(2)}) collective-permute-start(bf16[640,384]{1,0:T(8,128)(2,1)S(1)} %collective-permute-done.10.refs_5_), channel_id=1, source_target_pairs={{0,4},{4,0},{8,12},{12,8},{1,5},{5,1},{9,13},{13,9},{2,6},{6,2},{1... | collective-permute-start | bytes 1474568 | tf_op jit(solution)/shard_map/ppermute | solution.py:20
  70.8 1.9 %collective-permute-start.6 = (bf16[640,384]{1,0:T(8,128)(2,1)S(1)}, bf16[640,384]{1,0:T(8,128)(2,1)S(1)}, u32[]{:S(2)}, u32[]{:S(2)}) collective-permute-start(bf16[640,384]{1,0:T(8,128)(2,1)S(1)} %collective-permute-done.4.refs_1_), channel_id=1, source_target_pairs={{0,4},{4,0},{8,12},{12,8},{1,5},{5,1},{9,13},{13,9},{2,6},{6,2},{1... | collective-permute-start | bytes 1474568 | tf_op jit(solution)/shard_map/ppermute | solution.py:20
  76.3 16.1 %collective-permute-start.14 = (bf16[160,384]{1,0:T(8,128)(2,1)S(1)}, bf16[160,384]{1,0:T(8,128)(2,1)S(1)}, u32[]{:S(2)}, u32[]{:S(2)}) collective-permute-start(bf16[160,384]{1,0:T(8,128)(2,1)S(1)} %shard_map.161), channel_id=1, source_target_pairs={{0,1},{1,0},{2,3},{3,2},{4,5},{5,4},{6,7},{7,6},{8,9},{9,8},{10,11... | collective-permute-start | bytes 368648 | tf_op jit(solution)/shard_map/ppermute | solution.py:20
  80.0 12.4 %collective-permute-start.16 = (bf16[160,384]{1,0:T(8,128)(2,1)S(1)}, bf16[160,384]{1,0:T(8,128)(2,1)S(1)}, u32[]{:S(2)}, u32[]{:S(2)}) collective-permute-start(bf16[160,384]{1,0:T(8,128)(2,1)S(1)} %shard_map.162), channel_id=1, source_target_pairs={{0,2},{1,3},{2,0},{3,1},{4,6},{5,7},{6,4},{7,5},{8,10},{9,11},{10,... | collective-permute-start | bytes 368648 | tf_op jit(solution)/shard_map/ppermute | solution.py:20
  86.6 6.8 %collective-permute-start.18 = (bf16[160,384]{1,0:T(8,128)(2,1)S(1)}, bf16[160,384]{1,0:T(8,128)(2,1)S(1)}, u32[]{:S(2)}, u32[]{:S(2)}) collective-permute-start(bf16[160,384]{1,0:T(8,128)(2,1)S(1)} %shard_map.163), channel_id=1, source_target_pairs={{0,3},{1,2},{2,1},{3,0},{4,7},{5,6},{6,5},{7,4},{8,11},{9,10},{10,... | collective-permute-start | bytes 368648 | tf_op jit(solution)/shard_map/ppermute | solution.py:20

commit v2 on v1

v2 whole, which is shorter than its diff:
```python
import functools
import math

import jax
import jax.numpy as jnp
import numpy as np
from jax import lax
from jax.experimental import pallas as pl
from jax.experimental.pallas import tpu as pltpu
from jax.sharding import PartitionSpec as P

HEAD_DIM = 128
eps = 1e-06
LOG2E = 1.4426950408889634
NT = (((1,), (1,)), ((), ()))
TN = (((0,), (0,)), ((), ()))
VMEM_LIMIT = 20 * 1024 * 1024


def swap(x, axis, size, k):
    return lax.ppermute(x, axis, [(i, i ^ k) for i in range(size)])


def after(x, *others):
    return lax.optimization_barrier((x, *others))[0]


def swap_two(x, n_enc, k, n_col, j):
    moves = [
        (e * n_col + c, (e ^ k) * n_col + (c ^ j)) for e in range(n_enc) for c in range(n_col)
    ]
    return lax.ppermute(x, ("enc", "col"), moves)


def kernel_call(body, out_shape, cost=(0, 0, 0), **kw):
    return pl.pallas_call(
        body,
        out_shape=out_shape,
        compiler_params=pltpu.CompilerParams(vmem_limit_bytes=VMEM_LIMIT),
        cost_estimate=pl.CostEstimate(flops=cost[0], bytes_accessed=cost[1], transcendentals=cost[2]),
        **kw,
    )


def rope_tables(positions):
    half = HEAD_DIM // 2
    part_side = HEAD_DIM // 6
    part_time = half - 2 * part_side
    freq_time = 1.0 / 10000.0 ** (jnp.arange(part_time, dtype=jnp.float32) * 2.0 / (2 * part_time))
    freq_side = 1.0 / 10000.0 ** (jnp.arange(part_side, dtype=jnp.float32) * 2.0 / (2 * part_side))
    freq = jnp.repeat(jnp.concatenate([freq_time, freq_side, freq_side]), 2)
    pair = np.arange(HEAD_DIM) // 2
    coords = positions.astype(jnp.float32)
    coord = jnp.where(
        pair < part_time,
        coords[:, 0:1],
        jnp.where(pair < part_time + part_side, coords[:, 1:2], coords[:, 2:3]),
    )
    angles = coord * freq
    sign = np.where(np.arange(HEAD_DIM) % 2 == 0, -1.0, 1.0).astype(np.float32)
    return jnp.cos(angles), jnp.sin(angles) * sign


def columns_of(axis, k, width):
    start = (lax.axis_index(axis) ^ k) * width
    return pl.ds(pl.multiple_of(start, HEAD_DIM), width)


def join_rows(pieces, others, axis):
    rows, width = pieces[0].shape
    parts = len(pieces)
    n = parts + len(others)

    def body(*refs):
        for k in range(parts):
            start = (lax.axis_index(axis) ^ k) * rows
            here = pl.ds(pl.multiple_of(start, math.gcd(rows, 32)), rows)
            refs[n][here, :] = refs[k][...]
            refs[n + 1][0, here, :] = refs[k][...]
        for i, ref in enumerate(refs[parts:n]):
            refs[n + 1][i + 1] = ref[...]

    return kernel_call(
        body,
        [
            jax.ShapeDtypeStruct((rows * parts, width), pieces[0].dtype),
            jax.ShapeDtypeStruct((1 + len(others), rows * parts, width), pieces[0].dtype),
        ],
    )(*pieces, *others)


def join_columns(pieces, axis):
    rows, piece = pieces[0].shape
    parts = len(pieces)

    def body(*refs):
        copies = [
            pltpu.make_async_copy(
                refs[k], refs[parts].at[:, columns_of(axis, k, piece)], refs[parts + 1].at[k]
            )
            for k in range(parts)
        ]
        for copy in copies:
            copy.start()
        for copy in copies:
            copy.wait()

    return kernel_call(
        body,
        jax.ShapeDtypeStruct((rows, piece * parts), pieces[0].dtype),
        in_specs=[pl.BlockSpec(memory_space=pl.ANY)] * parts,
        out_specs=pl.BlockSpec(memory_space=pl.ANY),
        scratch_shapes=[pltpu.SemaphoreType.DMA((parts,))],
    )(*pieces)


def split_sum(x, y, parts):
    kinds, count, width = x.shape
    part = count // parts

    def body(x_ref, y_ref, *outs):
        for k in range(parts):
            here = slice(k * part, (k + 1) * part)
            outs[k][...] = x_ref[:, here] + y_ref[:, here]

    return kernel_call(body, [jax.ShapeDtypeStruct((kinds, part, width), x.dtype)] * parts)(x, y)


def square_sums(queries, keys):
    rows, width = queries.shape

    def body(q_ref, k_ref, out_ref):
        for i, ref in enumerate((q_ref, k_ref)):
            wide = ref[...].astype(jnp.float32)
            out_ref[:, i : i + 1] = jnp.sum(wide * wide, axis=1, keepdims=True)

    return kernel_call(
        body, jax.ShapeDtypeStruct((rows, 2), jnp.float32), (4 * rows * width, 4 * rows * width, 0)
    )(queries, keys)


def context_factor(wide):
    return lax.rsqrt(jnp.mean(wide * wide, axis=1, keepdims=True) + eps)


def context_shards(keys, values, gain, width, axis, parts):
    rows = keys.shape[0]

    def body(k_ref, v_ref, gain_ref, *outs):
        wide = k_ref[...].astype(jnp.float32)
        recip = context_factor(wide)
        for k in range(parts):
            cols = columns_of(axis, k, width)
            part = k_ref[:, cols].astype(jnp.float32) * recip * gain_ref[:, cols]
            outs[k][0] = part.astype(jnp.bfloat16)
            outs[k][1] = v_ref[:, cols]

    return kernel_call(body, [jax.ShapeDtypeStruct((2, rows, width), jnp.bfloat16)] * parts)(
        keys, values, gain[None, :]
    )


def context_gradients(keys, gain, pieces, axis):
    rows, full = keys.shape
    parts = len(pieces)
    width = full // parts
    flat = [x for piece in pieces for x in piece]

    def body(k_ref, gain_ref, *refs):
        grad_ref, values_ref, scaled = refs[len(flat) :]
        at = 0
        for k, piece in enumerate(pieces):
            total = refs[at][...]
            for i in range(1, len(piece)):
                total = total + refs[at + i][...]
            at += len(piece)
            cols = columns_of(axis, k, width)
            scaled[:, cols] = gain_ref[:, cols] * total[0]
            values_ref[:, cols] = total[1]
        wide = k_ref[...].astype(jnp.float32)
        recip = context_factor(wide)
        inner = jnp.mean(wide * scaled[...], axis=1, keepdims=True)
        grad_ref[...] = recip * scaled[...] - wide * (recip * recip * recip) * inner

    return kernel_call(
        body,
        [jax.ShapeDtypeStruct((rows, full), jnp.float32)] * 2,
        scratch_shapes=[pltpu.VMEM((rows, full), jnp.float32)],
    )(keys, gain[None, :], *flat)


def norm_factor(total_refs, which, full_width):
    total = total_refs[0][:, which : which + 1]
    for ref in total_refs[1:]:
        total = total + ref[:, which : which + 1]
    return lax.rsqrt(total / full_width + eps)


def normed_turned(x, which, totals, gain, cosine, sine, full_width, axis, parts, relative):
    rows, width = x.shape
    piece = width // parts
    n_totals = len(totals)

    def body(*refs):
        x_ref, gain_ref, cos_ref, sin_ref = refs[n_totals : n_totals + 4]
        outs = refs[n_totals + 4 :]
        recip = norm_factor(refs[:n_totals], which, full_width)
        cos = cos_ref[...]
        sin = sin_ref[...]
        even = lax.broadcasted_iota(jnp.int32, cos.shape, 1) % 2 == 0
        for k in range(parts):
            for h in range(piece // HEAD_DIM):
                start = k * piece + h * HEAD_DIM
                if parts > 1 and relative:
                    start = pl.multiple_of(
                        (lax.axis_index(axis) ^ k) * piece + h * HEAD_DIM, HEAD_DIM
                    )
                cols = pl.ds(start, HEAD_DIM)
                here = slice(h * HEAD_DIM, (h + 1) * HEAD_DIM)
                normed = x_ref[:, cols].astype(jnp.float32) * recip * gain_ref[:, cols]
                other = jnp.where(
                    even, pltpu.roll(normed, HEAD_DIM - 1, 1), pltpu.roll(normed, 1, 1)
                )
                turned = (normed * cos + other * sin).astype(jnp.bfloat16)
                if relative:
                    outs[k][:, here] = turned
                else:
                    outs[0][k, :, here] = turned

    shapes = [(rows, piece)] * parts if relative else [(parts, rows, piece)]
    return kernel_call(body, [jax.ShapeDtypeStruct(sh, jnp.bfloat16) for sh in shapes])(
        *totals, x, gain[None, :], cosine, sine
    )


def attention(query, keys, values):
    rows, width = query.shape
    factor = HEAD_DIM ** (-0.5) * LOG2E
    heads = [slice(h, h + HEAD_DIM) for h in range(0, width, HEAD_DIM)]
    pairs = [x if isinstance(x, tuple) else (x, None) for x in (*keys, *values)]
    arrays = []
    for x, _ in pairs:
        if not any(x is y for y in arrays):
            arrays.append(x)
    places = [(next(i for i, y in enumerate(arrays) if y is x), at) for x, at in pairs]

    def body(q_ref, *refs):
        def part(place, cols):
            i, at = place
            return refs[i][:, cols] if at is None else refs[i][at, :, cols]

        def scores(cols):
            q = q_ref[:, cols]
            return [
                lax.dot_general(q, part(place, cols), NT, preferred_element_type=jnp.float32)
                for place in places[: len(keys)]
            ]

        following = scores(heads[0])
        for j, cols in enumerate(heads):
            current = following
            if j + 1 < len(heads):
                following = scores(heads[j + 1])
            peak = functools.reduce(
                jnp.maximum, [jnp.max(s, axis=1, keepdims=True) for s in current]
            )
            weight_sum = 0.0
            mixed = 0.0
            for s, place in zip(current, places[len(keys) :]):
                weights = jnp.exp2((s - peak) * factor)
                weight_sum = weight_sum + jnp.sum(weights, axis=1, keepdims=True)
                mixed = mixed + jnp.dot(
                    weights.astype(jnp.bfloat16),
                    part(place, cols),
                    preferred_element_type=jnp.float32,
                )
            refs[-1][:, cols] = (mixed / weight_sum).astype(jnp.bfloat16)

    return kernel_call(body, jax.ShapeDtypeStruct((rows, width), jnp.bfloat16))(query, *arrays)


def image_attention(queries, totals, gain, full_width, context, cotangent):
    rows, width = queries.shape
    n_totals = len(totals)
    count = context.shape[1]
    heads = width // HEAD_DIM
    half = count // 2
    scale = HEAD_DIM ** (-0.5)

    def body(*refs):
        q_ref, gain_ref, c_ref, g_ref, out_ref, keep_ref, send_ref = refs[n_totals:]
        recip = norm_factor(refs[:n_totals], 0, full_width)
        for h in range(heads):
            cols = slice(h * HEAD_DIM, (h + 1) * HEAD_DIM)
            q = (q_ref[:, cols].astype(jnp.float32) * recip * gain_ref[:, cols]).astype(jnp.bfloat16)
            g = g_ref[:, cols]
            k = c_ref[0, :, cols]
            v = c_ref[1, :, cols]
            scores = lax.dot_general(k, q, NT, preferred_element_type=jnp.float32) * scale
            weights = jnp.exp(scores - jnp.max(scores, axis=0, keepdims=True))
            probs = weights / jnp.sum(weights, axis=0, keepdims=True)
            low = probs.astype(jnp.bfloat16)
            out_ref[:, cols] = lax.dot_general(
                low, v, TN, preferred_element_type=jnp.float32
            ).astype(jnp.bfloat16)
            grad_v = jnp.dot(low, g, preferred_element_type=jnp.float32)
            grad_p = lax.dot_general(v, g, NT, preferred_element_type=jnp.float32)
            inner = jnp.sum(probs * grad_p, axis=0, keepdims=True)
            grad_s = (probs * (grad_p - inner)).astype(jnp.bfloat16)
            grad_k = jnp.dot(grad_s, q, preferred_element_type=jnp.float32) * scale
            for i, grad in enumerate((grad_k, grad_v)):
                keep_ref[i, :, cols] = grad[:half]
                send_ref[i, :, cols] = grad[half:]

    return kernel_call(
        body,
        [
            jax.ShapeDtypeStruct((rows, width), jnp.bfloat16),
            jax.ShapeDtypeStruct((2, half, width), jnp.float32),
            jax.ShapeDtypeStruct((2, half, width), jnp.float32),
        ],
        (10 * rows * count * width, 80 * rows * width, rows * count * heads),
    )(*totals, queries, gain[None, :], context, cotangent)


def per_device(
    sizes,
    queries,
    self_keys,
    self_values,
    positions,
    query_gain,
    key_gain,
    context_keys,
    context_values,
    context_gain,
    image_cotangent,
):
    n_enc, n_row, n_col = sizes
    rows, width = queries.shape
    heads = width // HEAD_DIM
    full_width = width * n_enc
    row_bits = [1 << i for i in reversed(range(n_row.bit_length() - 1))]
    parts = n_col if heads % n_col == 0 and len(row_bits) == 2 else 1

    def relay(x):
        if parts == 1:
            return x
        return lax.all_to_all(x, "col", split_axis=0, concat_axis=0, tiled=True)

    value_split = jnp.swapaxes(self_values.reshape(rows, parts, width // parts), 0, 1)
    values_here = relay(value_split)

    own_count = context_keys.shape[0]
    context = context_shards(after(context_keys, value_split), context_values, context_gain, width, "enc", n_enc)
    context = [swap(x, "enc", n_enc, k) if k else x for k, x in enumerate(context)]
    sums = square_sums(after(queries, context[0]), self_keys)
    totals = [sums]
    bit = 1
    while bit < n_enc:
        if len(totals) > 1:
            totals = [totals[0] + totals[1]]
        totals = [totals[0], swap(totals[0], "enc", n_enc, bit)]
        bit *= 2
    cosine, sine = rope_tables(after(positions, sums))
    key_pieces = normed_turned(
        self_keys, 1, totals, key_gain, cosine, sine, full_width, "col", parts, True
    )
    context = jnp.concatenate(context, axis=1)
    bit = n_row // 2
    while bit:
        other = after(swap(context, "row", n_row, bit), key_pieces[0])
        context = jnp.concatenate([context, other], axis=1)
        bit //= 2
    key_pieces = [swap(x, "col", n_col, k) if k else x for k, x in enumerate(key_pieces)]

    values_here = after(values_here, key_pieces[0]).reshape(parts * rows, width // parts)
    image_out, grad, sent = image_attention(
        queries, totals, query_gain, full_width, after(context, values_here), image_cotangent
    )
    all_values = [values_here]
    if parts > 1:
        all_values += [swap(values_here, "row", n_row, row_bits[0])]
    key_pieces = [key_pieces[0], *(after(x, grad) for x in key_pieces[1:])]
    keys_here, bundle = join_rows(key_pieces, all_values, "col")
    query_here = normed_turned(
        after(queries, keys_here), 0, totals, query_gain, cosine, sine, full_width, "col", parts, True
    )
    got = keys_here
    if parts > 1:
        keys_there = swap(keys_here, "row", n_row, row_bits[0])
        query_here = [swap(x, "col", n_col, k) if k else x for k, x in enumerate(query_here)]
        got = swap(bundle, "row", n_row, row_bits[1])
        all_values += [(got, 1), (got, 2)]
        all_keys = [keys_here, keys_there, (got, 0)]
    else:
        all_keys = [lax.all_gather(keys_here, ("row", "col"), axis=0, tiled=True)]
        all_values = [lax.all_gather(values_here, ("row", "col"), axis=0, tiled=True)]

    for i in range(len(row_bits)):
        got = swap(after(sent, got), "row", n_row, 1 << i)
        if i + 1 < len(row_bits):
            grad, sent = split_sum(grad, got, 2)
        else:
            grad = split_sum(grad, got, 1)[0]
    if parts > 1:
        keys_there = after(keys_there, grad, *query_here)
        all_keys += [swap(keys_there, "row", n_row, row_bits[1])]

    mixed = [None] * parts
    col_bits = [1 << i for i in reversed(range(n_col.bit_length() - 1))]
    for bit in col_bits[:-1]:
        got = swap(grad, "col", n_col, bit)
        if bit > 2:
            grad = split_sum(grad, got, 1)[0]
    for i, k in enumerate(reversed(range(parts))):
        piece = attention(query_here[k], all_keys, all_values)
        mixed[k] = swap(piece, "col", n_col, k) if k else piece
        if i == min(1, parts - 1):
            got = after(got, piece)
    sent = split_sum(grad, got, n_enc)
    grad = []
    for k, x in enumerate(sent):
        grad.append([swap(x, "enc", n_enc, k) if k else x, swap_two(x, n_enc, k, n_col, col_bits[-1])])
    grad[0][0] = after(grad[0][0], mixed[0])
    grad_keys_in, grad_values_in = context_gradients(context_keys, context_gain, grad, "enc")
    self_out = join_columns(mixed, "col") if parts > 1 else mixed[0]

    return (self_out, image_out, grad_keys_in, grad_values_in)


def solution(mesh):
    sizes = tuple(mesh.shape[a] for a in ("enc", "row", "col"))
    return jax.shard_map(
        functools.partial(per_device, sizes),
        mesh=mesh,
        in_specs=(
            P(("row", "col"), "enc"),
            P(("row", "col"), "enc"),
            P(("row", "col"), "enc"),
            P(("row", "col"), None),
            P("enc"),
            P("enc"),
            P(("enc", "row"), None),
            P(("enc", "row"), None),
            P(),
            P(("row", "col"), "enc"),
        ),
        out_specs=(
            P(("row", "col"), "enc"),
            P(("row", "col"), "enc"),
            P(("enc", "row"), None),
            P(("enc", "row"), None),
        ),
        check_vma=False,
    )
```

time: 94.5 us -> 81.6 us (0.86)
  waiting for transfers between devices: 35.7 us -> 28.8 us
  Pallas kernels: 21.7 us -> 16.1 us
  starting transfers between devices: 30 us -> 32.7 us
  other arithmetic: 2.5 us -> 0.64 us
  local copies, waits for them, and re-layouts: 3.23 us -> 2.23 us
    ppermute x27 -> x21, waiting for transfers between devices: 35.7 us -> 18.1 us  [swap(): return lax.ppermute(x, axis, [(i, i ^ k) for i in range(size)])]
    ppermute x0 -> x2, waiting for transfers between devices: none -> 6.9 us  [swap_two(): return lax.ppermute(x, ('enc', 'col'), moves)]
    all_to_all x0 -> x1, starting transfers between devices: none -> 6.45 us  [relay(): return lax.all_to_all(x, 'col', split_axis=0, concat_axis=0, tiled=True)]
    pallas_call x7 -> x12, Pallas kernels: 15.9 us -> 10.3 us  [the longest x4 7.78 us: attention(): kernel_call(body, jax.ShapeDtypeStruct((rows, width), jnp.bfloat16))]
    ppermute x27 -> x21, starting transfers between devices: 30 us -> 24.5 us  [swap(): return lax.ppermute(x, axis, [(i, i ^ k) for i in range(size)])]
    all_to_all x0 -> x1, waiting for transfers between devices: none -> 3.79 us  [relay(): return lax.all_to_all(x, 'col', split_axis=0, concat_axis=0, tiled=True)]
    unnamed x36 -> x24, local copies, waits for them, and re-layouts: 2.9 us -> 0.06 us
    reshape x1, local copies, waits for them, and re-layouts: 0.03 us -> 1.93 us  [per_device(): self_values.reshape(rows, parts, width // parts)]
  transfers between devices with their start and end apart: 27 -> 24, of which waited for: 10 -> 9; matrix products, arithmetic and copies ran while one was open for 3% -> 1% of each run, Pallas kernels for 22% -> 19%
where the time goes in v2:
time: 81.6 us; the launch traced here: 81.4 us
  starting transfers between devices  32.7 us (40%)
  waiting for transfers between devices  28.8 us (35%)
  Pallas kernels  16.1 us (20%)
  local copies, waits for them, and re-layouts  2.23 us (3%)
  between operations  0.94 us (1%)
    ppermute x21, starting transfers between devices, swap(): return lax.ppermute(x, axis, [(i, i ^ k) for i in range(size)])  24.5 us
    ppermute x21, waiting for transfers between devices, swap(): return lax.ppermute(x, axis, [(i, i ^ k) for i in range(size)])  18.1 us
    pallas_call x4, Pallas kernels, attention(): kernel_call(body, jax.ShapeDtypeStruct((rows, width), jnp.bfloat16))  7.78 us
    ppermute x2, waiting for transfers between devices, swap_two(): return lax.ppermute(x, ('enc', 'col'), moves)  6.9 us
    all_to_all x1, starting transfers between devices, relay(): return lax.all_to_all(x, 'col', split_axis=0, concat_axis=0, tiled=True)  6.45 us
    pallas_call x1, Pallas kernels, image_attention(): kernel_call(body, [jax.ShapeDtypeStruct((rows, width), jnp.bfloat16), jax...  4.78 us
    all_to_all x1, waiting for transfers between devices, relay(): return lax.all_to_all(x, 'col', split_axis=0, concat_axis=0, tiled=True)  3.79 us
    reshape x1, local copies, waits for them, and re-layouts, per_device(): self_values.reshape(rows, parts, width // parts)  1.93 us
  transfers between devices with their start and end apart: 24, of which 9 were waited for; matrix products, arithmetic and copies ran while one was open for 1% of the time, Pallas kernels for 19%

profile of v2, /device:TPU:0, one launch (start us, length us, event | category | flops | bytes accessed | tf_op | source)
XLA Modules:
  0.0 81.4 jit_solution(2284111255430059318)
XLA Ops:
  0.7 1.9 %copy.21 = bf16[20,4,8,384]{3,2,0,1:T(8,128)(2,1)} copy(bf16[20,4,8,384]{3,2,1,0:T(8,128)(2,1)} %bitcast.20) | data formatting | bytes 983040 | tf_op jit(solution)/shard_map/reshape | solution.py:351
  2.7 6.4 %all-to-all-start = ((bf16[4,160,384]{2,1,0:T(8,128)(2,1)}), bf16[4,160,384]{2,1,0:T(8,128)(2,1)S(1)}, u32[]{:S(2)}, u32[]{:S(2)}) async-start(bf16[4,160,384]{2,1,0:T(8,128)(2,1)} %bitcast.11), calls=%async_computation | async-start | bytes 983040 | tf_op jit(solution)/shard_map/all_to_all | solution.py:349
  9.1 0.1 shard_map.156
  9.3 0.3 shard_map.157.refs_0_
  9.6 1.5 %collective-permute-start = (f32[160,2]{1,0:T(8,128)S(1)}, f32[160,2]{1,0:T(8,128)S(1)}, u32[]{:S(2)}, u32[]{:S(2)}) collective-permute-start(f32[160,2]{1,0:T(8,128)S(1)} %shard_map.157.refs_0_), channel_id=1, source_target_pairs={{0,16},{16,0},{1,17},{17,1},{2,18},{18,2},{3,19},{19,3},{4,20},{20... | collective-permute-start | bytes 3848 | tf_op jit(solution)/shard_map/ppermute | solution.py:21
  11.1 0.5 collective-permute-start.2
  11.7 0.1 pad_maximum_fusion.3
  11.8 0.1 broadcast_in_dim.63
  11.8 0.1 mul.20
  12.0 2.9 %collective-permute-done.2 = bf16[2,4,1536]{2,1,0:T(4,128)(2,1)S(1)} collective-permute-done((bf16[2,4,1536]{2,1,0:T(4,128)(2,1)S(1)}, bf16[2,4,1536]{2,1,0:T(4,128)(2,1)S(1)}, u32[]{:S(2)}, u32[]{:S(2)}) %collective-permute-start.2) | collective-permute-done | bytes 24608 | tf_op jit(solution)/shard_map/ppermute | solution.py:21
  15.0 1.6 %collective-permute-start.3 = (bf16[2,8,1536]{2,1,0:T(8,128)(2,1)S(1)}, bf16[2,8,1536]{2,1,0:T(8,128)(2,1)S(1)}, u32[]{:S(2)}, u32[]{:S(2)}) collective-permute-start(bf16[2,8,1536]{2,1,0:T(8,128)(2,1)S(1)} %pad_maximum_fusion.2), channel_id=1, source_target_pairs={{0,8},{4,12},{8,0},{12,4},{1,9},{5,13},{9,1},{13,5},{2,10},{6,14},... | collective-permute-start | bytes 147464 | tf_op jit(solution)/shard_map/ppermute | solution.py:21
  16.6 0.4 sine_multiply_fusion
  17.0 0.7 shard_map.158
  17.7 1.4 %collective-permute-done.3 = bf16[2,8,1536]{2,1,0:T(8,128)(2,1)S(1)} collective-permute-done((bf16[2,8,1536]{2,1,0:T(8,128)(2,1)S(1)}, bf16[2,8,1536]{2,1,0:T(8,128)(2,1)S(1)}, u32[]{:S(2)}, u32[]{:S(2)}) %collective-permute-start.3) | collective-permute-done | bytes 49184 | tf_op jit(solution)/shard_map/ppermute | solution.py:21
  19.1 3.8 %all-to-all-done = bf16[4,160,384]{2,1,0:T(8,128)(2,1)S(1)} async-done(((bf16[4,160,384]{2,1,0:T(8,128)(2,1)}), bf16[4,160,384]{2,1,0:T(8,128)(2,1)S(1)}, u32[]{:S(2)}, u32[]{:S(2)}) %all-to-all-start) | async-done | bytes 491552 | tf_op jit(solution)/shard_map/all_to_all | solution.py:349
  22.9 1.5 %collective-permute-start.7 = (bf16[640,384]{1,0:T(8,128)(2,1)S(1)}, bf16[640,384]{1,0:T(8,128)(2,1)S(1)}, u32[]{:S(2)}, u32[]{:S(2)}) collective-permute-start(bf16[640,384]{1,0:T(8,128)(2,1)S(1)} %bitcast.12), channel_id=1, source_target_pairs={{0,8},{4,12},{8,0},{12,4},{1,9},{5,13},{9,1},{13,5},{2,10},{6,14},... | collective-permute-start | bytes 1474568 | tf_op jit(solution)/shard_map/ppermute | solution.py:21
  24.5 0.1 collective-permute-start.4
  24.6 1.5 %collective-permute-start.6 = (bf16[160,384]{1,0:T(8,128)(2,1)S(1)}, bf16[160,384]{1,0:T(8,128)(2,1)S(1)}, u32[]{:S(2)}, u32[]{:S(2)}) collective-permute-start(bf16[160,384]{1,0:T(8,128)(2,1)S(1)} %get-tuple-element.56), channel_id=1, source_target_pairs={{0,3},{1,2},{2,1},{3,0},{4,7},{5,6},{6,5},{7,4},{8,11},{9,10},{10,... | collective-permute-start | bytes 368648 | tf_op jit(solution)/shard_map/ppermute | solution.py:21
  26.1 2.9 %collective-permute-start.1 = (bf16[160,384]{1,0:T(8,128)(2,1)S(1)}, bf16[160,384]{1,0:T(8,128)(2,1)S(1)}, u32[]{:S(2)}, u32[]{:S(2)}) collective-permute-start(bf16[160,384]{1,0:T(8,128)(2,1)S(1)} %get-tuple-element.46), channel_id=1, source_target_pairs={{0,1},{1,0},{2,3},{3,2},{4,5},{5,4},{6,7},{7,6},{8,9},{9,8},{10,11... | collective-permute-start | bytes 368648 | tf_op jit(solution)/shard_map/ppermute | solution.py:21
  29.1 4.8 %shard_map.159 = (bf16[160,1536]{1,0:T(8,128)(2,1)}, f32[2,16,1536]{2,1,0:T(8,128)S(1)}, f32[2,16,1536]{2,1,0:T(8,128)S(1)}) custom-call(f32[160,2]{1,0:T(8,128)S(1)} %shard_map.157.refs_0_, f32[160,2]{1,0:T(8,128)S(1)} %collective-permute-done.refs_1_, bf16[160,1536]{1,0:T(8,128)(2,1)S(1)} %copy-done, f32[1,1536]{1,0:T(1,128)S(1)} %broadcast_in_dim.64.refs_3_, ...), custom_call_target="tpu_custom_call" | custom-call | flops 78643200 | bytes 19660800 | tf_op jit(solution)/shard_map/pallas_call | solution.py:315
  33.9 3.6 %collective-permute-done.5.refs_2_ = bf16[160,384]{1,0:T(8,128)(2,1)S(1)} collective-permute-done((bf16[160,384]{1,0:T(8,128)(2,1)S(1)}, bf16[160,384]{1,0:T(8,128)(2,1)S(1)}, u32[]{:S(2)}, u32[]{:S(2)}) %collective-permute-start.5) | collective-permute-done | bytes 122912 | tf_op jit(solution)/shard_map/ppermute | solution.py:21
  37.5 0.2 shard_map.160
  37.6 0.1 collective-permute-start.9
  37.8 0.5 collective-permute-start.8
  38.3 2.7 %collective-permute-done.9.refs_2_ = bf16[3,640,384]{2,1,0:T(8,128)(2,1)S(1)} collective-permute-done((bf16[3,640,384]{2,1,0:T(8,128)(2,1)S(1)}, bf16[3,640,384]{2,1,0:T(8,128)(2,1)S(1)}, u32[]{:S(2)}, u32[]{:S(2)}) %collective-permute-start.9) | collective-permute-done | bytes 1474592 | tf_op jit(solution)/shard_map/ppermute | solution.py:21
  41.0 0.1 collective-permute-start.10
  41.1 0.7 shard_map.161
  41.8 0.1 collective-permute-start.12
  41.9 2.0 %collective-permute-start.13 = (bf16[160,384]{1,0:T(8,128)(2,1)S(1)}, bf16[160,384]{1,0:T(8,128)(2,1)S(1)}, u32[]{:S(2)}, u32[]{:S(2)}) collective-permute-start(bf16[160,384]{1,0:T(8,128)(2,1)S(1)} %get-tuple-element.68), channel_id=1, source_target_pairs={{0,2},{1,3},{2,0},{3,1},{4,6},{5,7},{6,4},{7,5},{8,10},{9,11},{10,... | collective-permute-start | bytes 368648 | tf_op jit(solution)/shard_map/ppermute | solution.py:21
  43.9 2.4 %collective-permute-start.14 = (bf16[160,384]{1,0:T(8,128)(2,1)S(1)}, bf16[160,384]{1,0:T(8,128)(2,1)S(1)}, u32[]{:S(2)}, u32[]{:S(2)}) collective-permute-start(bf16[160,384]{1,0:T(8,128)(2,1)S(1)} %get-tuple-element.69), channel_id=1, source_target_pairs={{0,3},{1,2},{2,1},{3,0},{4,7},{5,6},{6,5},{7,4},{8,11},{9,10},{10,... | collective-permute-start | bytes 368648 | tf_op jit(solution)/shard_map/ppermute | solution.py:21
  46.3 0.6 collective-permute-start.11
  46.9 6.6 %collective-permute-done.11.y_ref = f32[2,8,1536]{2,1,0:T(8,128)S(1)} collective-permute-done((f32[2,8,1536]{2,1,0:T(8,128)S(1)}, f32[2,8,1536]{2,1,0:T(8,128)S(1)}, u32[]{:S(2)}, u32[]{:S(2)}) %collective-permute-start.11) | collective-permute-done | bytes 98336 | tf_op jit(solution)/shard_map/ppermute | solution.py:21
  53.5 0.8 collective-permute-done.13.q_ref
  54.3 2.9 %collective-permute-start.19 = (f32[2,8,1536]{2,1,0:T(8,128)S(1)}, f32[2,8,1536]{2,1,0:T(8,128)S(1)}, u32[]{:S(2)}, u32[]{:S(2)}) collective-permute-start(f32[2,8,1536]{2,1,0:T(8,128)S(1)} %shard_map.163.x_ref), channel_id=1, source_target_pairs={{0,2},{1,3},{2,0},{3,1},{4,6},{5,7},{6,4},{7,5},{8,10},{9,11},{10,... | collective-permute-start | bytes 294920 | tf_op jit(solution)/shard_map/ppermute | solution.py:21
  57.2 2.0 %shard_map.167 = bf16[160,384]{1,0:T(8,128)(2,1)S(1)} custom-call(bf16[160,384]{1,0:T(8,128)(2,1)S(1)} %collective-permute-done.14.q_ref, bf16[640,384]{1,0:T(8,128)(2,1)S(1)} %get-tuple-element.58.refs_0_, bf16[640,384]{1,0:T(8,128)(2,1)S(1)} %collective-permute-done.8.refs_1_, bf16[3,640,384]{2,1,0:T(8,128)(2,1)S(1)} %collective-permute-done.9.refs_2_, ...), custom_call_target="tpu_custom_call" | custom-call | tf_op jit(solution)/shard_map/pallas_call | solution.py:279
  59.2 2.2 %collective-permute-start.18 = (bf16[160,384]{1,0:T(8,128)(2,1)S(1)}, bf16[160,384]{1,0:T(8,128)(2,1)S(1)}, u32[]{:S(2)}, u32[]{:S(2)}) collective-permute-start(bf16[160,384]{1,0:T(8,128)(2,1)S(1)} %shard_map.167), channel_id=1, source_target_pairs={{0,3},{1,2},{2,1},{3,0},{4,7},{5,6},{6,5},{7,4},{8,11},{9,10},{10,... | collective-permute-start | bytes 368648 | tf_op jit(solution)/shard_map/ppermute | solution.py:21
  61.3 1.9 %shard_map.166 = bf16[160,384]{1,0:T(8,128)(2,1)S(1)} custom-call(bf16[160,384]{1,0:T(8,128)(2,1)S(1)} %collective-permute-done.13.q_ref, bf16[640,384]{1,0:T(8,128)(2,1)S(1)} %get-tuple-element.58.refs_0_, bf16[640,384]{1,0:T(8,128)(2,1)S(1)} %collective-permute-done.8.refs_1_, bf16[3,640,384]{2,1,0:T(8,128)(2,1)S(1)} %collective-permute-done.9.refs_2_, ...), custom_call_target="tpu_custom_call" | custom-call | tf_op jit(solution)/shard_map/pallas_call | solution.py:279
  63.3 1.0 %collective-permute-start.17 = (bf16[160,384]{1,0:T(8,128)(2,1)S(1)}, bf16[160,384]{1,0:T(8,128)(2,1)S(1)}, u32[]{:S(2)}, u32[]{:S(2)}) collective-permute-start(bf16[160,384]{1,0:T(8,128)(2,1)S(1)} %shard_map.166), channel_id=1, source_target_pairs={{0,2},{1,3},{2,0},{3,1},{4,6},{5,7},{6,4},{7,5},{8,10},{9,11},{10,... | collective-permute-start | bytes 368648 | tf_op jit(solution)/shard_map/ppermute | solution.py:21
  64.3 1.9 %shard_map.165 = bf16[160,384]{1,0:T(8,128)(2,1)S(1)} custom-call(bf16[160,384]{1,0:T(8,128)(2,1)S(1)} %collective-permute-done.12.q_ref, bf16[640,384]{1,0:T(8,128)(2,1)S(1)} %get-tuple-element.58.refs_0_, bf16[640,384]{1,0:T(8,128)(2,1)S(1)} %collective-permute-done.8.refs_1_, bf16[3,640,384]{2,1,0:T(8,128)(2,1)S(1)} %collective-permute-done.9.refs_2_, ...), custom_call_target="tpu_custom_call" | custom-call | tf_op jit(solution)/shard_map/pallas_call | solution.py:279
  66.3 1.4 %collective-permute-start.16 = (bf16[160,384]{1,0:T(8,128)(2,1)S(1)}, bf16[160,384]{1,0:T(8,128)(2,1)S(1)}, u32[]{:S(2)}, u32[]{:S(2)}) collective-permute-start(bf16[160,384]{1,0:T(8,128)(2,1)S(1)} %shard_map.165), channel_id=1, source_target_pairs={{0,1},{1,0},{2,3},{3,2},{4,5},{5,4},{6,7},{7,6},{8,9},{9,8},{10,11... | collective-permute-start | bytes 368648 | tf_op jit(solution)/shard_map/ppermute | solution.py:21
  67.7 0.8 collective-permute-start.20
  68.5 1.5 %collective-permute-start.21 = (f32[2,4,1536]{2,1,0:T(4,128)S(1)}, f32[2,4,1536]{2,1,0:T(4,128)S(1)}, u32[]{:S(2)}, u32[]{:S(2)}) collective-permute-start(f32[2,4,1536]{2,1,0:T(4,128)S(1)} %get-tuple-element.75), channel_id=1, source_target_pairs={{0,16},{16,0},{1,17},{17,1},{2,18},{18,2},{3,19},{19,3},{4,20},{20... | collective-permute-start | bytes 147464 | tf_op jit(solution)/shard_map/ppermute | solution.py:21
  69.9 4.9 %collective-permute-done.20.refs_1_ = f32[2,4,1536]{2,1,0:T(4,128)S(1)} collective-permute-done((f32[2,4,1536]{2,1,0:T(4,128)S(1)}, f32[2,4,1536]{2,1,0:T(4,128)S(1)}, u32[]{:S(2)}, u32[]{:S(2)}) %collective-permute-start.20) | collective-permute-done | bytes 49184 | tf_op jit(solution)/shard_map/ppermute | solution.py:32
  74.8 1.0 %collective-permute-start.22 = (f32[2,4,1536]{2,1,0:T(4,128)S(1)}, f32[2,4,1536]{2,1,0:T(4,128)S(1)}, u32[]{:S(2)}, u32[]{:S(2)}) collective-permute-start(f32[2,4,1536]{2,1,0:T(4,128)S(1)} %get-tuple-element.75), channel_id=1, source_target_pairs={{0,17},{1,16},{2,19},{3,18},{16,1},{17,0},{18,3},{19,2},{4,21},{5,... | collective-permute-start | bytes 147464 | tf_op jit(solution)/shard_map/ppermute | solution.py:32
  75.8 1.9 %shard_map.164.refs_0_ = bf16[160,384]{1,0:T(8,128)(2,1)S(1)} custom-call(bf16[160,384]{1,0:T(8,128)(2,1)S(1)} %get-tuple-element.60.q_ref, bf16[640,384]{1,0:T(8,128)(2,1)S(1)} %get-tuple-element.58.refs_0_, bf16[640,384]{1,0:T(8,128)(2,1)S(1)} %collective-permute-done.8.refs_1_, bf16[3,640,384]{2,1,0:T(8,128)(2,1)S(1)} %collective-permute-done.9.refs_2_, ...), custom_call_target="tpu_custom_call" | custom-call | tf_op jit(solution)/shard_map/pallas_call | solution.py:279
  77.8 2.0 %collective-permute-done.22.refs_3_ = f32[2,4,1536]{2,1,0:T(4,128)S(1)} collective-permute-done((f32[2,4,1536]{2,1,0:T(4,128)S(1)}, f32[2,4,1536]{2,1,0:T(4,128)S(1)}, u32[]{:S(2)}, u32[]{:S(2)}) %collective-permute-start.22) | collective-permute-done | bytes 49184 | tf_op jit(solution)/shard_map/ppermute | solution.py:32
  79.8 0.8 shard_map.170
  80.6 0.8 shard_map.168
  (53 shorter events, 0.3 us)
Async XLA Ops:
  0.6 8.5 %copy-start.3 = (bf16[4,3072]{1,0:T(4,128)(2,1)S(1)}, bf16[4,3072]{1,0:T(4,128)(2,1)}, u32[]{:S(2)}) copy-start(bf16[4,3072]{1,0:T(4,128)(2,1)} %k_ref.4) | copy-start | bytes 73732
  0.6 8.5 %copy-start.4 = (f32[3072]{0:T(1024)S(1)}, f32[3072]{0:T(1024)}, u32[]{:S(2)}) copy-start(f32[3072]{0:T(1024)} %param.21) | copy-start | bytes 36868
  0.7 8.5 %copy-start.5 = (bf16[4,3072]{1,0:T(4,128)(2,1)S(1)}, bf16[4,3072]{1,0:T(4,128)(2,1)}, u32[]{:S(2)}) copy-start(bf16[4,3072]{1,0:T(4,128)(2,1)} %v_ref.1) | copy-start | bytes 73732
  0.7 8.6 %copy-start = (bf16[160,1536]{1,0:T(8,128)(2,1)S(1)}, bf16[160,1536]{1,0:T(8,128)(2,1)}, u32[]{:S(2)}) copy-start(bf16[160,1536]{1,0:T(8,128)(2,1)} %refs_2_.4) | copy-start | bytes 1474564
  0.7 8.6 %copy-start.1 = (bf16[160,1536]{1,0:T(8,128)(2,1)S(1)}, bf16[160,1536]{1,0:T(8,128)(2,1)}, u32[]{:S(2)}) copy-start(bf16[160,1536]{1,0:T(8,128)(2,1)} %refs_2_.2) | copy-start | bytes 1474564
  0.7 11.0 %copy-start.8 = (s32[160,3]{0,1:T(4,128)S(1)}, s32[160,3]{0,1:T(4,128)}, u32[]{:S(2)}) copy-start(s32[160,3]{0,1:T(4,128)} %param.16) | copy-start | bytes 5764
  0.7 15.9 %copy-start.9 = (pred[128]{0:T(512)(128)(4,1)S(1)}, pred[128]{0:T(512)(128)(4,1)}, u32[]{:S(2)}) copy-start(pred[128]{0:T(512)(128)(4,1)} %constant.10.clone) | copy-start | bytes 388
  0.7 15.8 %copy-start.10 = (pred[128]{0:T(512)(128)(4,1)S(1)}, pred[128]{0:T(512)(128)(4,1)}, u32[]{:S(2)}) copy-start(pred[128]{0:T(512)(128)(4,1)} %constant.22.clone) | copy-start | bytes 388
  0.7 15.8 %copy-start.11 = (f32[128]{0:T(128)S(1)}, f32[128]{0:T(128)}, u32[]{:S(2)}) copy-start(f32[128]{0:T(128)} %constant.23.clone) | copy-start | bytes 1540
  2.7 14.3 %copy-start.6 = (f32[1536]{0:T(1024)S(1)}, f32[1536]{0:T(1024)}, u32[]{:S(2)}) copy-start(f32[1536]{0:T(1024)} %param.18) | copy-start | bytes 18436
  2.7 20.2 %all-to-all-start = ((bf16[4,160,384]{2,1,0:T(8,128)(2,1)}), bf16[4,160,384]{2,1,0:T(8,128)(2,1)S(1)}, u32[]{:S(2)}, u32[]{:S(2)}) async-start(bf16[4,160,384]{2,1,0:T(8,128)(2,1)} %bitcast.11), calls=%async_computation | async-start | bytes 983040 | tf_op jit(solution)/shard_map/all_to_all | solution.py:349
  9.1 15.4 %copy-start.7 = (f32[1536]{0:T(1024)S(1)}, f32[1536]{0:T(1024)}, u32[]{:S(2)}) copy-start(f32[1536]{0:T(1024)} %param.17) | copy-start | bytes 18436
  9.1 19.9 %copy-start.2 = (bf16[160,1536]{1,0:T(8,128)(2,1)S(1)}, bf16[160,1536]{1,0:T(8,128)(2,1)}, u32[]{:S(2)}) copy-start(bf16[160,1536]{1,0:T(8,128)(2,1)} %refs_5_.1) | copy-start | bytes 1474564
  9.6 7.4 %collective-permute-start = (f32[160,2]{1,0:T(8,128)S(1)}, f32[160,2]{1,0:T(8,128)S(1)}, u32[]{:S(2)}, u32[]{:S(2)}) collective-permute-start(f32[160,2]{1,0:T(8,128)S(1)} %shard_map.157.refs_0_), channel_id=1, source_target_pairs={{0,16},{16,0},{1,17},{17,1},{2,18},{18,2},{3,19},{19,3},{4,20},{20... | collective-permute-start | bytes 3848 | tf_op jit(solution)/shard_map/ppermute | solution.py:21
  11.1 3.8 %collective-permute-start.2 = (bf16[2,4,1536]{2,1,0:T(4,128)(2,1)S(1)}, bf16[2,4,1536]{2,1,0:T(4,128)(2,1)S(1)}, u32[]{:S(2)}, u32[]{:S(2)}) collective-permute-start(bf16[2,4,1536]{2,1,0:T(4,128)(2,1)S(1)} %get-tuple-element.47), channel_id=1, source_target_pairs={{0,16},{16,0},{1,17},{17,1},{2,18},{18,2},{3,19},{19,3},{4,20},{20... | collective-permute-start | bytes 73736 | tf_op jit(solution)/shard_map/ppermute | solution.py:21
  15.0 4.2 %collective-permute-start.3 = (bf16[2,8,1536]{2,1,0:T(8,128)(2,1)S(1)}, bf16[2,8,1536]{2,1,0:T(8,128)(2,1)S(1)}, u32[]{:S(2)}, u32[]{:S(2)}) collective-permute-start(bf16[2,8,1536]{2,1,0:T(8,128)(2,1)S(1)} %pad_maximum_fusion.2), channel_id=1, source_target_pairs={{0,8},{4,12},{8,0},{12,4},{1,9},{5,13},{9,1},{13,5},{2,10},{6,14},... | collective-permute-start | bytes 147464 | tf_op jit(solution)/shard_map/ppermute | solution.py:21
  22.9 14.6 %collective-permute-start.7 = (bf16[640,384]{1,0:T(8,128)(2,1)S(1)}, bf16[640,384]{1,0:T(8,128)(2,1)S(1)}, u32[]{:S(2)}, u32[]{:S(2)}) collective-permute-start(bf16[640,384]{1,0:T(8,128)(2,1)S(1)} %bitcast.12), channel_id=1, source_target_pairs={{0,8},{4,12},{8,0},{12,4},{1,9},{5,13},{9,1},{13,5},{2,10},{6,14},... | collective-permute-start | bytes 1474568 | tf_op jit(solution)/shard_map/ppermute | solution.py:21
  24.5 4.6 %collective-permute-start.4 = (bf16[2,16,1536]{2,1,0:T(8,128)(2,1)S(1)}, bf16[2,16,1536]{2,1,0:T(8,128)(2,1)S(1)}, u32[]{:S(2)}, u32[]{:S(2)}) collective-permute-start(bf16[2,16,1536]{2,1,0:T(8,128)(2,1)S(1)} %pad_maximum_fusion.1), channel_id=1, source_target_pairs={{0,4},{4,0},{8,12},{12,8},{1,5},{5,1},{9,13},{13,9},{2,6},{6,2},{1... | collective-permute-start | bytes 294920 | tf_op jit(solution)/shard_map/ppermute | solution.py:21
  24.6 9.3 %collective-permute-start.6 = (bf16[160,384]{1,0:T(8,128)(2,1)S(1)}, bf16[160,384]{1,0:T(8,128)(2,1)S(1)}, u32[]{:S(2)}, u32[]{:S(2)}) collective-permute-start(bf16[160,384]{1,0:T(8,128)(2,1)S(1)} %get-tuple-element.56), channel_id=1, source_target_pairs={{0,3},{1,2},{2,1},{3,0},{4,7},{5,6},{6,5},{7,4},{8,11},{9,10},{10,... | collective-permute-start | bytes 368648 | tf_op jit(solution)/shard_map/ppermute | solution.py:21
  26.1 11.4 %collective-permute-start.5 = (bf16[160,384]{1,0:T(8,128)(2,1)S(1)}, bf16[160,384]{1,0:T(8,128)(2,1)S(1)}, u32[]{:S(2)}, u32[]{:S(2)}) collective-permute-start(bf16[160,384]{1,0:T(8,128)(2,1)S(1)} %get-tuple-element.54), channel_id=1, source_target_pairs={{0,2},{1,3},{2,0},{3,1},{4,6},{5,7},{6,4},{7,5},{8,10},{9,11},{10,... | collective-permute-start | bytes 368648 | tf_op jit(solution)/shard_map/ppermute | solution.py:21
  26.1 11.4 %collective-permute-start.1 = (bf16[160,384]{1,0:T(8,128)(2,1)S(1)}, bf16[160,384]{1,0:T(8,128)(2,1)S(1)}, u32[]{:S(2)}, u32[]{:S(2)}) collective-permute-start(bf16[160,384]{1,0:T(8,128)(2,1)S(1)} %get-tuple-element.46), channel_id=1, source_target_pairs={{0,1},{1,0},{2,3},{3,2},{4,5},{5,4},{6,7},{7,6},{8,9},{9,8},{10,11... | collective-permute-start | bytes 368648 | tf_op jit(solution)/shard_map/ppermute | solution.py:21
  37.6 3.3 %collective-permute-start.9 = (bf16[3,640,384]{2,1,0:T(8,128)(2,1)S(1)}, bf16[3,640,384]{2,1,0:T(8,128)(2,1)S(1)}, u32[]{:S(2)}, u32[]{:S(2)}) collective-permute-start(bf16[3,640,384]{2,1,0:T(8,128)(2,1)S(1)} %get-tuple-element.61), channel_id=1, source_target_pairs={{0,4},{4,0},{8,12},{12,8},{1,5},{5,1},{9,13},{13,9},{2,6},{6,2},{1... | collective-permute-start | bytes 4423688 | tf_op jit(solution)/shard_map/ppermute | solution.py:21
  37.8 16.6 %collective-permute-start.8 = (bf16[640,384]{1,0:T(8,128)(2,1)S(1)}, bf16[640,384]{1,0:T(8,128)(2,1)S(1)}, u32[]{:S(2)}, u32[]{:S(2)}) collective-permute-start(bf16[640,384]{1,0:T(8,128)(2,1)S(1)} %get-tuple-element.58.refs_0_), channel_id=1, source_target_pairs={{0,8},{4,12},{8,0},{12,4},{1,9},{5,13},{9,1},{13,5},{2,10},{6,14},... | collective-permute-start | bytes 1474568 | tf_op jit(solution)/shard_map/ppermute | solution.py:21
  41.0 5.3 %collective-permute-start.10 = (f32[2,16,1536]{2,1,0:T(8,128)S(1)}, f32[2,16,1536]{2,1,0:T(8,128)S(1)}, u32[]{:S(2)}, u32[]{:S(2)}) collective-permute-start(f32[2,16,1536]{2,1,0:T(8,128)S(1)} %get-tuple-element.63), channel_id=1, source_target_pairs={{0,4},{4,0},{8,12},{12,8},{1,5},{5,1},{9,13},{13,9},{2,6},{6,2},{1... | collective-permute-start | bytes 589832 | tf_op jit(solution)/shard_map/ppermute | solution.py:21
  41.8 11.7 %collective-permute-start.12 = (bf16[160,384]{1,0:T(8,128)(2,1)S(1)}, bf16[160,384]{1,0:T(8,128)(2,1)S(1)}, u32[]{:S(2)}, u32[]{:S(2)}) collective-permute-start(bf16[160,384]{1,0:T(8,128)(2,1)S(1)} %get-tuple-element.67), channel_id=1, source_target_pairs={{0,1},{1,0},{2,3},{3,2},{4,5},{5,4},{6,7},{7,6},{8,9},{9,8},{10,11... | collective-permute-start | bytes 368648 | tf_op jit(solution)/shard_map/ppermute | solution.py:21
  41.9 12.4 %collective-permute-start.13 = (bf16[160,384]{1,0:T(8,128)(2,1)S(1)}, bf16[160,384]{1,0:T(8,128)(2,1)S(1)}, u32[]{:S(2)}, u32[]{:S(2)}) collective-permute-start(bf16[160,384]{1,0:T(8,128)(2,1)S(1)} %get-tuple-element.68), channel_id=1, source_target_pairs={{0,2},{1,3},{2,0},{3,1},{4,6},{5,7},{6,4},{7,5},{8,10},{9,11},{10,... | collective-permute-start | bytes 368648 | tf_op jit(solution)/shard_map/ppermute | solution.py:21
  43.9 10.4 %collective-permute-start.14 = (bf16[160,384]{1,0:T(8,128)(2,1)S(1)}, bf16[160,384]{1,0:T(8,128)(2,1)S(1)}, u32[]{:S(2)}, u32[]{:S(2)}) collective-permute-start(bf16[160,384]{1,0:T(8,128)(2,1)S(1)} %get-tuple-element.69), channel_id=1, source_target_pairs={{0,3},{1,2},{2,1},{3,0},{4,7},{5,6},{6,5},{7,4},{8,11},{9,10},{10,... | collective-permute-start | bytes 368648 | tf_op jit(solution)/shard_map/ppermute | solution.py:21
  46.3 7.2 %collective-permute-start.11 = (f32[2,8,1536]{2,1,0:T(8,128)S(1)}, f32[2,8,1536]{2,1,0:T(8,128)S(1)}, u32[]{:S(2)}, u32[]{:S(2)}) collective-permute-start(f32[2,8,1536]{2,1,0:T(8,128)S(1)} %get-tuple-element.66), channel_id=1, source_target_pairs={{0,8},{4,12},{8,0},{12,4},{1,9},{5,13},{9,1},{13,5},{2,10},{6,14},... | collective-permute-start | bytes 294920 | tf_op jit(solution)/shard_map/ppermute | solution.py:21
  54.3 2.9 %collective-permute-start.15 = (bf16[640,384]{1,0:T(8,128)(2,1)S(1)}, bf16[640,384]{1,0:T(8,128)(2,1)S(1)}, u32[]{:S(2)}, u32[]{:S(2)}) collective-permute-start(bf16[640,384]{1,0:T(8,128)(2,1)S(1)} %collective-permute-done.8.refs_1_), channel_id=1, source_target_pairs={{0,4},{4,0},{8,12},{12,8},{1,5},{5,1},{9,13},{13,9},{2,6},{6,2},{1... | collective-permute-start | bytes 1474568 | tf_op jit(solution)/shard_map/ppermute | solution.py:21
  54.3 13.3 %collective-permute-start.19 = (f32[2,8,1536]{2,1,0:T(8,128)S(1)}, f32[2,8,1536]{2,1,0:T(8,128)S(1)}, u32[]{:S(2)}, u32[]{:S(2)}) collective-permute-start(f32[2,8,1536]{2,1,0:T(8,128)S(1)} %shard_map.163.x_ref), channel_id=1, source_target_pairs={{0,2},{1,3},{2,0},{3,1},{4,6},{5,7},{6,4},{7,5},{8,10},{9,11},{10,... | collective-permute-start | bytes 294920 | tf_op jit(solution)/shard_map/ppermute | solution.py:21
  59.2 21.4 %collective-permute-start.18 = (bf16[160,384]{1,0:T(8,128)(2,1)S(1)}, bf16[160,384]{1,0:T(8,128)(2,1)S(1)}, u32[]{:S(2)}, u32[]{:S(2)}) collective-permute-start(bf16[160,384]{1,0:T(8,128)(2,1)S(1)} %shard_map.167), channel_id=1, source_target_pairs={{0,3},{1,2},{2,1},{3,0},{4,7},{5,6},{6,5},{7,4},{8,11},{9,10},{10,... | collective-permute-start | bytes 368648 | tf_op jit(solution)/shard_map/ppermute | solution.py:21
  63.3 17.3 %collective-permute-start.17 = (bf16[160,384]{1,0:T(8,128)(2,1)S(1)}, bf16[160,384]{1,0:T(8,128)(2,1)S(1)}, u32[]{:S(2)}, u32[]{:S(2)}) collective-permute-start(bf16[160,384]{1,0:T(8,128)(2,1)S(1)} %shard_map.166), channel_id=1, source_target_pairs={{0,2},{1,3},{2,0},{3,1},{4,6},{5,7},{6,4},{7,5},{8,10},{9,11},{10,... | collective-permute-start | bytes 368648 | tf_op jit(solution)/shard_map/ppermute | solution.py:21
  66.3 14.3 %collective-permute-start.16 = (bf16[160,384]{1,0:T(8,128)(2,1)S(1)}, bf16[160,384]{1,0:T(8,128)(2,1)S(1)}, u32[]{:S(2)}, u32[]{:S(2)}) collective-permute-start(bf16[160,384]{1,0:T(8,128)(2,1)S(1)} %shard_map.165), channel_id=1, source_target_pairs={{0,1},{1,0},{2,3},{3,2},{4,5},{5,4},{6,7},{7,6},{8,9},{9,8},{10,11... | collective-permute-start | bytes 368648 | tf_op jit(solution)/shard_map/ppermute | solution.py:21
  67.7 7.1 %collective-permute-start.20 = (f32[2,4,1536]{2,1,0:T(4,128)S(1)}, f32[2,4,1536]{2,1,0:T(4,128)S(1)}, u32[]{:S(2)}, u32[]{:S(2)}) collective-permute-start(f32[2,4,1536]{2,1,0:T(4,128)S(1)} %get-tuple-element.74.refs_0_), channel_id=1, source_target_pairs={{0,1},{1,0},{2,3},{3,2},{16,17},{17,16},{18,19},{19,18},{4,5},{5,4... | collective-permute-start | bytes 147464 | tf_op jit(solution)/shard_map/ppermute | solution.py:32
  68.5 9.3 %collective-permute-start.21 = (f32[2,4,1536]{2,1,0:T(4,128)S(1)}, f32[2,4,1536]{2,1,0:T(4,128)S(1)}, u32[]{:S(2)}, u32[]{:S(2)}) collective-permute-start(f32[2,4,1536]{2,1,0:T(4,128)S(1)} %get-tuple-element.75), channel_id=1, source_target_pairs={{0,16},{16,0},{1,17},{17,1},{2,18},{18,2},{3,19},{19,3},{4,20},{20... | collective-permute-start | bytes 147464 | tf_op jit(solution)/shard_map/ppermute | solution.py:21
  74.8 5.0 %collective-permute-start.22 = (f32[2,4,1536]{2,1,0:T(4,128)S(1)}, f32[2,4,1536]{2,1,0:T(4,128)S(1)}, u32[]{:S(2)}, u32[]{:S(2)}) collective-permute-start(f32[2,4,1536]{2,1,0:T(4,128)S(1)} %get-tuple-element.75), channel_id=1, source_target_pairs={{0,17},{1,16},{2,19},{3,18},{16,1},{17,0},{18,3},{19,2},{4,21},{5,... | collective-permute-start | bytes 147464 | tf_op jit(solution)/shard_map/ppermute | solution.py:32

commit v3 on v2

--- a/solution.py
+++ b/solution.py
@@ -32,11 +32,11 @@
     return lax.ppermute(x, ("enc", "col"), moves)
 
 
-def kernel_call(body, out_shape, cost=(0, 0, 0), **kw):
+def kernel_call(body, out_shape, cost=(0, 0, 0), vmem=VMEM_LIMIT, **kw):
     return pl.pallas_call(
         body,
         out_shape=out_shape,
-        compiler_params=pltpu.CompilerParams(vmem_limit_bytes=VMEM_LIMIT),
+        compiler_params=pltpu.CompilerParams(vmem_limit_bytes=vmem),
         cost_estimate=pl.CostEstimate(flops=cost[0], bytes_accessed=cost[1], transcendentals=cost[2]),
         **kw,
     )
@@ -64,6 +64,29 @@
 def columns_of(axis, k, width):
     start = (lax.axis_index(axis) ^ k) * width
     return pl.ds(pl.multiple_of(start, HEAD_DIM), width)
+
+
+def split_columns(x, parts):
+    rows, width = x.shape
+    piece = width // parts
+
+    def body(x_ref, out_ref, sems):
+        copies = [
+            pltpu.make_async_copy(x_ref.at[:, pl.ds(z * piece, piece)], out_ref.at[z], sems.at[z])
+            for z in range(parts)
+        ]
+        for copy in copies:
+            copy.start()
+        for copy in copies:
+            copy.wait()
+
+    return kernel_call(
+        body,
+        jax.ShapeDtypeStruct((parts, rows, piece), x.dtype),
+        in_specs=[pl.BlockSpec(memory_space=pltpu.VMEM)],
+        out_specs=pl.BlockSpec(memory_space=pl.ANY),
+        scratch_shapes=[pltpu.SemaphoreType.DMA((parts,))],
+    )(x)
 
 
 def join_rows(pieces, others, axis):
@@ -283,30 +306,35 @@
     rows, width = queries.shape
     n_totals = len(totals)
     count = context.shape[1]
-    heads = width // HEAD_DIM
     half = count // 2
     scale = HEAD_DIM ** (-0.5)
 
     def body(*refs):
         q_ref, gain_ref, c_ref, g_ref, out_ref, keep_ref, send_ref = refs[n_totals:]
         recip = norm_factor(refs[:n_totals], 0, full_width)
-        for h in range(heads):
-            cols = slice(h * HEAD_DIM, (h + 1) * HEAD_DIM)
+        sides = [slice(h, h + HEAD_DIM) for h in range(0, width, HEAD_DIM)]
+        heads = []
+        for cols in sides:
             q = (q_ref[:, cols].astype(jnp.float32) * recip * gain_ref[:, cols]).astype(jnp.bfloat16)
-            g = g_ref[:, cols]
-            k = c_ref[0, :, cols]
-            v = c_ref[1, :, cols]
-            scores = lax.dot_general(k, q, NT, preferred_element_type=jnp.float32) * scale
+            scores = scale * lax.dot_general(
+                c_ref[0, :, cols], q, NT, preferred_element_type=jnp.float32
+            )
+            grad_p = lax.dot_general(
+                c_ref[1, :, cols], g_ref[:, cols], NT, preferred_element_type=jnp.float32
+            )
+            heads.append((q, scores, grad_p))
+        rounded = []
+        for q, scores, grad_p in heads:
             weights = jnp.exp(scores - jnp.max(scores, axis=0, keepdims=True))
             probs = weights / jnp.sum(weights, axis=0, keepdims=True)
-            low = probs.astype(jnp.bfloat16)
+            inner = jnp.sum(probs * grad_p, axis=0, keepdims=True)
+            grad_s = probs * (grad_p - inner)
+            rounded.append((q, probs.astype(jnp.bfloat16), grad_s.astype(jnp.bfloat16)))
+        for cols, (q, low, grad_s) in zip(sides, rounded):
             out_ref[:, cols] = lax.dot_general(
-                low, v, TN, preferred_element_type=jnp.float32
+                low, c_ref[1, :, cols], TN, preferred_element_type=jnp.float32
             ).astype(jnp.bfloat16)
-            grad_v = jnp.dot(low, g, preferred_element_type=jnp.float32)
-            grad_p = lax.dot_general(v, g, NT, preferred_element_type=jnp.float32)
-            inner = jnp.sum(probs * grad_p, axis=0, keepdims=True)
-            grad_s = (probs * (grad_p - inner)).astype(jnp.bfloat16)
+            grad_v = jnp.dot(low, g_ref[:, cols], preferred_element_type=jnp.float32)
             grad_k = jnp.dot(grad_s, q, preferred_element_type=jnp.float32) * scale
             for i, grad in enumerate((grad_k, grad_v)):
                 keep_ref[i, :, cols] = grad[:half]
@@ -319,7 +347,7 @@
             jax.ShapeDtypeStruct((2, half, width), jnp.float32),
             jax.ShapeDtypeStruct((2, half, width), jnp.float32),
         ],
-        (10 * rows * count * width, 80 * rows * width, rows * count * heads),
+        (1000, 1000, 0),
     )(*totals, queries, gain[None, :], context, cotangent)
 
 
@@ -348,7 +376,7 @@
             return x
         return lax.all_to_all(x, "col", split_axis=0, concat_axis=0, tiled=True)
 
-    value_split = jnp.swapaxes(self_values.reshape(rows, parts, width // parts), 0, 1)
+    value_split = split_columns(self_values, parts)
     values_here = relay(value_split)
 
     own_count = context_keys.shape[0]
@@ -374,55 +402,56 @@
         bit //= 2
     key_pieces = [swap(x, "col", n_col, k) if k else x for k, x in enumerate(key_pieces)]
 
-    values_here = after(values_here, key_pieces[0]).reshape(parts * rows, width // parts)
     image_out, grad, sent = image_attention(
-        queries, totals, query_gain, full_width, after(context, values_here), image_cotangent
-    )
+        queries, totals, query_gain, full_width, context, image_cotangent
+    )
+    values_here = after(values_here, context).reshape(parts * rows, width // parts)
+
     all_values = [values_here]
     if parts > 1:
         all_values += [swap(values_here, "row", n_row, row_bits[0])]
-    key_pieces = [key_pieces[0], *(after(x, grad) for x in key_pieces[1:])]
+    query_here = normed_turned(
+        after(queries, grad), 0, totals, query_gain, cosine, sine, full_width, "col", parts, True
+    )
+    key_pieces = [key_pieces[0], *(after(x, values_here, *query_here) for x in key_pieces[1:])]
     keys_here, bundle = join_rows(key_pieces, all_values, "col")
-    query_here = normed_turned(
-        after(queries, keys_here), 0, totals, query_gain, cosine, sine, full_width, "col", parts, True
-    )
     got = keys_here
     if parts > 1:
         keys_there = swap(keys_here, "row", n_row, row_bits[0])
         query_here = [swap(x, "col", n_col, k) if k else x for k, x in enumerate(query_here)]
-        got = swap(bundle, "row", n_row, row_bits[1])
-        all_values += [(got, 1), (got, 2)]
-        all_keys = [keys_here, keys_there, (got, 0)]
+        across = swap(bundle, "row", n_row, row_bits[1])
+        all_values += [(across, 1), (across, 2)]
+        all_keys = [keys_here, keys_there, (across, 0)]
+        got = across
     else:
         all_keys = [lax.all_gather(keys_here, ("row", "col"), axis=0, tiled=True)]
         all_values = [lax.all_gather(values_here, ("row", "col"), axis=0, tiled=True)]
 
     for i in range(len(row_bits)):
-        got = swap(after(sent, got), "row", n_row, 1 << i)
         if i + 1 < len(row_bits):
-            grad, sent = split_sum(grad, got, 2)
+            grad, sent = split_sum(grad, after(swap(sent, "row", n_row, 1 << i), keys_here), 2)
         else:
-            grad = split_sum(grad, got, 1)[0]
+            grad = split_sum(grad, swap(after(sent, got), "row", n_row, 1 << i), 1)[0]
     if parts > 1:
-        keys_there = after(keys_there, grad, *query_here)
+        keys_there = after(keys_there, grad, across, *query_here)
         all_keys += [swap(keys_there, "row", n_row, row_bits[1])]
 
     mixed = [None] * parts
     col_bits = [1 << i for i in reversed(range(n_col.bit_length() - 1))]
-    for bit in col_bits[:-1]:
-        got = swap(grad, "col", n_col, bit)
-        if bit > 2:
-            grad = split_sum(grad, got, 1)[0]
+    for bit in col_bits[:-2]:
+        grad = split_sum(grad, swap(grad, "col", n_col, bit), 1)[0]
+    steps = col_bits[-2:]
+    got = swap(grad, "col", n_col, steps[0])
     for i, k in enumerate(reversed(range(parts))):
         piece = attention(query_here[k], all_keys, all_values)
         mixed[k] = swap(piece, "col", n_col, k) if k else piece
-        if i == min(1, parts - 1):
+        if i == 0:
             got = after(got, piece)
-    sent = split_sum(grad, got, n_enc)
-    grad = []
-    for k, x in enumerate(sent):
-        grad.append([swap(x, "enc", n_enc, k) if k else x, swap_two(x, n_enc, k, n_col, col_bits[-1])])
-    grad[0][0] = after(grad[0][0], mixed[0])
+    if len(steps) > 1:
+        grad = split_sum(grad, got, 1)[0]
+        got = after(swap(grad, "col", n_col, steps[1]), mixed[0])
+    grad = split_sum(grad, got, n_enc)
+    grad = [[swap(x, "enc", n_enc, k) if k else x] for k, x in enumerate(grad)]
     grad_keys_in, grad_values_in = context_gradients(context_keys, context_gain, grad, "enc")
     self_out = join_columns(mixed, "col") if parts > 1 else mixed[0]
 

time: 81.6 us -> 77.3 us (0.947)
  starting transfers between devices: 32.7 us -> 29.2 us
  Pallas kernels: 16.1 us -> 13.9 us
  waiting for transfers between devices: 28.8 us -> 30.9 us
  local copies, waits for them, and re-layouts: 2.23 us -> 1.4 us
    ppermute x21 -> x22, waiting for transfers between devices: 18.1 us -> 28.6 us  [swap(): return lax.ppermute(x, axis, [(i, i ^ k) for i in range(size)])]
    ppermute x2 -> x0, waiting for transfers between devices: 6.9 us -> none  [swap_two(): return lax.ppermute(x, ('enc', 'col'), moves)]
    pallas_call x1, Pallas kernels: 4.78 us -> 1.92 us  [image_attention(): kernel_call(body, [jax.ShapeDtypeStruct((rows, width), jnp.bfloat16), jax...]
    reshape x1 -> x0, local copies, waits for them, and re-layouts: 1.93 us -> none  [per_device(): self_values.reshape(rows, parts, width // parts)]
    ppermute x2 -> x0, starting transfers between devices: 1.78 us -> none  [swap_two(): return lax.ppermute(x, ('enc', 'col'), moves)]
    ppermute x21 -> x22, starting transfers between devices: 24.5 us -> 22.9 us  [swap(): return lax.ppermute(x, axis, [(i, i ^ k) for i in range(size)])]
    all_to_all x1, waiting for transfers between devices: 3.79 us -> 2.33 us  [relay(): return lax.all_to_all(x, 'col', split_axis=0, concat_axis=0, tiled=True)]
    unnamed x24 -> x26, local copies, waits for them, and re-layouts: 0.06 us -> 1.17 us
  transfers between devices with their start and end apart: 24 -> 23, of which waited for: 9 -> 11; matrix products, arithmetic and copies ran while one was open for 1% -> 1% of each run, Pallas kernels for 19% -> 16%
where the time goes in v3:
time: 77.3 us; the launch traced here: 77.1 us
  waiting for transfers between devices  30.9 us (40%)
  starting transfers between devices  29.2 us (38%)
  Pallas kernels  13.9 us (18%)
  local copies, waits for them, and re-layouts  1.4 us (2%)
  between operations  0.99 us (1%)
    ppermute x22, waiting for transfers between devices, swap(): return lax.ppermute(x, axis, [(i, i ^ k) for i in range(size)])  28.6 us
    ppermute x22, starting transfers between devices, swap(): return lax.ppermute(x, axis, [(i, i ^ k) for i in range(size)])  22.9 us
    pallas_call x4, Pallas kernels, attention(): kernel_call(body, jax.ShapeDtypeStruct((rows, width), jnp.bfloat16))  7.66 us
    all_to_all x1, starting transfers between devices, relay(): return lax.all_to_all(x, 'col', split_axis=0, concat_axis=0, tiled=True)  6.33 us
    all_to_all x1, waiting for transfers between devices, relay(): return lax.all_to_all(x, 'col', split_axis=0, concat_axis=0, tiled=True)  2.33 us
    pallas_call x1, Pallas kernels, image_attention(): kernel_call(body, [jax.ShapeDtypeStruct((rows, width), jnp.bfloat16), jax...  1.92 us
  transfers between devices with their start and end apart: 23, of which 11 were waited for; matrix products, arithmetic and copies ran while one was open for 1% of the time, Pallas kernels for 16%

profile of v3, /device:TPU:0, one launch (start us, length us, event | category | flops | bytes accessed | tf_op | source)
XLA Modules:
  0.0 77.1 jit_solution(7291948182080624589)
XLA Ops:
  0.7 1.1 %copy-done.2 = bf16[160,1536]{1,0:T(8,128)(2,1)S(1)} copy-done((bf16[160,1536]{1,0:T(8,128)(2,1)S(1)}, bf16[160,1536]{1,0:T(8,128)(2,1)}, u32[]{:S(2)}) %copy-start.2) | copy-done | bytes 491544
  1.8 0.8 %shard_map.156 = bf16[4,160,384]{2,1,0:T(8,128)(2,1)} custom-call(bf16[160,1536]{1,0:T(8,128)(2,1)S(1)} %copy-done.2), custom_call_target="tpu_custom_call" | custom-call | tf_op jit(solution)/shard_map/pallas_call | solution.py:83
  2.6 6.3 %all-to-all-start = ((bf16[4,160,384]{2,1,0:T(8,128)(2,1)}), bf16[4,160,384]{2,1,0:T(8,128)(2,1)S(1)}, u32[]{:S(2)}, u32[]{:S(2)}) async-start(bf16[4,160,384]{2,1,0:T(8,128)(2,1)} %shard_map.156), calls=%async_computation | async-start | bytes 983040 | tf_op jit(solution)/shard_map/all_to_all | solution.py:377
  9.0 0.1 shard_map.157
  9.2 0.3 shard_map.158.refs_0_
  9.4 1.5 %collective-permute-start = (f32[160,2]{1,0:T(8,128)S(1)}, f32[160,2]{1,0:T(8,128)S(1)}, u32[]{:S(2)}, u32[]{:S(2)}) collective-permute-start(f32[160,2]{1,0:T(8,128)S(1)} %shard_map.158.refs_0_), channel_id=1, source_target_pairs={{0,16},{16,0},{1,17},{17,1},{2,18},{18,2},{3,19},{19,3},{4,20},{20... | collective-permute-start | bytes 3848 | tf_op jit(solution)/shard_map/ppermute | solution.py:21
  11.0 0.5 collective-permute-start.1
  11.5 0.1 pad_maximum_fusion.3
  11.6 0.1 broadcast_in_dim.64
  11.7 0.1 mul.20
  11.8 2.9 %collective-permute-done.1 = bf16[2,4,1536]{2,1,0:T(4,128)(2,1)S(1)} collective-permute-done((bf16[2,4,1536]{2,1,0:T(4,128)(2,1)S(1)}, bf16[2,4,1536]{2,1,0:T(4,128)(2,1)S(1)}, u32[]{:S(2)}, u32[]{:S(2)}) %collective-permute-start.1) | collective-permute-done | bytes 24608 | tf_op jit(solution)/shard_map/ppermute | solution.py:21
  14.8 1.6 %collective-permute-start.2 = (bf16[2,8,1536]{2,1,0:T(8,128)(2,1)S(1)}, bf16[2,8,1536]{2,1,0:T(8,128)(2,1)S(1)}, u32[]{:S(2)}, u32[]{:S(2)}) collective-permute-start(bf16[2,8,1536]{2,1,0:T(8,128)(2,1)S(1)} %pad_maximum_fusion.2), channel_id=1, source_target_pairs={{0,8},{4,12},{8,0},{12,4},{1,9},{5,13},{9,1},{13,5},{2,10},{6,14},... | collective-permute-start | bytes 147464 | tf_op jit(solution)/shard_map/ppermute | solution.py:21
  16.4 0.4 sine_multiply_fusion
  16.9 0.7 shard_map.159
  17.5 1.4 %collective-permute-done.2 = bf16[2,8,1536]{2,1,0:T(8,128)(2,1)S(1)} collective-permute-done((bf16[2,8,1536]{2,1,0:T(8,128)(2,1)S(1)}, bf16[2,8,1536]{2,1,0:T(8,128)(2,1)S(1)}, u32[]{:S(2)}, u32[]{:S(2)}) %collective-permute-start.2) | collective-permute-done | bytes 49184 | tf_op jit(solution)/shard_map/ppermute | solution.py:21
  19.0 0.1 collective-permute-start.3
  19.1 1.3 %collective-permute-done.3 = bf16[2,16,1536]{2,1,0:T(8,128)(2,1)S(1)} collective-permute-done((bf16[2,16,1536]{2,1,0:T(8,128)(2,1)S(1)}, bf16[2,16,1536]{2,1,0:T(8,128)(2,1)S(1)}, u32[]{:S(2)}, u32[]{:S(2)}) %collective-permute-start.3) | collective-permute-done | bytes 98336 | tf_op jit(solution)/shard_map/ppermute | solution.py:21
  20.4 2.3 %all-to-all-done = bf16[4,160,384]{2,1,0:T(8,128)(2,1)S(1)} async-done(((bf16[4,160,384]{2,1,0:T(8,128)(2,1)}), bf16[4,160,384]{2,1,0:T(8,128)(2,1)S(1)}, u32[]{:S(2)}, u32[]{:S(2)}) %all-to-all-start) | async-done | bytes 491552 | tf_op jit(solution)/shard_map/all_to_all | solution.py:377
  22.8 1.5 %collective-permute-start.7 = (bf16[640,384]{1,0:T(8,128)(2,1)S(1)}, bf16[640,384]{1,0:T(8,128)(2,1)S(1)}, u32[]{:S(2)}, u32[]{:S(2)}) collective-permute-start(bf16[640,384]{1,0:T(8,128)(2,1)S(1)} %bitcast.5), channel_id=1, source_target_pairs={{0,8},{4,12},{8,0},{12,4},{1,9},{5,13},{9,1},{13,5},{2,10},{6,14},... | collective-permute-start | bytes 1474568 | tf_op jit(solution)/shard_map/ppermute | solution.py:21
  24.3 1.6 %collective-permute-start.6 = (bf16[160,384]{1,0:T(8,128)(2,1)S(1)}, bf16[160,384]{1,0:T(8,128)(2,1)S(1)}, u32[]{:S(2)}, u32[]{:S(2)}) collective-permute-start(bf16[160,384]{1,0:T(8,128)(2,1)S(1)} %get-tuple-element.59), channel_id=1, source_target_pairs={{0,3},{1,2},{2,1},{3,0},{4,7},{5,6},{6,5},{7,4},{8,11},{9,10},{10,... | collective-permute-start | bytes 368648 | tf_op jit(solution)/shard_map/ppermute | solution.py:21
  25.9 2.8 %collective-permute-start.4 = (bf16[160,384]{1,0:T(8,128)(2,1)S(1)}, bf16[160,384]{1,0:T(8,128)(2,1)S(1)}, u32[]{:S(2)}, u32[]{:S(2)}) collective-permute-start(bf16[160,384]{1,0:T(8,128)(2,1)S(1)} %get-tuple-element.51), channel_id=1, source_target_pairs={{0,1},{1,0},{2,3},{3,2},{4,5},{5,4},{6,7},{7,6},{8,9},{9,8},{10,11... | collective-permute-start | bytes 368648 | tf_op jit(solution)/shard_map/ppermute | solution.py:21
  28.7 1.9 %shard_map.160 = (bf16[160,1536]{1,0:T(8,128)(2,1)}, f32[2,16,1536]{2,1,0:T(8,128)S(1)}, f32[2,16,1536]{2,1,0:T(8,128)S(1)}) custom-call(f32[160,2]{1,0:T(8,128)S(1)} %shard_map.158.refs_0_, f32[160,2]{1,0:T(8,128)S(1)} %collective-permute-done.refs_1_, bf16[160,1536]{1,0:T(8,128)(2,1)S(1)} %copy-done, f32[1,1536]{1,0:T(1,128)S(1)} %broadcast_in_dim.54.refs_3_, ...), custom_call_target="tpu_custom_call" | custom-call | flops 1000 | bytes 1000 | tf_op jit(solution)/shard_map/pallas_call | solution.py:343
  30.6 0.7 shard_map.161
  31.3 1.1 %collective-permute-done.6.refs_3_ = bf16[160,384]{1,0:T(8,128)(2,1)S(1)} collective-permute-done((bf16[160,384]{1,0:T(8,128)(2,1)S(1)}, bf16[160,384]{1,0:T(8,128)(2,1)S(1)}, u32[]{:S(2)}, u32[]{:S(2)}) %collective-permute-start.6) | collective-permute-done | bytes 122912 | tf_op jit(solution)/shard_map/ppermute | solution.py:21
  32.3 4.1 %collective-permute-done.5.refs_2_ = bf16[160,384]{1,0:T(8,128)(2,1)S(1)} collective-permute-done((bf16[160,384]{1,0:T(8,128)(2,1)S(1)}, bf16[160,384]{1,0:T(8,128)(2,1)S(1)}, u32[]{:S(2)}, u32[]{:S(2)}) %collective-permute-start.5) | collective-permute-done | bytes 122912 | tf_op jit(solution)/shard_map/ppermute | solution.py:21
  36.5 0.2 shard_map.162
  36.8 0.6 collective-permute-start.8
  37.3 0.2 collective-permute-start.10
  37.5 0.3 collective-permute-start.12
  37.8 2.6 %collective-permute-start.13 = (bf16[160,384]{1,0:T(8,128)(2,1)S(1)}, bf16[160,384]{1,0:T(8,128)(2,1)S(1)}, u32[]{:S(2)}, u32[]{:S(2)}) collective-permute-start(bf16[160,384]{1,0:T(8,128)(2,1)S(1)} %get-tuple-element.54), channel_id=1, source_target_pairs={{0,2},{1,3},{2,0},{3,1},{4,6},{5,7},{6,4},{7,5},{8,10},{9,11},{10,... | collective-permute-start | bytes 368648 | tf_op jit(solution)/shard_map/ppermute | solution.py:21
  40.4 2.2 %collective-permute-start.14 = (bf16[160,384]{1,0:T(8,128)(2,1)S(1)}, bf16[160,384]{1,0:T(8,128)(2,1)S(1)}, u32[]{:S(2)}, u32[]{:S(2)}) collective-permute-start(bf16[160,384]{1,0:T(8,128)(2,1)S(1)} %get-tuple-element.55), channel_id=1, source_target_pairs={{0,3},{1,2},{2,1},{3,0},{4,7},{5,6},{6,5},{7,4},{8,11},{9,10},{10,... | collective-permute-start | bytes 368648 | tf_op jit(solution)/shard_map/ppermute | solution.py:21
  42.7 0.8 %collective-permute-start.11 = (f32[2,8,1536]{2,1,0:T(8,128)S(1)}, f32[2,8,1536]{2,1,0:T(8,128)S(1)}, u32[]{:S(2)}, u32[]{:S(2)}) collective-permute-start(f32[2,8,1536]{2,1,0:T(8,128)S(1)} %get-tuple-element.67), channel_id=1, source_target_pairs={{0,8},{4,12},{8,0},{12,4},{1,9},{5,13},{9,1},{13,5},{2,10},{6,14},... | collective-permute-start | bytes 294920 | tf_op jit(solution)/shard_map/ppermute | solution.py:21
  43.5 9.0 %collective-permute-done.11.y_ref = f32[2,8,1536]{2,1,0:T(8,128)S(1)} collective-permute-done((f32[2,8,1536]{2,1,0:T(8,128)S(1)}, f32[2,8,1536]{2,1,0:T(8,128)S(1)}, u32[]{:S(2)}, u32[]{:S(2)}) %collective-permute-start.11) | collective-permute-done | bytes 98336 | tf_op jit(solution)/shard_map/ppermute | solution.py:21
  52.6 0.8 %collective-permute-start.19 = (f32[2,8,1536]{2,1,0:T(8,128)S(1)}, f32[2,8,1536]{2,1,0:T(8,128)S(1)}, u32[]{:S(2)}, u32[]{:S(2)}) collective-permute-start(f32[2,8,1536]{2,1,0:T(8,128)S(1)} %shard_map.164.x_ref), channel_id=1, source_target_pairs={{0,2},{1,3},{2,0},{3,1},{4,6},{5,7},{6,4},{7,5},{8,10},{9,11},{10,... | collective-permute-start | bytes 294920 | tf_op jit(solution)/shard_map/ppermute | solution.py:21
  53.4 1.1 %collective-permute-done.15.refs_3_ = bf16[640,384]{1,0:T(8,128)(2,1)S(1)} collective-permute-done((bf16[640,384]{1,0:T(8,128)(2,1)S(1)}, bf16[640,384]{1,0:T(8,128)(2,1)S(1)}, u32[]{:S(2)}, u32[]{:S(2)}) %collective-permute-start.15) | collective-permute-done | bytes 491552 | tf_op jit(solution)/shard_map/ppermute | solution.py:21
  54.5 1.9 %shard_map.168 = bf16[160,384]{1,0:T(8,128)(2,1)S(1)} custom-call(bf16[160,384]{1,0:T(8,128)(2,1)S(1)} %collective-permute-done.14.q_ref, bf16[640,384]{1,0:T(8,128)(2,1)S(1)} %get-tuple-element.61.refs_0_, bf16[640,384]{1,0:T(8,128)(2,1)S(1)} %collective-permute-done.8.refs_1_, bf16[3,640,384]{2,1,0:T(8,128)(2,1)S(1)} %collective-permute-done.9.refs_2_, ...), custom_call_target="tpu_custom_call" | custom-call | tf_op jit(solution)/shard_map/pallas_call | solution.py:302
  56.4 4.2 %collective-permute-done.19.y_ref = f32[2,8,1536]{2,1,0:T(8,128)S(1)} collective-permute-done((f32[2,8,1536]{2,1,0:T(8,128)S(1)}, f32[2,8,1536]{2,1,0:T(8,128)S(1)}, u32[]{:S(2)}, u32[]{:S(2)}) %collective-permute-start.19) | collective-permute-done | bytes 98336 | tf_op jit(solution)/shard_map/ppermute | solution.py:21
  60.7 2.0 %collective-permute-start.18 = (bf16[160,384]{1,0:T(8,128)(2,1)S(1)}, bf16[160,384]{1,0:T(8,128)(2,1)S(1)}, u32[]{:S(2)}, u32[]{:S(2)}) collective-permute-start(bf16[160,384]{1,0:T(8,128)(2,1)S(1)} %shard_map.168), channel_id=1, source_target_pairs={{0,3},{1,2},{2,1},{3,0},{4,7},{5,6},{6,5},{7,4},{8,11},{9,10},{10,... | collective-permute-start | bytes 368648 | tf_op jit(solution)/shard_map/ppermute | solution.py:21
  62.7 1.9 %shard_map.167 = bf16[160,384]{1,0:T(8,128)(2,1)S(1)} custom-call(bf16[160,384]{1,0:T(8,128)(2,1)S(1)} %collective-permute-done.13.q_ref, bf16[640,384]{1,0:T(8,128)(2,1)S(1)} %get-tuple-element.61.refs_0_, bf16[640,384]{1,0:T(8,128)(2,1)S(1)} %collective-permute-done.8.refs_1_, bf16[3,640,384]{2,1,0:T(8,128)(2,1)S(1)} %collective-permute-done.9.refs_2_, ...), custom_call_target="tpu_custom_call" | custom-call | tf_op jit(solution)/shard_map/pallas_call | solution.py:302
  64.6 1.5 %collective-permute-start.17 = (bf16[160,384]{1,0:T(8,128)(2,1)S(1)}, bf16[160,384]{1,0:T(8,128)(2,1)S(1)}, u32[]{:S(2)}, u32[]{:S(2)}) collective-permute-start(bf16[160,384]{1,0:T(8,128)(2,1)S(1)} %shard_map.167), channel_id=1, source_target_pairs={{0,2},{1,3},{2,0},{3,1},{4,6},{5,7},{6,4},{7,5},{8,10},{9,11},{10,... | collective-permute-start | bytes 368648 | tf_op jit(solution)/shard_map/ppermute | solution.py:21
  66.1 1.9 %shard_map.166 = bf16[160,384]{1,0:T(8,128)(2,1)S(1)} custom-call(bf16[160,384]{1,0:T(8,128)(2,1)S(1)} %collective-permute-done.12.q_ref, bf16[640,384]{1,0:T(8,128)(2,1)S(1)} %get-tuple-element.61.refs_0_, bf16[640,384]{1,0:T(8,128)(2,1)S(1)} %collective-permute-done.8.refs_1_, bf16[3,640,384]{2,1,0:T(8,128)(2,1)S(1)} %collective-permute-done.9.refs_2_, ...), custom_call_target="tpu_custom_call" | custom-call | tf_op jit(solution)/shard_map/pallas_call | solution.py:302
  68.0 1.0 %collective-permute-start.16 = (bf16[160,384]{1,0:T(8,128)(2,1)S(1)}, bf16[160,384]{1,0:T(8,128)(2,1)S(1)}, u32[]{:S(2)}, u32[]{:S(2)}) collective-permute-start(bf16[160,384]{1,0:T(8,128)(2,1)S(1)} %shard_map.166), channel_id=1, source_target_pairs={{0,1},{1,0},{2,3},{3,2},{4,5},{5,4},{6,7},{7,6},{8,9},{9,8},{10,11... | collective-permute-start | bytes 368648 | tf_op jit(solution)/shard_map/ppermute | solution.py:21
  69.1 1.9 %shard_map.165.refs_0_ = bf16[160,384]{1,0:T(8,128)(2,1)S(1)} custom-call(bf16[160,384]{1,0:T(8,128)(2,1)S(1)} %get-tuple-element.50.q_ref, bf16[640,384]{1,0:T(8,128)(2,1)S(1)} %get-tuple-element.61.refs_0_, bf16[640,384]{1,0:T(8,128)(2,1)S(1)} %collective-permute-done.8.refs_1_, bf16[3,640,384]{2,1,0:T(8,128)(2,1)S(1)} %collective-permute-done.9.refs_2_, ...), custom_call_target="tpu_custom_call" | custom-call | tf_op jit(solution)/shard_map/pallas_call | solution.py:302
  71.0 0.9 %collective-permute-start.21 = (f32[2,4,1536]{2,1,0:T(4,128)S(1)}, f32[2,4,1536]{2,1,0:T(4,128)S(1)}, u32[]{:S(2)}, u32[]{:S(2)}) collective-permute-start(f32[2,4,1536]{2,1,0:T(4,128)S(1)} %get-tuple-element.73), channel_id=1, source_target_pairs={{0,16},{16,0},{1,17},{17,1},{2,18},{18,2},{3,19},{19,3},{4,20},{20... | collective-permute-start | bytes 147464 | tf_op jit(solution)/shard_map/ppermute | solution.py:21
  72.0 3.1 %collective-permute-done.17.refs_2_ = bf16[160,384]{1,0:T(8,128)(2,1)S(1)} collective-permute-done((bf16[160,384]{1,0:T(8,128)(2,1)S(1)}, bf16[160,384]{1,0:T(8,128)(2,1)S(1)}, u32[]{:S(2)}, u32[]{:S(2)}) %collective-permute-start.17) | collective-permute-done | bytes 122912 | tf_op jit(solution)/shard_map/ppermute | solution.py:21
  75.1 0.4 collective-permute-done.16.refs_1_
  75.5 0.8 %shard_map.169 = bf16[160,1536]{1,0:T(8,128)(2,1)} custom-call(bf16[160,384]{1,0:T(8,128)(2,1)S(1)} %shard_map.165.refs_0_, bf16[160,384]{1,0:T(8,128)(2,1)S(1)} %collective-permute-done.16.refs_1_, bf16[160,384]{1,0:T(8,128)(2,1)S(1)} %collective-permute-done.17.refs_2_, bf16[160,384]{1,0:T(8,128)(2,1)S(1)} %collective-permute-done.18.refs_3_), custom_call_target="tpu_custom_call" | custom-call | tf_op jit(solution)/shard_map/pallas_call | solution.py:131
  76.3 0.8 shard_map.172
  (54 shorter events, 0.5 us)
Async XLA Ops:
  0.6 15.8 %copy-start.10 = (pred[128]{0:T(512)(128)(4,1)S(1)}, pred[128]{0:T(512)(128)(4,1)}, u32[]{:S(2)}) copy-start(pred[128]{0:T(512)(128)(4,1)} %constant.10.clone) | copy-start | bytes 388
  0.6 15.8 %copy-start.11 = (pred[128]{0:T(512)(128)(4,1)S(1)}, pred[128]{0:T(512)(128)(4,1)}, u32[]{:S(2)}) copy-start(pred[128]{0:T(512)(128)(4,1)} %constant.22.clone) | copy-start | bytes 388
  0.7 8.5 %copy-start = (bf16[160,1536]{1,0:T(8,128)(2,1)S(1)}, bf16[160,1536]{1,0:T(8,128)(2,1)}, u32[]{:S(2)}) copy-start(bf16[160,1536]{1,0:T(8,128)(2,1)} %refs_2_.4) | copy-start | bytes 1474564
  0.7 8.5 %copy-start.1 = (bf16[160,1536]{1,0:T(8,128)(2,1)S(1)}, bf16[160,1536]{1,0:T(8,128)(2,1)}, u32[]{:S(2)}) copy-start(bf16[160,1536]{1,0:T(8,128)(2,1)} %refs_2_.2) | copy-start | bytes 1474564
  0.7 1.1 %copy-start.2 = (bf16[160,1536]{1,0:T(8,128)(2,1)S(1)}, bf16[160,1536]{1,0:T(8,128)(2,1)}, u32[]{:S(2)}) copy-start(bf16[160,1536]{1,0:T(8,128)(2,1)} %x_ref.1) | copy-start | bytes 1474564
  1.8 7.2 %copy-start.4 = (bf16[4,3072]{1,0:T(4,128)(2,1)S(1)}, bf16[4,3072]{1,0:T(4,128)(2,1)}, u32[]{:S(2)}) copy-start(bf16[4,3072]{1,0:T(4,128)(2,1)} %k_ref.4) | copy-start | bytes 73732
  1.8 7.2 %copy-start.5 = (f32[3072]{0:T(1024)S(1)}, f32[3072]{0:T(1024)}, u32[]{:S(2)}) copy-start(f32[3072]{0:T(1024)} %param.21) | copy-start | bytes 36868
  1.8 7.2 %copy-start.6 = (bf16[4,3072]{1,0:T(4,128)(2,1)S(1)}, bf16[4,3072]{1,0:T(4,128)(2,1)}, u32[]{:S(2)}) copy-start(bf16[4,3072]{1,0:T(4,128)(2,1)} %v_ref.1) | copy-start | bytes 73732
  1.8 9.7 %copy-start.9 = (s32[160,3]{0,1:T(4,128)S(1)}, s32[160,3]{0,1:T(4,128)}, u32[]{:S(2)}) copy-start(s32[160,3]{0,1:T(4,128)} %param.16) | copy-start | bytes 5764
  1.8 14.6 %copy-start.12 = (f32[128]{0:T(128)S(1)}, f32[128]{0:T(128)}, u32[]{:S(2)}) copy-start(f32[128]{0:T(128)} %constant.23.clone) | copy-start | bytes 1540
  2.6 14.2 %copy-start.7 = (f32[1536]{0:T(1024)S(1)}, f32[1536]{0:T(1024)}, u32[]{:S(2)}) copy-start(f32[1536]{0:T(1024)} %param.18) | copy-start | bytes 18436
  2.6 20.1 %all-to-all-start = ((bf16[4,160,384]{2,1,0:T(8,128)(2,1)}), bf16[4,160,384]{2,1,0:T(8,128)(2,1)S(1)}, u32[]{:S(2)}, u32[]{:S(2)}) async-start(bf16[4,160,384]{2,1,0:T(8,128)(2,1)} %shard_map.156), calls=%async_computation | async-start | bytes 983040 | tf_op jit(solution)/shard_map/all_to_all | solution.py:377
  9.0 19.7 %copy-start.8 = (f32[1536]{0:T(1024)S(1)}, f32[1536]{0:T(1024)}, u32[]{:S(2)}) copy-start(f32[1536]{0:T(1024)} %param.17) | copy-start | bytes 18436
  9.0 19.7 %copy-start.3 = (bf16[160,1536]{1,0:T(8,128)(2,1)S(1)}, bf16[160,1536]{1,0:T(8,128)(2,1)}, u32[]{:S(2)}) copy-start(bf16[160,1536]{1,0:T(8,128)(2,1)} %refs_5_.1) | copy-start | bytes 1474564
  9.4 7.4 %collective-permute-start = (f32[160,2]{1,0:T(8,128)S(1)}, f32[160,2]{1,0:T(8,128)S(1)}, u32[]{:S(2)}, u32[]{:S(2)}) collective-permute-start(f32[160,2]{1,0:T(8,128)S(1)} %shard_map.158.refs_0_), channel_id=1, source_target_pairs={{0,16},{16,0},{1,17},{17,1},{2,18},{18,2},{3,19},{19,3},{4,20},{20... | collective-permute-start | bytes 3848 | tf_op jit(solution)/shard_map/ppermute | solution.py:21
  11.0 3.8 %collective-permute-start.1 = (bf16[2,4,1536]{2,1,0:T(4,128)(2,1)S(1)}, bf16[2,4,1536]{2,1,0:T(4,128)(2,1)S(1)}, u32[]{:S(2)}, u32[]{:S(2)}) collective-permute-start(bf16[2,4,1536]{2,1,0:T(4,128)(2,1)S(1)} %get-tuple-element.43), channel_id=1, source_target_pairs={{0,16},{16,0},{1,17},{17,1},{2,18},{18,2},{3,19},{19,3},{4,20},{20... | collective-permute-start | bytes 73736 | tf_op jit(solution)/shard_map/ppermute | solution.py:21
  14.8 4.2 %collective-permute-start.2 = (bf16[2,8,1536]{2,1,0:T(8,128)(2,1)S(1)}, bf16[2,8,1536]{2,1,0:T(8,128)(2,1)S(1)}, u32[]{:S(2)}, u32[]{:S(2)}) collective-permute-start(bf16[2,8,1536]{2,1,0:T(8,128)(2,1)S(1)} %pad_maximum_fusion.2), channel_id=1, source_target_pairs={{0,8},{4,12},{8,0},{12,4},{1,9},{5,13},{9,1},{13,5},{2,10},{6,14},... | collective-permute-start | bytes 147464 | tf_op jit(solution)/shard_map/ppermute | solution.py:21
  19.0 1.4 %collective-permute-start.3 = (bf16[2,16,1536]{2,1,0:T(8,128)(2,1)S(1)}, bf16[2,16,1536]{2,1,0:T(8,128)(2,1)S(1)}, u32[]{:S(2)}, u32[]{:S(2)}) collective-permute-start(bf16[2,16,1536]{2,1,0:T(8,128)(2,1)S(1)} %pad_maximum_fusion.1), channel_id=1, source_target_pairs={{0,4},{4,0},{8,12},{12,8},{1,5},{5,1},{9,13},{13,9},{2,6},{6,2},{1... | collective-permute-start | bytes 294920 | tf_op jit(solution)/shard_map/ppermute | solution.py:21
  22.8 13.7 %collective-permute-start.7 = (bf16[640,384]{1,0:T(8,128)(2,1)S(1)}, bf16[640,384]{1,0:T(8,128)(2,1)S(1)}, u32[]{:S(2)}, u32[]{:S(2)}) collective-permute-start(bf16[640,384]{1,0:T(8,128)(2,1)S(1)} %bitcast.5), channel_id=1, source_target_pairs={{0,8},{4,12},{8,0},{12,4},{1,9},{5,13},{9,1},{13,5},{2,10},{6,14},... | collective-permute-start | bytes 1474568 | tf_op jit(solution)/shard_map/ppermute | solution.py:21
  24.3 8.1 %collective-permute-start.6 = (bf16[160,384]{1,0:T(8,128)(2,1)S(1)}, bf16[160,384]{1,0:T(8,128)(2,1)S(1)}, u32[]{:S(2)}, u32[]{:S(2)}) collective-permute-start(bf16[160,384]{1,0:T(8,128)(2,1)S(1)} %get-tuple-element.59), channel_id=1, source_target_pairs={{0,3},{1,2},{2,1},{3,0},{4,7},{5,6},{6,5},{7,4},{8,11},{9,10},{10,... | collective-permute-start | bytes 368648 | tf_op jit(solution)/shard_map/ppermute | solution.py:21
  25.9 10.6 %collective-permute-start.5 = (bf16[160,384]{1,0:T(8,128)(2,1)S(1)}, bf16[160,384]{1,0:T(8,128)(2,1)S(1)}, u32[]{:S(2)}, u32[]{:S(2)}) collective-permute-start(bf16[160,384]{1,0:T(8,128)(2,1)S(1)} %get-tuple-element.57), channel_id=1, source_target_pairs={{0,2},{1,3},{2,0},{3,1},{4,6},{5,7},{6,4},{7,5},{8,10},{9,11},{10,... | collective-permute-start | bytes 368648 | tf_op jit(solution)/shard_map/ppermute | solution.py:21
  25.9 10.6 %collective-permute-start.4 = (bf16[160,384]{1,0:T(8,128)(2,1)S(1)}, bf16[160,384]{1,0:T(8,128)(2,1)S(1)}, u32[]{:S(2)}, u32[]{:S(2)}) collective-permute-start(bf16[160,384]{1,0:T(8,128)(2,1)S(1)} %get-tuple-element.51), channel_id=1, source_target_pairs={{0,1},{1,0},{2,3},{3,2},{4,5},{5,4},{6,7},{7,6},{8,9},{9,8},{10,11... | collective-permute-start | bytes 368648 | tf_op jit(solution)/shard_map/ppermute | solution.py:21
  36.7 6.0 %collective-permute-start.9 = (bf16[3,640,384]{2,1,0:T(8,128)(2,1)S(1)}, bf16[3,640,384]{2,1,0:T(8,128)(2,1)S(1)}, u32[]{:S(2)}, u32[]{:S(2)}) collective-permute-start(bf16[3,640,384]{2,1,0:T(8,128)(2,1)S(1)} %get-tuple-element.62), channel_id=1, source_target_pairs={{0,4},{4,0},{8,12},{12,8},{1,5},{5,1},{9,13},{13,9},{2,6},{6,2},{1... | collective-permute-start | bytes 4423688 | tf_op jit(solution)/shard_map/ppermute | solution.py:21
  36.8 15.8 %collective-permute-start.8 = (bf16[640,384]{1,0:T(8,128)(2,1)S(1)}, bf16[640,384]{1,0:T(8,128)(2,1)S(1)}, u32[]{:S(2)}, u32[]{:S(2)}) collective-permute-start(bf16[640,384]{1,0:T(8,128)(2,1)S(1)} %get-tuple-element.61.refs_0_), channel_id=1, source_target_pairs={{0,8},{4,12},{8,0},{12,4},{1,9},{5,13},{9,1},{13,5},{2,10},{6,14},... | collective-permute-start | bytes 1474568 | tf_op jit(solution)/shard_map/ppermute | solution.py:21
  37.3 3.1 %collective-permute-start.10 = (f32[2,16,1536]{2,1,0:T(8,128)S(1)}, f32[2,16,1536]{2,1,0:T(8,128)S(1)}, u32[]{:S(2)}, u32[]{:S(2)}) collective-permute-start(f32[2,16,1536]{2,1,0:T(8,128)S(1)} %get-tuple-element.63), channel_id=1, source_target_pairs={{0,4},{4,0},{8,12},{12,8},{1,5},{5,1},{9,13},{13,9},{2,6},{6,2},{1... | collective-permute-start | bytes 589832 | tf_op jit(solution)/shard_map/ppermute | solution.py:21
  37.5 15.0 %collective-permute-start.12 = (bf16[160,384]{1,0:T(8,128)(2,1)S(1)}, bf16[160,384]{1,0:T(8,128)(2,1)S(1)}, u32[]{:S(2)}, u32[]{:S(2)}) collective-permute-start(bf16[160,384]{1,0:T(8,128)(2,1)S(1)} %get-tuple-element.53), channel_id=1, source_target_pairs={{0,1},{1,0},{2,3},{3,2},{4,5},{5,4},{6,7},{7,6},{8,9},{9,8},{10,11... | collective-permute-start | bytes 368648 | tf_op jit(solution)/shard_map/ppermute | solution.py:21
  37.8 14.7 %collective-permute-start.13 = (bf16[160,384]{1,0:T(8,128)(2,1)S(1)}, bf16[160,384]{1,0:T(8,128)(2,1)S(1)}, u32[]{:S(2)}, u32[]{:S(2)}) collective-permute-start(bf16[160,384]{1,0:T(8,128)(2,1)S(1)} %get-tuple-element.54), channel_id=1, source_target_pairs={{0,2},{1,3},{2,0},{3,1},{4,6},{5,7},{6,4},{7,5},{8,10},{9,11},{10,... | collective-permute-start | bytes 368648 | tf_op jit(solution)/shard_map/ppermute | solution.py:21
  40.4 12.1 %collective-permute-start.14 = (bf16[160,384]{1,0:T(8,128)(2,1)S(1)}, bf16[160,384]{1,0:T(8,128)(2,1)S(1)}, u32[]{:S(2)}, u32[]{:S(2)}) collective-permute-start(bf16[160,384]{1,0:T(8,128)(2,1)S(1)} %get-tuple-element.55), channel_id=1, source_target_pairs={{0,3},{1,2},{2,1},{3,0},{4,7},{5,6},{6,5},{7,4},{8,11},{9,10},{10,... | collective-permute-start | bytes 368648 | tf_op jit(solution)/shard_map/ppermute | solution.py:21
  42.7 9.8 %collective-permute-start.11 = (f32[2,8,1536]{2,1,0:T(8,128)S(1)}, f32[2,8,1536]{2,1,0:T(8,128)S(1)}, u32[]{:S(2)}, u32[]{:S(2)}) collective-permute-start(f32[2,8,1536]{2,1,0:T(8,128)S(1)} %get-tuple-element.67), channel_id=1, source_target_pairs={{0,8},{4,12},{8,0},{12,4},{1,9},{5,13},{9,1},{13,5},{2,10},{6,14},... | collective-permute-start | bytes 294920 | tf_op jit(solution)/shard_map/ppermute | solution.py:21
  52.6 1.9 %collective-permute-start.15 = (bf16[640,384]{1,0:T(8,128)(2,1)S(1)}, bf16[640,384]{1,0:T(8,128)(2,1)S(1)}, u32[]{:S(2)}, u32[]{:S(2)}) collective-permute-start(bf16[640,384]{1,0:T(8,128)(2,1)S(1)} %collective-permute-done.8.refs_1_), channel_id=1, source_target_pairs={{0,4},{4,0},{8,12},{12,8},{1,5},{5,1},{9,13},{13,9},{2,6},{6,2},{1... | collective-permute-start | bytes 1474568 | tf_op jit(solution)/shard_map/ppermute | solution.py:21
  52.6 7.9 %collective-permute-start.19 = (f32[2,8,1536]{2,1,0:T(8,128)S(1)}, f32[2,8,1536]{2,1,0:T(8,128)S(1)}, u32[]{:S(2)}, u32[]{:S(2)}) collective-permute-start(f32[2,8,1536]{2,1,0:T(8,128)S(1)} %shard_map.164.x_ref), channel_id=1, source_target_pairs={{0,2},{1,3},{2,0},{3,1},{4,6},{5,7},{6,4},{7,5},{8,10},{9,11},{10,... | collective-permute-start | bytes 294920 | tf_op jit(solution)/shard_map/ppermute | solution.py:21
  60.6 10.4 %collective-permute-start.20 = (f32[2,8,1536]{2,1,0:T(8,128)S(1)}, f32[2,8,1536]{2,1,0:T(8,128)S(1)}, u32[]{:S(2)}, u32[]{:S(2)}) collective-permute-start(f32[2,8,1536]{2,1,0:T(8,128)S(1)} %shard_map.170.x_ref), channel_id=1, source_target_pairs={{0,1},{1,0},{2,3},{3,2},{4,5},{5,4},{6,7},{7,6},{8,9},{9,8},{10,11... | collective-permute-start | bytes 294920 | tf_op jit(solution)/shard_map/ppermute | solution.py:21
  60.7 11.3 %collective-permute-start.18 = (bf16[160,384]{1,0:T(8,128)(2,1)S(1)}, bf16[160,384]{1,0:T(8,128)(2,1)S(1)}, u32[]{:S(2)}, u32[]{:S(2)}) collective-permute-start(bf16[160,384]{1,0:T(8,128)(2,1)S(1)} %shard_map.168), channel_id=1, source_target_pairs={{0,3},{1,2},{2,1},{3,0},{4,7},{5,6},{6,5},{7,4},{8,11},{9,10},{10,... | collective-permute-start | bytes 368648 | tf_op jit(solution)/shard_map/ppermute | solution.py:21
  64.6 10.5 %collective-permute-start.17 = (bf16[160,384]{1,0:T(8,128)(2,1)S(1)}, bf16[160,384]{1,0:T(8,128)(2,1)S(1)}, u32[]{:S(2)}, u32[]{:S(2)}) collective-permute-start(bf16[160,384]{1,0:T(8,128)(2,1)S(1)} %shard_map.167), channel_id=1, source_target_pairs={{0,2},{1,3},{2,0},{3,1},{4,6},{5,7},{6,4},{7,5},{8,10},{9,11},{10,... | collective-permute-start | bytes 368648 | tf_op jit(solution)/shard_map/ppermute | solution.py:21
  68.0 7.5 %collective-permute-start.16 = (bf16[160,384]{1,0:T(8,128)(2,1)S(1)}, bf16[160,384]{1,0:T(8,128)(2,1)S(1)}, u32[]{:S(2)}, u32[]{:S(2)}) collective-permute-start(bf16[160,384]{1,0:T(8,128)(2,1)S(1)} %shard_map.166), channel_id=1, source_target_pairs={{0,1},{1,0},{2,3},{3,2},{4,5},{5,4},{6,7},{7,6},{8,9},{9,8},{10,11... | collective-permute-start | bytes 368648 | tf_op jit(solution)/shard_map/ppermute | solution.py:21
  71.0 5.3 %collective-permute-start.21 = (f32[2,4,1536]{2,1,0:T(4,128)S(1)}, f32[2,4,1536]{2,1,0:T(4,128)S(1)}, u32[]{:S(2)}, u32[]{:S(2)}) collective-permute-start(f32[2,4,1536]{2,1,0:T(4,128)S(1)} %get-tuple-element.73), channel_id=1, source_target_pairs={{0,16},{16,0},{1,17},{17,1},{2,18},{18,2},{3,19},{19,3},{4,20},{20... | collective-permute-start | bytes 147464 | tf_op jit(solution)/shard_map/ppermute | solution.py:21

commit v4 on v3

--- a/solution.py
+++ b/solution.py
@@ -70,23 +70,11 @@
     rows, width = x.shape
     piece = width // parts
 
-    def body(x_ref, out_ref, sems):
-        copies = [
-            pltpu.make_async_copy(x_ref.at[:, pl.ds(z * piece, piece)], out_ref.at[z], sems.at[z])
-            for z in range(parts)
-        ]
-        for copy in copies:
-            copy.start()
-        for copy in copies:
-            copy.wait()
-
-    return kernel_call(
-        body,
-        jax.ShapeDtypeStruct((parts, rows, piece), x.dtype),
-        in_specs=[pl.BlockSpec(memory_space=pltpu.VMEM)],
-        out_specs=pl.BlockSpec(memory_space=pl.ANY),
-        scratch_shapes=[pltpu.SemaphoreType.DMA((parts,))],
-    )(x)
+    def body(x_ref, out_ref):
+        for z in range(parts):
+            out_ref[z] = x_ref[:, z * piece : (z + 1) * piece]
+
+    return kernel_call(body, jax.ShapeDtypeStruct((parts, rows, piece), x.dtype))(x)
 
 
 def join_rows(pieces, others, axis):
@@ -138,7 +126,7 @@
 
 
 def split_sum(x, y, parts):
-    kinds, count, width = x.shape
+    kinds, count, *rest = x.shape
     part = count // parts
 
     def body(x_ref, y_ref, *outs):
@@ -146,7 +134,7 @@
             here = slice(k * part, (k + 1) * part)
             outs[k][...] = x_ref[:, here] + y_ref[:, here]
 
-    return kernel_call(body, [jax.ShapeDtypeStruct((kinds, part, width), x.dtype)] * parts)(x, y)
+    return kernel_call(body, [jax.ShapeDtypeStruct((kinds, part, *rest), x.dtype)] * parts)(x, y)
 
 
 def square_sums(queries, keys):
@@ -183,23 +171,15 @@
     )
 
 
-def context_gradients(keys, gain, pieces, axis):
+def context_gradients(keys, gain, first, second, axis):
     rows, full = keys.shape
-    parts = len(pieces)
-    width = full // parts
-    flat = [x for piece in pieces for x in piece]
-
-    def body(k_ref, gain_ref, *refs):
-        grad_ref, values_ref, scaled = refs[len(flat) :]
-        at = 0
-        for k, piece in enumerate(pieces):
-            total = refs[at][...]
-            for i in range(1, len(piece)):
-                total = total + refs[at + i][...]
-            at += len(piece)
+    width = first.shape[-1]
+
+    def body(k_ref, gain_ref, first_ref, second_ref, grad_ref, values_ref, scaled):
+        for k in range(full // width):
             cols = columns_of(axis, k, width)
-            scaled[:, cols] = gain_ref[:, cols] * total[0]
-            values_ref[:, cols] = total[1]
+            scaled[:, cols] = gain_ref[:, cols] * (first_ref[2 * k, 0] + second_ref[2 * k, 0])
+            values_ref[:, cols] = first_ref[2 * k + 1, 0] + second_ref[2 * k + 1, 0]
         wide = k_ref[...].astype(jnp.float32)
         recip = context_factor(wide)
         inner = jnp.mean(wide * scaled[...], axis=1, keepdims=True)
@@ -209,7 +189,22 @@
         body,
         [jax.ShapeDtypeStruct((rows, full), jnp.float32)] * 2,
         scratch_shapes=[pltpu.VMEM((rows, full), jnp.float32)],
-    )(keys, gain[None, :], *flat)
+    )(keys, gain[None, :], first, second)
+
+
+def halves(arrays):
+    kinds, count, *rest = arrays[0].shape
+    half = count // 2
+    n = len(arrays)
+
+    def body(*refs):
+        for i in range(n):
+            refs[n][i * kinds : (i + 1) * kinds] = refs[i][:, :half]
+            refs[n + 1][i * kinds : (i + 1) * kinds] = refs[i][:, half:]
+
+    return kernel_call(
+        body, [jax.ShapeDtypeStruct((n * kinds, half, *rest), arrays[0].dtype)] * 2
+    )(*arrays)
 
 
 def norm_factor(total_refs, which, full_width):
@@ -302,15 +297,15 @@
     return kernel_call(body, jax.ShapeDtypeStruct((rows, width), jnp.bfloat16))(query, *arrays)
 
 
-def image_attention(queries, totals, gain, full_width, context, cotangent):
+def image_attention(queries, totals, gain, full_width, context, cotangent, own_count, parts):
     rows, width = queries.shape
     n_totals = len(totals)
     count = context.shape[1]
-    half = count // 2
+    groups = count // (own_count * parts)
     scale = HEAD_DIM ** (-0.5)
 
     def body(*refs):
-        q_ref, gain_ref, c_ref, g_ref, out_ref, keep_ref, send_ref = refs[n_totals:]
+        q_ref, gain_ref, c_ref, g_ref, out_ref, *grad_refs = refs[n_totals:]
         recip = norm_factor(refs[:n_totals], 0, full_width)
         sides = [slice(h, h + HEAD_DIM) for h in range(0, width, HEAD_DIM)]
         heads = []
@@ -337,15 +332,15 @@
             grad_v = jnp.dot(low, g_ref[:, cols], preferred_element_type=jnp.float32)
             grad_k = jnp.dot(grad_s, q, preferred_element_type=jnp.float32) * scale
             for i, grad in enumerate((grad_k, grad_v)):
-                keep_ref[i, :, cols] = grad[:half]
-                send_ref[i, :, cols] = grad[half:]
+                grad = grad.reshape(groups, parts, own_count, HEAD_DIM)
+                for k in range(parts):
+                    grad_refs[k][i, :, :, cols] = grad[:, k]
 
     return kernel_call(
         body,
         [
             jax.ShapeDtypeStruct((rows, width), jnp.bfloat16),
-            jax.ShapeDtypeStruct((2, half, width), jnp.float32),
-            jax.ShapeDtypeStruct((2, half, width), jnp.float32),
+            *[jax.ShapeDtypeStruct((2, groups, own_count, width), jnp.float32)] * parts,
         ],
         (1000, 1000, 0),
     )(*totals, queries, gain[None, :], context, cotangent)
@@ -395,25 +390,26 @@
         self_keys, 1, totals, key_gain, cosine, sine, full_width, "col", parts, True
     )
     context = jnp.concatenate(context, axis=1)
-    bit = n_row // 2
-    while bit:
-        other = after(swap(context, "row", n_row, bit), key_pieces[0])
-        context = jnp.concatenate([context, other], axis=1)
-        bit //= 2
+    others = [0]
+    for bit in row_bits:
+        others += [k ^ bit for k in others]
+    context = [after(swap(context, "row", n_row, k), key_pieces[0]) if k else context for k in others]
+    context = jnp.concatenate(context, axis=1)
     key_pieces = [swap(x, "col", n_col, k) if k else x for k, x in enumerate(key_pieces)]
 
-    image_out, grad, sent = image_attention(
-        queries, totals, query_gain, full_width, context, image_cotangent
-    )
-    values_here = after(values_here, context).reshape(parts * rows, width // parts)
-
+    image_out, *grads = image_attention(
+        queries, totals, query_gain, full_width, context, image_cotangent, own_count, n_enc
+    )
+
+    values_here = after(values_here, grads[0]).reshape(parts * rows, width // parts)
     all_values = [values_here]
     if parts > 1:
         all_values += [swap(values_here, "row", n_row, row_bits[0])]
+    grad, sent = halves([swap(x, "enc", n_enc, k) if k else x for k, x in enumerate(grads)])
     query_here = normed_turned(
-        after(queries, grad), 0, totals, query_gain, cosine, sine, full_width, "col", parts, True
-    )
-    key_pieces = [key_pieces[0], *(after(x, values_here, *query_here) for x in key_pieces[1:])]
+        after(queries, values_here), 0, totals, query_gain, cosine, sine, full_width, "col", parts, True
+    )
+    key_pieces = [key_pieces[0], *(after(x, values_here, sent, *query_here) for x in key_pieces[1:])]
     keys_here, bundle = join_rows(key_pieces, all_values, "col")
     got = keys_here
     if parts > 1:
@@ -429,7 +425,7 @@
 
     for i in range(len(row_bits)):
         if i + 1 < len(row_bits):
-            grad, sent = split_sum(grad, after(swap(sent, "row", n_row, 1 << i), keys_here), 2)
+            grad, sent = split_sum(grad, swap(sent, "row", n_row, 1 << i), 2)
         else:
             grad = split_sum(grad, swap(after(sent, got), "row", n_row, 1 << i), 1)[0]
     if parts > 1:
@@ -449,11 +445,10 @@
             got = after(got, piece)
     if len(steps) > 1:
         grad = split_sum(grad, got, 1)[0]
-        got = after(swap(grad, "col", n_col, steps[1]), mixed[0])
-    grad = split_sum(grad, got, n_enc)
-    grad = [[swap(x, "enc", n_enc, k) if k else x] for k, x in enumerate(grad)]
-    grad_keys_in, grad_values_in = context_gradients(context_keys, context_gain, grad, "enc")
+        got = swap(grad, "col", n_col, steps[1])
     self_out = join_columns(mixed, "col") if parts > 1 else mixed[0]
+    got = after(got, self_out)
+    grad_keys_in, grad_values_in = context_gradients(context_keys, context_gain, grad, got, "enc")
 
     return (self_out, image_out, grad_keys_in, grad_values_in)
 

time: 77.3 us -> 75.2 us (0.973)
  waiting for transfers between devices: 30.9 us -> 27.3 us
  starting transfers between devices: 29.2 us -> 30.7 us
    all_to_all x1, waiting for transfers between devices: 2.33 us -> 0.19 us  [relay(): return lax.all_to_all(x, 'col', split_axis=0, concat_axis=0, tiled=True)]
    ppermute x22 -> x23, waiting for transfers between devices: 28.6 us -> 27.1 us  [swap(): return lax.ppermute(x, axis, [(i, i ^ k) for i in range(size)])]
    ppermute x22 -> x23, starting transfers between devices: 22.9 us -> 24.3 us  [swap(): return lax.ppermute(x, axis, [(i, i ^ k) for i in range(size)])]
  transfers between devices with their start and end apart: 23 -> 24, of which waited for: 11 -> 11; matrix products, arithmetic and copies ran while one was open for 1% -> 1% of each run, Pallas kernels for 16% -> 16%
where the time goes in v4:
time: 75.2 us; the launch traced here: 74.9 us
  starting transfers between devices  30.7 us (41%)
  waiting for transfers between devices  27.3 us (36%)
  Pallas kernels  14 us (19%)
  local copies, waits for them, and re-layouts  1.44 us (2%)
  between operations  0.96 us (1%)
    ppermute x23, waiting for transfers between devices, swap(): return lax.ppermute(x, axis, [(i, i ^ k) for i in range(size)])  27.1 us
    ppermute x23, starting transfers between devices, swap(): return lax.ppermute(x, axis, [(i, i ^ k) for i in range(size)])  24.3 us
    pallas_call x4, Pallas kernels, attention(): kernel_call(body, jax.ShapeDtypeStruct((rows, width), jnp.bfloat16))  7.68 us
    all_to_all x1, starting transfers between devices, relay(): return lax.all_to_all(x, 'col', split_axis=0, concat_axis=0, tiled=True)  6.45 us
    pallas_call x1, Pallas kernels, image_attention(): kernel_call(body, [jax.ShapeDtypeStruct((rows, width), jnp.bfloat16), *[j...  1.92 us
  transfers between devices with their start and end apart: 24, of which 11 were waited for; matrix products, arithmetic and copies ran while one was open for 1% of the time, Pallas kernels for 16%

profile of v4, /device:TPU:0, one launch (start us, length us, event | category | flops | bytes accessed | tf_op | source)
XLA Modules:
  0.0 74.9 jit_solution(11853211266561761875)
XLA Ops:
  0.7 1.1 %copy-done.2 = bf16[160,1536]{1,0:T(8,128)(2,1)S(1)} copy-done((bf16[160,1536]{1,0:T(8,128)(2,1)S(1)}, bf16[160,1536]{1,0:T(8,128)(2,1)}, u32[]{:S(2)}) %copy-start.2) | copy-done | bytes 491544
  1.8 0.8 %shard_map.156 = bf16[4,160,384]{2,1,0:T(8,128)(2,1)} custom-call(bf16[160,1536]{1,0:T(8,128)(2,1)S(1)} %copy-done.2), custom_call_target="tpu_custom_call" | custom-call | tf_op jit(solution)/shard_map/pallas_call | solution.py:77
  2.6 6.4 %all-to-all-start = ((bf16[4,160,384]{2,1,0:T(8,128)(2,1)}), bf16[4,160,384]{2,1,0:T(8,128)(2,1)S(1)}, u32[]{:S(2)}, u32[]{:S(2)}) async-start(bf16[4,160,384]{2,1,0:T(8,128)(2,1)} %shard_map.156), calls=%async_computation | async-start | bytes 983040 | tf_op jit(solution)/shard_map/all_to_all | solution.py:372
  9.1 0.1 shard_map.157
  9.3 0.3 shard_map.158.refs_0_
  9.5 1.5 %collective-permute-start = (f32[160,2]{1,0:T(8,128)S(1)}, f32[160,2]{1,0:T(8,128)S(1)}, u32[]{:S(2)}, u32[]{:S(2)}) collective-permute-start(f32[160,2]{1,0:T(8,128)S(1)} %shard_map.158.refs_0_), channel_id=1, source_target_pairs={{0,16},{16,0},{1,17},{17,1},{2,18},{18,2},{3,19},{19,3},{4,20},{20... | collective-permute-start | bytes 3848 | tf_op jit(solution)/shard_map/ppermute | solution.py:21
  11.1 0.5 collective-permute-start.1
  11.6 0.1 pad_maximum_fusion.1
  11.7 0.1 broadcast_in_dim.64
  11.8 0.1 mul.20
  11.9 2.9 %collective-permute-done.1 = bf16[2,4,1536]{2,1,0:T(4,128)(2,1)S(1)} collective-permute-done((bf16[2,4,1536]{2,1,0:T(4,128)(2,1)S(1)}, bf16[2,4,1536]{2,1,0:T(4,128)(2,1)S(1)}, u32[]{:S(2)}, u32[]{:S(2)}) %collective-permute-start.1) | collective-permute-done | bytes 24608 | tf_op jit(solution)/shard_map/ppermute | solution.py:21
  15.0 1.6 %collective-permute-start.3 = (bf16[2,8,1536]{2,1,0:T(8,128)(2,1)S(1)}, bf16[2,8,1536]{2,1,0:T(8,128)(2,1)S(1)}, u32[]{:S(2)}, u32[]{:S(2)}) collective-permute-start(bf16[2,8,1536]{2,1,0:T(8,128)(2,1)S(1)} %pad_maximum_fusion), channel_id=1, source_target_pairs={{0,4},{4,0},{8,12},{12,8},{1,5},{5,1},{9,13},{13,9},{2,6},{6,2},{1... | collective-permute-start | bytes 147464 | tf_op jit(solution)/shard_map/ppermute | solution.py:21
  16.6 0.5 collective-permute-start.2
  17.1 0.4 sine_multiply_fusion
  17.6 0.7 shard_map.159
  18.3 0.7 collective-permute-done.4
  19.0 1.8 %collective-permute-done.2 = bf16[2,8,1536]{2,1,0:T(8,128)(2,1)S(1)} collective-permute-done((bf16[2,8,1536]{2,1,0:T(8,128)(2,1)S(1)}, bf16[2,8,1536]{2,1,0:T(8,128)(2,1)S(1)}, u32[]{:S(2)}, u32[]{:S(2)}) %collective-permute-start.2) | collective-permute-done | bytes 49184 | tf_op jit(solution)/shard_map/ppermute | solution.py:21
  20.8 1.9 %shard_map.160 = (bf16[160,1536]{1,0:T(8,128)(2,1)}, f32[2,4,4,1536]{3,2,1,0:T(4,128)S(1)}, f32[2,4,4,1536]{3,2,1,0:T(4,128)S(1)}) custom-call(f32[160,2]{1,0:T(8,128)S(1)} %shard_map.158.refs_0_, f32[160,2]{1,0:T(8,128)S(1)} %collective-permute-done.refs_1_, bf16[160,1536]{1,0:T(8,128)(2,1)S(1)} %copy-done, f32[1,1536]{1,0:T(1,128)S(1)} %broadcast_in_dim.54.refs_3_, ...), custom_call_target="tpu_custom_call" | custom-call | flops 1000 | bytes 1000 | tf_op jit(solution)/shard_map/pallas_call | solution.py:339
  22.7 0.2 all-to-all-done
  22.9 1.5 %collective-permute-start.9 = (bf16[640,384]{1,0:T(8,128)(2,1)S(1)}, bf16[640,384]{1,0:T(8,128)(2,1)S(1)}, u32[]{:S(2)}, u32[]{:S(2)}) collective-permute-start(bf16[640,384]{1,0:T(8,128)(2,1)S(1)} %bitcast.5), channel_id=1, source_target_pairs={{0,8},{4,12},{8,0},{12,4},{1,9},{5,13},{9,1},{13,5},{2,10},{6,14},... | collective-permute-start | bytes 1474568 | tf_op jit(solution)/shard_map/ppermute | solution.py:21
  24.4 1.5 %collective-permute-start.6 = (f32[2,4,4,1536]{3,2,1,0:T(4,128)S(1)}, f32[2,4,4,1536]{3,2,1,0:T(4,128)S(1)}, u32[]{:S(2)}, u32[]{:S(2)}) collective-permute-start(f32[2,4,4,1536]{3,2,1,0:T(4,128)S(1)} %get-tuple-element.54), channel_id=1, source_target_pairs={{0,16},{16,0},{1,17},{17,1},{2,18},{18,2},{3,19},{19,3},{4,20},{20... | collective-permute-start | bytes 589832 | tf_op jit(solution)/shard_map/ppermute | solution.py:21
  25.9 2.0 %collective-permute-start.8 = (bf16[160,384]{1,0:T(8,128)(2,1)S(1)}, bf16[160,384]{1,0:T(8,128)(2,1)S(1)}, u32[]{:S(2)}, u32[]{:S(2)}) collective-permute-start(bf16[160,384]{1,0:T(8,128)(2,1)S(1)} %get-tuple-element.62), channel_id=1, source_target_pairs={{0,3},{1,2},{2,1},{3,0},{4,7},{5,6},{6,5},{7,4},{8,11},{9,10},{10,... | collective-permute-start | bytes 368648 | tf_op jit(solution)/shard_map/ppermute | solution.py:21
  27.9 2.4 %collective-permute-start.5 = (bf16[160,384]{1,0:T(8,128)(2,1)S(1)}, bf16[160,384]{1,0:T(8,128)(2,1)S(1)}, u32[]{:S(2)}, u32[]{:S(2)}) collective-permute-start(bf16[160,384]{1,0:T(8,128)(2,1)S(1)} %get-tuple-element.53), channel_id=1, source_target_pairs={{0,1},{1,0},{2,3},{3,2},{4,5},{5,4},{6,7},{7,6},{8,9},{9,8},{10,11... | collective-permute-start | bytes 368648 | tf_op jit(solution)/shard_map/ppermute | solution.py:21
  30.3 0.7 shard_map.161
  31.0 3.0 %collective-permute-done.8.refs_3_ = bf16[160,384]{1,0:T(8,128)(2,1)S(1)} collective-permute-done((bf16[160,384]{1,0:T(8,128)(2,1)S(1)}, bf16[160,384]{1,0:T(8,128)(2,1)S(1)}, u32[]{:S(2)}, u32[]{:S(2)}) %collective-permute-start.8) | collective-permute-done | bytes 122912 | tf_op jit(solution)/shard_map/ppermute | solution.py:21
  34.0 4.0 %collective-permute-done.7.refs_2_ = bf16[160,384]{1,0:T(8,128)(2,1)S(1)} collective-permute-done((bf16[160,384]{1,0:T(8,128)(2,1)S(1)}, bf16[160,384]{1,0:T(8,128)(2,1)S(1)}, u32[]{:S(2)}, u32[]{:S(2)}) %collective-permute-start.7) | collective-permute-done | bytes 122912 | tf_op jit(solution)/shard_map/ppermute | solution.py:21
  38.0 0.2 shard_map.163
  38.3 0.8 %collective-permute-start.10 = (bf16[640,384]{1,0:T(8,128)(2,1)S(1)}, bf16[640,384]{1,0:T(8,128)(2,1)S(1)}, u32[]{:S(2)}, u32[]{:S(2)}) collective-permute-start(bf16[640,384]{1,0:T(8,128)(2,1)S(1)} %get-tuple-element.64.refs_0_), channel_id=1, source_target_pairs={{0,8},{4,12},{8,0},{12,4},{1,9},{5,13},{9,1},{13,5},{2,10},{6,14},... | collective-permute-start | bytes 1474568 | tf_op jit(solution)/shard_map/ppermute | solution.py:21
  39.1 0.2 collective-permute-start.12
  39.3 2.9 %collective-permute-start.15 = (bf16[160,384]{1,0:T(8,128)(2,1)S(1)}, bf16[160,384]{1,0:T(8,128)(2,1)S(1)}, u32[]{:S(2)}, u32[]{:S(2)}) collective-permute-start(bf16[160,384]{1,0:T(8,128)(2,1)S(1)} %get-tuple-element.57), channel_id=1, source_target_pairs={{0,2},{1,3},{2,0},{3,1},{4,6},{5,7},{6,4},{7,5},{8,10},{9,11},{10,... | collective-permute-start | bytes 368648 | tf_op jit(solution)/shard_map/ppermute | solution.py:21
  42.2 1.7 %collective-permute-start.16 = (bf16[160,384]{1,0:T(8,128)(2,1)S(1)}, bf16[160,384]{1,0:T(8,128)(2,1)S(1)}, u32[]{:S(2)}, u32[]{:S(2)}) collective-permute-start(bf16[160,384]{1,0:T(8,128)(2,1)S(1)} %get-tuple-element.58), channel_id=1, source_target_pairs={{0,3},{1,2},{2,1},{3,0},{4,7},{5,6},{6,5},{7,4},{8,11},{9,10},{10,... | collective-permute-start | bytes 368648 | tf_op jit(solution)/shard_map/ppermute | solution.py:21
  44.0 1.1 %collective-permute-start.13 = (f32[4,1,4,1536]{3,2,1,0:T(4,128)S(1)}, f32[4,1,4,1536]{3,2,1,0:T(4,128)S(1)}, u32[]{:S(2)}, u32[]{:S(2)}) collective-permute-start(f32[4,1,4,1536]{3,2,1,0:T(4,128)S(1)} %get-tuple-element.69), channel_id=1, source_target_pairs={{0,8},{4,12},{8,0},{12,4},{1,9},{5,13},{9,1},{13,5},{2,10},{6,14},... | collective-permute-start | bytes 294920 | tf_op jit(solution)/shard_map/ppermute | solution.py:21
  45.1 9.0 %collective-permute-done.13.y_ref = f32[4,1,4,1536]{3,2,1,0:T(4,128)S(1)} collective-permute-done((f32[4,1,4,1536]{3,2,1,0:T(4,128)S(1)}, f32[4,1,4,1536]{3,2,1,0:T(4,128)S(1)}, u32[]{:S(2)}, u32[]{:S(2)}) %collective-permute-start.13) | collective-permute-done | bytes 98336 | tf_op jit(solution)/shard_map/ppermute | solution.py:21
  54.2 1.0 %collective-permute-start.21 = (f32[4,1,4,1536]{3,2,1,0:T(4,128)S(1)}, f32[4,1,4,1536]{3,2,1,0:T(4,128)S(1)}, u32[]{:S(2)}, u32[]{:S(2)}) collective-permute-start(f32[4,1,4,1536]{3,2,1,0:T(4,128)S(1)} %shard_map.165.x_ref), channel_id=1, source_target_pairs={{0,2},{1,3},{2,0},{3,1},{4,6},{5,7},{6,4},{7,5},{8,10},{9,11},{10,... | collective-permute-start | bytes 294920 | tf_op jit(solution)/shard_map/ppermute | solution.py:21
  55.2 0.8 %collective-permute-done.17.refs_3_ = bf16[640,384]{1,0:T(8,128)(2,1)S(1)} collective-permute-done((bf16[640,384]{1,0:T(8,128)(2,1)S(1)}, bf16[640,384]{1,0:T(8,128)(2,1)S(1)}, u32[]{:S(2)}, u32[]{:S(2)}) %collective-permute-start.17) | collective-permute-done | bytes 491552 | tf_op jit(solution)/shard_map/ppermute | solution.py:21
  56.0 1.9 %shard_map.169 = bf16[160,384]{1,0:T(8,128)(2,1)S(1)} custom-call(bf16[160,384]{1,0:T(8,128)(2,1)S(1)} %collective-permute-done.16.q_ref, bf16[640,384]{1,0:T(8,128)(2,1)S(1)} %get-tuple-element.64.refs_0_, bf16[640,384]{1,0:T(8,128)(2,1)S(1)} %collective-permute-done.10.refs_1_, bf16[3,640,384]{2,1,0:T(8,128)(2,1)S(1)} %collective-permute-done.11.refs_2_, ...), custom_call_target="tpu_custom_call" | custom-call | tf_op jit(solution)/shard_map/pallas_call | solution.py:297
  57.9 2.2 %collective-permute-start.20 = (bf16[160,384]{1,0:T(8,128)(2,1)S(1)}, bf16[160,384]{1,0:T(8,128)(2,1)S(1)}, u32[]{:S(2)}, u32[]{:S(2)}) collective-permute-start(bf16[160,384]{1,0:T(8,128)(2,1)S(1)} %shard_map.169), channel_id=1, source_target_pairs={{0,3},{1,2},{2,1},{3,0},{4,7},{5,6},{6,5},{7,4},{8,11},{9,10},{10,... | collective-permute-start | bytes 368648 | tf_op jit(solution)/shard_map/ppermute | solution.py:21
  60.1 1.9 %shard_map.168 = bf16[160,384]{1,0:T(8,128)(2,1)S(1)} custom-call(bf16[160,384]{1,0:T(8,128)(2,1)S(1)} %collective-permute-done.15.q_ref, bf16[640,384]{1,0:T(8,128)(2,1)S(1)} %get-tuple-element.64.refs_0_, bf16[640,384]{1,0:T(8,128)(2,1)S(1)} %collective-permute-done.10.refs_1_, bf16[3,640,384]{2,1,0:T(8,128)(2,1)S(1)} %collective-permute-done.11.refs_2_, ...), custom_call_target="tpu_custom_call" | custom-call | tf_op jit(solution)/shard_map/pallas_call | solution.py:297
  62.0 0.3 collective-permute-start.19
  62.3 1.9 %shard_map.167 = bf16[160,384]{1,0:T(8,128)(2,1)S(1)} custom-call(bf16[160,384]{1,0:T(8,128)(2,1)S(1)} %collective-permute-done.14.q_ref, bf16[640,384]{1,0:T(8,128)(2,1)S(1)} %get-tuple-element.64.refs_0_, bf16[640,384]{1,0:T(8,128)(2,1)S(1)} %collective-permute-done.10.refs_1_, bf16[3,640,384]{2,1,0:T(8,128)(2,1)S(1)} %collective-permute-done.11.refs_2_, ...), custom_call_target="tpu_custom_call" | custom-call | tf_op jit(solution)/shard_map/pallas_call | solution.py:297
  64.2 2.1 %collective-permute-start.18 = (bf16[160,384]{1,0:T(8,128)(2,1)S(1)}, bf16[160,384]{1,0:T(8,128)(2,1)S(1)}, u32[]{:S(2)}, u32[]{:S(2)}) collective-permute-start(bf16[160,384]{1,0:T(8,128)(2,1)S(1)} %shard_map.167), channel_id=1, source_target_pairs={{0,1},{1,0},{2,3},{3,2},{4,5},{5,4},{6,7},{7,6},{8,9},{9,8},{10,11... | collective-permute-start | bytes 368648 | tf_op jit(solution)/shard_map/ppermute | solution.py:21
  66.4 0.1 collective-permute-start.22
  66.5 1.9 %shard_map.166.refs_0_ = bf16[160,384]{1,0:T(8,128)(2,1)S(1)} custom-call(bf16[160,384]{1,0:T(8,128)(2,1)S(1)} %get-tuple-element.52.q_ref, bf16[640,384]{1,0:T(8,128)(2,1)S(1)} %get-tuple-element.64.refs_0_, bf16[640,384]{1,0:T(8,128)(2,1)S(1)} %collective-permute-done.10.refs_1_, bf16[3,640,384]{2,1,0:T(8,128)(2,1)S(1)} %collective-permute-done.11.refs_2_, ...), custom_call_target="tpu_custom_call" | custom-call | tf_op jit(solution)/shard_map/pallas_call | solution.py:297
  68.4 4.2 %collective-permute-done.19.refs_2_ = bf16[160,384]{1,0:T(8,128)(2,1)S(1)} collective-permute-done((bf16[160,384]{1,0:T(8,128)(2,1)S(1)}, bf16[160,384]{1,0:T(8,128)(2,1)S(1)}, u32[]{:S(2)}, u32[]{:S(2)}) %collective-permute-start.19) | collective-permute-done | bytes 122912 | tf_op jit(solution)/shard_map/ppermute | solution.py:21
  72.6 0.5 collective-permute-done.18.refs_1_
  73.1 0.8 %shard_map.170 = bf16[160,1536]{1,0:T(8,128)(2,1)} custom-call(bf16[160,384]{1,0:T(8,128)(2,1)S(1)} %shard_map.166.refs_0_, bf16[160,384]{1,0:T(8,128)(2,1)S(1)} %collective-permute-done.18.refs_1_, bf16[160,384]{1,0:T(8,128)(2,1)S(1)} %collective-permute-done.19.refs_2_, bf16[160,384]{1,0:T(8,128)(2,1)S(1)} %collective-permute-done.20.refs_3_), custom_call_target="tpu_custom_call" | custom-call | tf_op jit(solution)/shard_map/pallas_call | solution.py:119
  73.9 0.2 collective-permute-done.22.second_ref
  74.2 0.8 %shard_map.172 = (f32[4,3072]{1,0:T(4,128)}, f32[4,3072]{1,0:T(4,128)}) custom-call(bf16[4,3072]{1,0:T(4,128)(2,1)S(1)} %copy-done.4, f32[1,3072]{1,0:T(1,128)S(1)} %bitcast.12, f32[4,1,4,1536]{3,2,1,0:T(4,128)S(1)} %shard_map.171.first_ref, f32[4,1,4,1536]{3,2,1,0:T(4,128)S(1)} %collective-permute-done.22.second_ref), custom_call_target="tpu_custom_call" | custom-call | tf_op jit(solution)/shard_map/pallas_call | solution.py:188
  (55 shorter events, 0.5 us)
Async XLA Ops:
  0.6 16.5 %copy-start.10 = (pred[128]{0:T(512)(128)(4,1)S(1)}, pred[128]{0:T(512)(128)(4,1)}, u32[]{:S(2)}) copy-start(pred[128]{0:T(512)(128)(4,1)} %constant.10.clone) | copy-start | bytes 388
  0.6 16.5 %copy-start.11 = (pred[128]{0:T(512)(128)(4,1)S(1)}, pred[128]{0:T(512)(128)(4,1)}, u32[]{:S(2)}) copy-start(pred[128]{0:T(512)(128)(4,1)} %constant.22.clone) | copy-start | bytes 388
  0.7 8.6 %copy-start = (bf16[160,1536]{1,0:T(8,128)(2,1)S(1)}, bf16[160,1536]{1,0:T(8,128)(2,1)}, u32[]{:S(2)}) copy-start(bf16[160,1536]{1,0:T(8,128)(2,1)} %refs_2_.4) | copy-start | bytes 1474564
  0.7 8.6 %copy-start.1 = (bf16[160,1536]{1,0:T(8,128)(2,1)S(1)}, bf16[160,1536]{1,0:T(8,128)(2,1)}, u32[]{:S(2)}) copy-start(bf16[160,1536]{1,0:T(8,128)(2,1)} %refs_2_.2) | copy-start | bytes 1474564
  0.7 1.1 %copy-start.2 = (bf16[160,1536]{1,0:T(8,128)(2,1)S(1)}, bf16[160,1536]{1,0:T(8,128)(2,1)}, u32[]{:S(2)}) copy-start(bf16[160,1536]{1,0:T(8,128)(2,1)} %x_ref.1) | copy-start | bytes 1474564
  1.8 7.3 %copy-start.4 = (bf16[4,3072]{1,0:T(4,128)(2,1)S(1)}, bf16[4,3072]{1,0:T(4,128)(2,1)}, u32[]{:S(2)}) copy-start(bf16[4,3072]{1,0:T(4,128)(2,1)} %k_ref.4) | copy-start | bytes 73732
  1.8 7.3 %copy-start.5 = (f32[3072]{0:T(1024)S(1)}, f32[3072]{0:T(1024)}, u32[]{:S(2)}) copy-start(f32[3072]{0:T(1024)} %param.21) | copy-start | bytes 36868
  1.8 7.3 %copy-start.6 = (bf16[4,3072]{1,0:T(4,128)(2,1)S(1)}, bf16[4,3072]{1,0:T(4,128)(2,1)}, u32[]{:S(2)}) copy-start(bf16[4,3072]{1,0:T(4,128)(2,1)} %v_ref.1) | copy-start | bytes 73732
  1.8 9.8 %copy-start.9 = (s32[160,3]{0,1:T(4,128)S(1)}, s32[160,3]{0,1:T(4,128)}, u32[]{:S(2)}) copy-start(s32[160,3]{0,1:T(4,128)} %param.16) | copy-start | bytes 5764
  1.8 15.3 %copy-start.12 = (f32[128]{0:T(128)S(1)}, f32[128]{0:T(128)}, u32[]{:S(2)}) copy-start(f32[128]{0:T(128)} %constant.23.clone) | copy-start | bytes 1540
  2.6 14.9 %copy-start.7 = (f32[1536]{0:T(1024)S(1)}, f32[1536]{0:T(1024)}, u32[]{:S(2)}) copy-start(f32[1536]{0:T(1024)} %param.18) | copy-start | bytes 18436
  2.6 14.9 %copy-start.8 = (f32[1536]{0:T(1024)S(1)}, f32[1536]{0:T(1024)}, u32[]{:S(2)}) copy-start(f32[1536]{0:T(1024)} %param.17) | copy-start | bytes 18436
  2.6 20.2 %all-to-all-start = ((bf16[4,160,384]{2,1,0:T(8,128)(2,1)}), bf16[4,160,384]{2,1,0:T(8,128)(2,1)S(1)}, u32[]{:S(2)}, u32[]{:S(2)}) async-start(bf16[4,160,384]{2,1,0:T(8,128)(2,1)} %shard_map.156), calls=%async_computation | async-start | bytes 983040 | tf_op jit(solution)/shard_map/all_to_all | solution.py:372
  9.1 11.7 %copy-start.3 = (bf16[160,1536]{1,0:T(8,128)(2,1)S(1)}, bf16[160,1536]{1,0:T(8,128)(2,1)}, u32[]{:S(2)}) copy-start(bf16[160,1536]{1,0:T(8,128)(2,1)} %refs_5_.1) | copy-start | bytes 1474564
  9.5 8.1 %collective-permute-start = (f32[160,2]{1,0:T(8,128)S(1)}, f32[160,2]{1,0:T(8,128)S(1)}, u32[]{:S(2)}, u32[]{:S(2)}) collective-permute-start(f32[160,2]{1,0:T(8,128)S(1)} %shard_map.158.refs_0_), channel_id=1, source_target_pairs={{0,16},{16,0},{1,17},{17,1},{2,18},{18,2},{3,19},{19,3},{4,20},{20... | collective-permute-start | bytes 3848 | tf_op jit(solution)/shard_map/ppermute | solution.py:21
  11.1 3.8 %collective-permute-start.1 = (bf16[2,4,1536]{2,1,0:T(4,128)(2,1)S(1)}, bf16[2,4,1536]{2,1,0:T(4,128)(2,1)S(1)}, u32[]{:S(2)}, u32[]{:S(2)}) collective-permute-start(bf16[2,4,1536]{2,1,0:T(4,128)(2,1)S(1)} %get-tuple-element.43), channel_id=1, source_target_pairs={{0,16},{16,0},{1,17},{17,1},{2,18},{18,2},{3,19},{19,3},{4,20},{20... | collective-permute-start | bytes 73736 | tf_op jit(solution)/shard_map/ppermute | solution.py:21
  14.9 4.0 %collective-permute-start.4 = (bf16[2,8,1536]{2,1,0:T(8,128)(2,1)S(1)}, bf16[2,8,1536]{2,1,0:T(8,128)(2,1)S(1)}, u32[]{:S(2)}, u32[]{:S(2)}) collective-permute-start(bf16[2,8,1536]{2,1,0:T(8,128)(2,1)S(1)} %pad_maximum_fusion), channel_id=1, source_target_pairs={{0,12},{4,8},{8,4},{12,0},{1,13},{5,9},{9,5},{13,1},{2,14},{6,10},... | collective-permute-start | bytes 147464 | tf_op jit(solution)/shard_map/ppermute | solution.py:21
  15.0 4.0 %collective-permute-start.3 = (bf16[2,8,1536]{2,1,0:T(8,128)(2,1)S(1)}, bf16[2,8,1536]{2,1,0:T(8,128)(2,1)S(1)}, u32[]{:S(2)}, u32[]{:S(2)}) collective-permute-start(bf16[2,8,1536]{2,1,0:T(8,128)(2,1)S(1)} %pad_maximum_fusion), channel_id=1, source_target_pairs={{0,4},{4,0},{8,12},{12,8},{1,5},{5,1},{9,13},{13,9},{2,6},{6,2},{1... | collective-permute-start | bytes 147464 | tf_op jit(solution)/shard_map/ppermute | solution.py:21
  16.6 4.1 %collective-permute-start.2 = (bf16[2,8,1536]{2,1,0:T(8,128)(2,1)S(1)}, bf16[2,8,1536]{2,1,0:T(8,128)(2,1)S(1)}, u32[]{:S(2)}, u32[]{:S(2)}) collective-permute-start(bf16[2,8,1536]{2,1,0:T(8,128)(2,1)S(1)} %pad_maximum_fusion), channel_id=1, source_target_pairs={{0,8},{4,12},{8,0},{12,4},{1,9},{5,13},{9,1},{13,5},{2,10},{6,14},... | collective-permute-start | bytes 147464 | tf_op jit(solution)/shard_map/ppermute | solution.py:21
  22.9 15.1 %collective-permute-start.9 = (bf16[640,384]{1,0:T(8,128)(2,1)S(1)}, bf16[640,384]{1,0:T(8,128)(2,1)S(1)}, u32[]{:S(2)}, u32[]{:S(2)}) collective-permute-start(bf16[640,384]{1,0:T(8,128)(2,1)S(1)} %bitcast.5), channel_id=1, source_target_pairs={{0,8},{4,12},{8,0},{12,4},{1,9},{5,13},{9,1},{13,5},{2,10},{6,14},... | collective-permute-start | bytes 1474568 | tf_op jit(solution)/shard_map/ppermute | solution.py:21
  24.4 5.9 %collective-permute-start.6 = (f32[2,4,4,1536]{3,2,1,0:T(4,128)S(1)}, f32[2,4,4,1536]{3,2,1,0:T(4,128)S(1)}, u32[]{:S(2)}, u32[]{:S(2)}) collective-permute-start(f32[2,4,4,1536]{3,2,1,0:T(4,128)S(1)} %get-tuple-element.54), channel_id=1, source_target_pairs={{0,16},{16,0},{1,17},{17,1},{2,18},{18,2},{3,19},{19,3},{4,20},{20... | collective-permute-start | bytes 589832 | tf_op jit(solution)/shard_map/ppermute | solution.py:21
  25.9 8.1 %collective-permute-start.8 = (bf16[160,384]{1,0:T(8,128)(2,1)S(1)}, bf16[160,384]{1,0:T(8,128)(2,1)S(1)}, u32[]{:S(2)}, u32[]{:S(2)}) collective-permute-start(bf16[160,384]{1,0:T(8,128)(2,1)S(1)} %get-tuple-element.62), channel_id=1, source_target_pairs={{0,3},{1,2},{2,1},{3,0},{4,7},{5,6},{6,5},{7,4},{8,11},{9,10},{10,... | collective-permute-start | bytes 368648 | tf_op jit(solution)/shard_map/ppermute | solution.py:21
  27.9 10.1 %collective-permute-start.7 = (bf16[160,384]{1,0:T(8,128)(2,1)S(1)}, bf16[160,384]{1,0:T(8,128)(2,1)S(1)}, u32[]{:S(2)}, u32[]{:S(2)}) collective-permute-start(bf16[160,384]{1,0:T(8,128)(2,1)S(1)} %get-tuple-element.60), channel_id=1, source_target_pairs={{0,2},{1,3},{2,0},{3,1},{4,6},{5,7},{6,4},{7,5},{8,10},{9,11},{10,... | collective-permute-start | bytes 368648 | tf_op jit(solution)/shard_map/ppermute | solution.py:21
  27.9 10.1 %collective-permute-start.5 = (bf16[160,384]{1,0:T(8,128)(2,1)S(1)}, bf16[160,384]{1,0:T(8,128)(2,1)S(1)}, u32[]{:S(2)}, u32[]{:S(2)}) collective-permute-start(bf16[160,384]{1,0:T(8,128)(2,1)S(1)} %get-tuple-element.53), channel_id=1, source_target_pairs={{0,1},{1,0},{2,3},{3,2},{4,5},{5,4},{6,7},{7,6},{8,9},{9,8},{10,11... | collective-permute-start | bytes 368648 | tf_op jit(solution)/shard_map/ppermute | solution.py:21
  38.2 5.7 %collective-permute-start.11 = (bf16[3,640,384]{2,1,0:T(8,128)(2,1)S(1)}, bf16[3,640,384]{2,1,0:T(8,128)(2,1)S(1)}, u32[]{:S(2)}, u32[]{:S(2)}) collective-permute-start(bf16[3,640,384]{2,1,0:T(8,128)(2,1)S(1)} %get-tuple-element.65), channel_id=1, source_target_pairs={{0,4},{4,0},{8,12},{12,8},{1,5},{5,1},{9,13},{13,9},{2,6},{6,2},{1... | collective-permute-start | bytes 4423688 | tf_op jit(solution)/shard_map/ppermute | solution.py:21
  38.3 15.8 %collective-permute-start.10 = (bf16[640,384]{1,0:T(8,128)(2,1)S(1)}, bf16[640,384]{1,0:T(8,128)(2,1)S(1)}, u32[]{:S(2)}, u32[]{:S(2)}) collective-permute-start(bf16[640,384]{1,0:T(8,128)(2,1)S(1)} %get-tuple-element.64.refs_0_), channel_id=1, source_target_pairs={{0,8},{4,12},{8,0},{12,4},{1,9},{5,13},{9,1},{13,5},{2,10},{6,14},... | collective-permute-start | bytes 1474568 | tf_op jit(solution)/shard_map/ppermute | solution.py:21
  39.1 3.1 %collective-permute-start.12 = (f32[4,2,4,1536]{3,2,1,0:T(4,128)S(1)}, f32[4,2,4,1536]{3,2,1,0:T(4,128)S(1)}, u32[]{:S(2)}, u32[]{:S(2)}) collective-permute-start(f32[4,2,4,1536]{3,2,1,0:T(4,128)S(1)} %get-tuple-element.55), channel_id=1, source_target_pairs={{0,4},{4,0},{8,12},{12,8},{1,5},{5,1},{9,13},{13,9},{2,6},{6,2},{1... | collective-permute-start | bytes 589832 | tf_op jit(solution)/shard_map/ppermute | solution.py:21
  39.3 14.8 %collective-permute-start.14 = (bf16[160,384]{1,0:T(8,128)(2,1)S(1)}, bf16[160,384]{1,0:T(8,128)(2,1)S(1)}, u32[]{:S(2)}, u32[]{:S(2)}) collective-permute-start(bf16[160,384]{1,0:T(8,128)(2,1)S(1)} %get-tuple-element.56), channel_id=1, source_target_pairs={{0,1},{1,0},{2,3},{3,2},{4,5},{5,4},{6,7},{7,6},{8,9},{9,8},{10,11... | collective-permute-start | bytes 368648 | tf_op jit(solution)/shard_map/ppermute | solution.py:21
  39.3 14.8 %collective-permute-start.15 = (bf16[160,384]{1,0:T(8,128)(2,1)S(1)}, bf16[160,384]{1,0:T(8,128)(2,1)S(1)}, u32[]{:S(2)}, u32[]{:S(2)}) collective-permute-start(bf16[160,384]{1,0:T(8,128)(2,1)S(1)} %get-tuple-element.57), channel_id=1, source_target_pairs={{0,2},{1,3},{2,0},{3,1},{4,6},{5,7},{6,4},{7,5},{8,10},{9,11},{10,... | collective-permute-start | bytes 368648 | tf_op jit(solution)/shard_map/ppermute | solution.py:21
  42.2 11.8 %collective-permute-start.16 = (bf16[160,384]{1,0:T(8,128)(2,1)S(1)}, bf16[160,384]{1,0:T(8,128)(2,1)S(1)}, u32[]{:S(2)}, u32[]{:S(2)}) collective-permute-start(bf16[160,384]{1,0:T(8,128)(2,1)S(1)} %get-tuple-element.58), channel_id=1, source_target_pairs={{0,3},{1,2},{2,1},{3,0},{4,7},{5,6},{6,5},{7,4},{8,11},{9,10},{10,... | collective-permute-start | bytes 368648 | tf_op jit(solution)/shard_map/ppermute | solution.py:21
  44.0 10.1 %collective-permute-start.13 = (f32[4,1,4,1536]{3,2,1,0:T(4,128)S(1)}, f32[4,1,4,1536]{3,2,1,0:T(4,128)S(1)}, u32[]{:S(2)}, u32[]{:S(2)}) collective-permute-start(f32[4,1,4,1536]{3,2,1,0:T(4,128)S(1)} %get-tuple-element.69), channel_id=1, source_target_pairs={{0,8},{4,12},{8,0},{12,4},{1,9},{5,13},{9,1},{13,5},{2,10},{6,14},... | collective-permute-start | bytes 294920 | tf_op jit(solution)/shard_map/ppermute | solution.py:21
  54.1 1.9 %collective-permute-start.17 = (bf16[640,384]{1,0:T(8,128)(2,1)S(1)}, bf16[640,384]{1,0:T(8,128)(2,1)S(1)}, u32[]{:S(2)}, u32[]{:S(2)}) collective-permute-start(bf16[640,384]{1,0:T(8,128)(2,1)S(1)} %collective-permute-done.10.refs_1_), channel_id=1, source_target_pairs={{0,4},{4,0},{8,12},{12,8},{1,5},{5,1},{9,13},{13,9},{2,6},{6,2},{1... | collective-permute-start | bytes 1474568 | tf_op jit(solution)/shard_map/ppermute | solution.py:21
  54.2 12.2 %collective-permute-start.21 = (f32[4,1,4,1536]{3,2,1,0:T(4,128)S(1)}, f32[4,1,4,1536]{3,2,1,0:T(4,128)S(1)}, u32[]{:S(2)}, u32[]{:S(2)}) collective-permute-start(f32[4,1,4,1536]{3,2,1,0:T(4,128)S(1)} %shard_map.165.x_ref), channel_id=1, source_target_pairs={{0,2},{1,3},{2,0},{3,1},{4,6},{5,7},{6,4},{7,5},{8,10},{9,11},{10,... | collective-permute-start | bytes 294920 | tf_op jit(solution)/shard_map/ppermute | solution.py:21
  57.9 10.5 %collective-permute-start.20 = (bf16[160,384]{1,0:T(8,128)(2,1)S(1)}, bf16[160,384]{1,0:T(8,128)(2,1)S(1)}, u32[]{:S(2)}, u32[]{:S(2)}) collective-permute-start(bf16[160,384]{1,0:T(8,128)(2,1)S(1)} %shard_map.169), channel_id=1, source_target_pairs={{0,3},{1,2},{2,1},{3,0},{4,7},{5,6},{6,5},{7,4},{8,11},{9,10},{10,... | collective-permute-start | bytes 368648 | tf_op jit(solution)/shard_map/ppermute | solution.py:21
  62.0 10.6 %collective-permute-start.19 = (bf16[160,384]{1,0:T(8,128)(2,1)S(1)}, bf16[160,384]{1,0:T(8,128)(2,1)S(1)}, u32[]{:S(2)}, u32[]{:S(2)}) collective-permute-start(bf16[160,384]{1,0:T(8,128)(2,1)S(1)} %shard_map.168), channel_id=1, source_target_pairs={{0,2},{1,3},{2,0},{3,1},{4,6},{5,7},{6,4},{7,5},{8,10},{9,11},{10,... | collective-permute-start | bytes 368648 | tf_op jit(solution)/shard_map/ppermute | solution.py:21
  64.2 8.9 %collective-permute-start.18 = (bf16[160,384]{1,0:T(8,128)(2,1)S(1)}, bf16[160,384]{1,0:T(8,128)(2,1)S(1)}, u32[]{:S(2)}, u32[]{:S(2)}) collective-permute-start(bf16[160,384]{1,0:T(8,128)(2,1)S(1)} %shard_map.167), channel_id=1, source_target_pairs={{0,1},{1,0},{2,3},{3,2},{4,5},{5,4},{6,7},{7,6},{8,9},{9,8},{10,11... | collective-permute-start | bytes 368648 | tf_op jit(solution)/shard_map/ppermute | solution.py:21
  66.4 7.8 %collective-permute-start.22 = (f32[4,1,4,1536]{3,2,1,0:T(4,128)S(1)}, f32[4,1,4,1536]{3,2,1,0:T(4,128)S(1)}, u32[]{:S(2)}, u32[]{:S(2)}) collective-permute-start(f32[4,1,4,1536]{3,2,1,0:T(4,128)S(1)} %shard_map.171.first_ref), channel_id=1, source_target_pairs={{0,1},{1,0},{2,3},{3,2},{4,5},{5,4},{6,7},{7,6},{8,9},{9,8},{10,11... | collective-permute-start | bytes 294920 | tf_op jit(solution)/shard_map/ppermute | solution.py:21

commit v5 on v4

--- a/solution.py
+++ b/solution.py
@@ -23,13 +23,6 @@
 
 def after(x, *others):
     return lax.optimization_barrier((x, *others))[0]
-
-
-def swap_two(x, n_enc, k, n_col, j):
-    moves = [
-        (e * n_col + c, (e ^ k) * n_col + (c ^ j)) for e in range(n_enc) for c in range(n_col)
-    ]
-    return lax.ppermute(x, ("enc", "col"), moves)
 
 
 def kernel_call(body, out_shape, cost=(0, 0, 0), vmem=VMEM_LIMIT, **kw):
@@ -77,27 +70,16 @@
     return kernel_call(body, jax.ShapeDtypeStruct((parts, rows, piece), x.dtype))(x)
 
 
-def join_rows(pieces, others, axis):
+def join_rows(pieces, axis):
     rows, width = pieces[0].shape
     parts = len(pieces)
-    n = parts + len(others)
 
     def body(*refs):
         for k in range(parts):
-            start = (lax.axis_index(axis) ^ k) * rows
-            here = pl.ds(pl.multiple_of(start, math.gcd(rows, 32)), rows)
-            refs[n][here, :] = refs[k][...]
-            refs[n + 1][0, here, :] = refs[k][...]
-        for i, ref in enumerate(refs[parts:n]):
-            refs[n + 1][i + 1] = ref[...]
-
-    return kernel_call(
-        body,
-        [
-            jax.ShapeDtypeStruct((rows * parts, width), pieces[0].dtype),
-            jax.ShapeDtypeStruct((1 + len(others), rows * parts, width), pieces[0].dtype),
-        ],
-    )(*pieces, *others)
+            start = (lax.axis_index(axis) ^ k) * rows if parts > 1 else 0
+            refs[parts][pl.ds(pl.multiple_of(start, math.gcd(rows, 32)), rows), :] = refs[k][...]
+
+    return kernel_call(body, jax.ShapeDtypeStruct((rows * parts, width), pieces[0].dtype))(*pieces)
 
 
 def join_columns(pieces, axis):
@@ -107,7 +89,7 @@
     def body(*refs):
         copies = [
             pltpu.make_async_copy(
-                refs[k], refs[parts].at[:, columns_of(axis, k, piece)], refs[parts + 1].at[k]
+                refs[parts - 1 - k], refs[parts].at[:, columns_of(axis, k, piece)], refs[parts + 1].at[k]
             )
             for k in range(parts)
         ]
@@ -122,7 +104,7 @@
         in_specs=[pl.BlockSpec(memory_space=pl.ANY)] * parts,
         out_specs=pl.BlockSpec(memory_space=pl.ANY),
         scratch_shapes=[pltpu.SemaphoreType.DMA((parts,))],
-    )(*pieces)
+    )(*pieces[::-1])
 
 
 def split_sum(x, y, parts):
@@ -409,16 +391,16 @@
     query_here = normed_turned(
         after(queries, values_here), 0, totals, query_gain, cosine, sine, full_width, "col", parts, True
     )
-    key_pieces = [key_pieces[0], *(after(x, values_here, sent, *query_here) for x in key_pieces[1:])]
-    keys_here, bundle = join_rows(key_pieces, all_values, "col")
+    key_pieces = [
+        key_pieces[0], *(after(x, all_values[-1], sent, *query_here) for x in key_pieces[1:])
+    ]
+    keys_here = join_rows(key_pieces, "col")
     got = keys_here
     if parts > 1:
         keys_there = swap(keys_here, "row", n_row, row_bits[0])
         query_here = [swap(x, "col", n_col, k) if k else x for k, x in enumerate(query_here)]
-        across = swap(bundle, "row", n_row, row_bits[1])
-        all_values += [(across, 1), (across, 2)]
-        all_keys = [keys_here, keys_there, (across, 0)]
-        got = across
+        all_values += [swap(x, "row", n_row, row_bits[1]) for x in all_values]
+        all_keys = [keys_here, keys_there, swap(keys_here, "row", n_row, row_bits[1])]
     else:
         all_keys = [lax.all_gather(keys_here, ("row", "col"), axis=0, tiled=True)]
         all_values = [lax.all_gather(values_here, ("row", "col"), axis=0, tiled=True)]
@@ -429,7 +411,7 @@
         else:
             grad = split_sum(grad, swap(after(sent, got), "row", n_row, 1 << i), 1)[0]
     if parts > 1:
-        keys_there = after(keys_there, grad, across, *query_here)
+        keys_there = after(keys_there, grad, *query_here)
         all_keys += [swap(keys_there, "row", n_row, row_bits[1])]
 
     mixed = [None] * parts

time: 75.2 us -> 74.5 us (level)
  waiting for transfers between devices: 27.3 us -> 25.2 us
  local copies, waits for them, and re-layouts: 1.44 us -> 2.99 us
    ppermute x23 -> x25, waiting for transfers between devices: 27.1 us -> 23.4 us  [swap(): return lax.ppermute(x, axis, [(i, i ^ k) for i in range(size)])]
    all_to_all x1, waiting for transfers between devices: 0.19 us -> 1.79 us  [relay(): return lax.all_to_all(x, 'col', split_axis=0, concat_axis=0, tiled=True)]
    unnamed x26, local copies, waits for them, and re-layouts: 1.16 us -> 2.7 us
    ppermute x23 -> x25, starting transfers between devices: 24.3 us -> 24 us  [swap(): return lax.ppermute(x, axis, [(i, i ^ k) for i in range(size)])]
  transfers between devices with their start and end apart: 24 -> 26, of which waited for: 11 -> 12; matrix products, arithmetic and copies ran while one was open for 1% -> 1% of each run, Pallas kernels for 16% -> 17%
where the time goes in v5:
time: 74.5 us; the launch traced here: 74.2 us
  starting transfers between devices  30.5 us (41%)
  waiting for transfers between devices  25.2 us (34%)
  Pallas kernels  14.2 us (19%)
  local copies, waits for them, and re-layouts  2.99 us (4%)
  between operations  0.85 us (1%)
    ppermute x25, starting transfers between devices, swap(): return lax.ppermute(x, axis, [(i, i ^ k) for i in range(size)])  24 us
    ppermute x25, waiting for transfers between devices, swap(): return lax.ppermute(x, axis, [(i, i ^ k) for i in range(size)])  23.4 us
    pallas_call x4, Pallas kernels, attention(): kernel_call(body, jax.ShapeDtypeStruct((rows, width), jnp.bfloat16))  7.99 us
    all_to_all x1, starting transfers between devices, relay(): return lax.all_to_all(x, 'col', split_axis=0, concat_axis=0, tiled=True)  6.45 us
    unnamed x26, local copies, waits for them, and re-layouts  2.7 us
    pallas_call x1, Pallas kernels, image_attention(): kernel_call(body, [jax.ShapeDtypeStruct((rows, width), jnp.bfloat16), *[j...  1.92 us
    all_to_all x1, waiting for transfers between devices, relay(): return lax.all_to_all(x, 'col', split_axis=0, concat_axis=0, tiled=True)  1.79 us
  transfers between devices with their start and end apart: 26, of which 12 were waited for; matrix products, arithmetic and copies ran while one was open for 1% of the time, Pallas kernels for 17%

profile of v5, /device:TPU:0, one launch (start us, length us, event | category | flops | bytes accessed | tf_op | source)
XLA Modules:
  0.0 74.2 jit_solution(12714140119015202121)
XLA Ops:
  0.6 1.0 %copy-done.2 = bf16[160,1536]{1,0:T(8,128)(2,1)S(1)} copy-done((bf16[160,1536]{1,0:T(8,128)(2,1)S(1)}, bf16[160,1536]{1,0:T(8,128)(2,1)}, u32[]{:S(2)}) %copy-start.2) | copy-done | bytes 491544
  1.7 0.8 %shard_map.156 = bf16[4,160,384]{2,1,0:T(8,128)(2,1)} custom-call(bf16[160,1536]{1,0:T(8,128)(2,1)S(1)} %copy-done.2), custom_call_target="tpu_custom_call" | custom-call | tf_op jit(solution)/shard_map/pallas_call | solution.py:70
  2.5 6.4 %all-to-all-start = ((bf16[4,160,384]{2,1,0:T(8,128)(2,1)}), bf16[4,160,384]{2,1,0:T(8,128)(2,1)S(1)}, u32[]{:S(2)}, u32[]{:S(2)}) async-start(bf16[4,160,384]{2,1,0:T(8,128)(2,1)} %shard_map.156), calls=%async_computation | async-start | bytes 983040 | tf_op jit(solution)/shard_map/all_to_all | solution.py:354
  9.0 0.1 shard_map.157
  9.1 1.6 %collective-permute-start.1 = (bf16[2,4,1536]{2,1,0:T(4,128)(2,1)S(1)}, bf16[2,4,1536]{2,1,0:T(4,128)(2,1)S(1)}, u32[]{:S(2)}, u32[]{:S(2)}) collective-permute-start(bf16[2,4,1536]{2,1,0:T(4,128)(2,1)S(1)} %get-tuple-element.41), channel_id=1, source_target_pairs={{0,16},{16,0},{1,17},{17,1},{2,18},{18,2},{3,19},{19,3},{4,20},{20... | collective-permute-start | bytes 73736 | tf_op jit(solution)/shard_map/ppermute | solution.py:21
  10.6 0.3 shard_map.158.refs_0_
  10.9 0.6 collective-permute-start
  11.7 0.1 mul.20
  11.8 1.3 %collective-permute-done.1 = bf16[2,4,1536]{2,1,0:T(4,128)(2,1)S(1)} collective-permute-done((bf16[2,4,1536]{2,1,0:T(4,128)(2,1)S(1)}, bf16[2,4,1536]{2,1,0:T(4,128)(2,1)S(1)}, u32[]{:S(2)}, u32[]{:S(2)}) %collective-permute-start.1) | collective-permute-done | bytes 24608 | tf_op jit(solution)/shard_map/ppermute | solution.py:21
  13.2 1.6 %collective-permute-start.3 = (bf16[2,8,1536]{2,1,0:T(8,128)(2,1)S(1)}, bf16[2,8,1536]{2,1,0:T(8,128)(2,1)S(1)}, u32[]{:S(2)}, u32[]{:S(2)}) collective-permute-start(bf16[2,8,1536]{2,1,0:T(8,128)(2,1)S(1)} %pad_maximum_fusion), channel_id=1, source_target_pairs={{0,4},{4,0},{8,12},{12,8},{1,5},{5,1},{9,13},{13,9},{2,6},{6,2},{1... | collective-permute-start | bytes 147464 | tf_op jit(solution)/shard_map/ppermute | solution.py:21
  14.9 0.5 collective-permute-start.2
  15.4 0.6 copy-done.10
  16.1 0.4 sine_multiply_fusion
  16.5 0.3 copy-done.7
  16.8 0.7 copy-done.8
  17.5 0.7 shard_map.159
  18.2 0.8 %collective-permute-done.2 = bf16[2,8,1536]{2,1,0:T(8,128)(2,1)S(1)} collective-permute-done((bf16[2,8,1536]{2,1,0:T(8,128)(2,1)S(1)}, bf16[2,8,1536]{2,1,0:T(8,128)(2,1)S(1)}, u32[]{:S(2)}, u32[]{:S(2)}) %collective-permute-start.2) | collective-permute-done | bytes 49184 | tf_op jit(solution)/shard_map/ppermute | solution.py:21
  19.0 1.9 %shard_map.160 = (bf16[160,1536]{1,0:T(8,128)(2,1)}, f32[2,4,4,1536]{3,2,1,0:T(4,128)S(1)}, f32[2,4,4,1536]{3,2,1,0:T(4,128)S(1)}) custom-call(f32[160,2]{1,0:T(8,128)S(1)} %shard_map.158.refs_0_, f32[160,2]{1,0:T(8,128)S(1)} %collective-permute-done.refs_1_, bf16[160,1536]{1,0:T(8,128)(2,1)S(1)} %copy-done, f32[1,1536]{1,0:T(1,128)S(1)} %broadcast_in_dim.54.refs_3_, ...), custom_call_target="tpu_custom_call" | custom-call | flops 1000 | bytes 1000 | tf_op jit(solution)/shard_map/pallas_call | solution.py:321
  20.9 1.8 %all-to-all-done = bf16[4,160,384]{2,1,0:T(8,128)(2,1)S(1)} async-done(((bf16[4,160,384]{2,1,0:T(8,128)(2,1)}), bf16[4,160,384]{2,1,0:T(8,128)(2,1)S(1)}, u32[]{:S(2)}, u32[]{:S(2)}) %all-to-all-start) | async-done | bytes 491552 | tf_op jit(solution)/shard_map/all_to_all | solution.py:354
  22.7 1.5 %collective-permute-start.7 = (bf16[640,384]{1,0:T(8,128)(2,1)S(1)}, bf16[640,384]{1,0:T(8,128)(2,1)S(1)}, u32[]{:S(2)}, u32[]{:S(2)}) collective-permute-start(bf16[640,384]{1,0:T(8,128)(2,1)S(1)} %bitcast.5), channel_id=1, source_target_pairs={{0,8},{4,12},{8,0},{12,4},{1,9},{5,13},{9,1},{13,5},{2,10},{6,14},... | collective-permute-start | bytes 1474568 | tf_op jit(solution)/shard_map/ppermute | solution.py:21
  24.3 1.5 %collective-permute-start.8 = (f32[2,4,4,1536]{3,2,1,0:T(4,128)S(1)}, f32[2,4,4,1536]{3,2,1,0:T(4,128)S(1)}, u32[]{:S(2)}, u32[]{:S(2)}) collective-permute-start(f32[2,4,4,1536]{3,2,1,0:T(4,128)S(1)} %get-tuple-element.52), channel_id=1, source_target_pairs={{0,16},{16,0},{1,17},{17,1},{2,18},{18,2},{3,19},{19,3},{4,20},{20... | collective-permute-start | bytes 589832 | tf_op jit(solution)/shard_map/ppermute | solution.py:21
  25.7 1.5 %collective-permute-start.10 = (bf16[160,384]{1,0:T(8,128)(2,1)S(1)}, bf16[160,384]{1,0:T(8,128)(2,1)S(1)}, u32[]{:S(2)}, u32[]{:S(2)}) collective-permute-start(bf16[160,384]{1,0:T(8,128)(2,1)S(1)} %get-tuple-element.60), channel_id=1, source_target_pairs={{0,3},{1,2},{2,1},{3,0},{4,7},{5,6},{6,5},{7,4},{8,11},{9,10},{10,... | collective-permute-start | bytes 368648 | tf_op jit(solution)/shard_map/ppermute | solution.py:21
  27.2 2.9 %collective-permute-start.6 = (bf16[160,384]{1,0:T(8,128)(2,1)S(1)}, bf16[160,384]{1,0:T(8,128)(2,1)S(1)}, u32[]{:S(2)}, u32[]{:S(2)}) collective-permute-start(bf16[160,384]{1,0:T(8,128)(2,1)S(1)} %get-tuple-element.51), channel_id=1, source_target_pairs={{0,1},{1,0},{2,3},{3,2},{4,5},{5,4},{6,7},{7,6},{8,9},{9,8},{10,11... | collective-permute-start | bytes 368648 | tf_op jit(solution)/shard_map/ppermute | solution.py:21
  30.2 0.7 shard_map.161
  30.8 3.0 %collective-permute-done.10.refs_3_ = bf16[160,384]{1,0:T(8,128)(2,1)S(1)} collective-permute-done((bf16[160,384]{1,0:T(8,128)(2,1)S(1)}, bf16[160,384]{1,0:T(8,128)(2,1)S(1)}, u32[]{:S(2)}, u32[]{:S(2)}) %collective-permute-start.10) | collective-permute-done | bytes 122912 | tf_op jit(solution)/shard_map/ppermute | solution.py:21
  33.8 1.1 %collective-permute-done.7.refs_5_ = bf16[640,384]{1,0:T(8,128)(2,1)S(1)} collective-permute-done((bf16[640,384]{1,0:T(8,128)(2,1)S(1)}, bf16[640,384]{1,0:T(8,128)(2,1)S(1)}, u32[]{:S(2)}, u32[]{:S(2)}) %collective-permute-start.7) | collective-permute-done | bytes 491552 | tf_op jit(solution)/shard_map/ppermute | solution.py:21
  34.9 2.6 %collective-permute-done.9.refs_2_ = bf16[160,384]{1,0:T(8,128)(2,1)S(1)} collective-permute-done((bf16[160,384]{1,0:T(8,128)(2,1)S(1)}, bf16[160,384]{1,0:T(8,128)(2,1)S(1)}, u32[]{:S(2)}, u32[]{:S(2)}) %collective-permute-start.9) | collective-permute-done | bytes 122912 | tf_op jit(solution)/shard_map/ppermute | solution.py:21
  37.6 0.9 %collective-permute-start.11 = (bf16[640,384]{1,0:T(8,128)(2,1)S(1)}, bf16[640,384]{1,0:T(8,128)(2,1)S(1)}, u32[]{:S(2)}, u32[]{:S(2)}) collective-permute-start(bf16[640,384]{1,0:T(8,128)(2,1)S(1)} %shard_map.163.refs_0_), channel_id=1, source_target_pairs={{0,8},{4,12},{8,0},{12,4},{1,9},{5,13},{9,1},{13,5},{2,10},{6,14},... | collective-permute-start | bytes 1474568 | tf_op jit(solution)/shard_map/ppermute | solution.py:21
  38.5 2.0 %collective-permute-start.5 = (bf16[160,384]{1,0:T(8,128)(2,1)S(1)}, bf16[160,384]{1,0:T(8,128)(2,1)S(1)}, u32[]{:S(2)}, u32[]{:S(2)}) collective-permute-start(bf16[160,384]{1,0:T(8,128)(2,1)S(1)} %get-tuple-element.50), channel_id=1, source_target_pairs={{0,3},{1,2},{2,1},{3,0},{4,7},{5,6},{6,5},{7,4},{8,11},{9,10},{10,... | collective-permute-start | bytes 368648 | tf_op jit(solution)/shard_map/ppermute | solution.py:21
  40.5 2.4 %collective-permute-start.16 = (bf16[160,384]{1,0:T(8,128)(2,1)S(1)}, bf16[160,384]{1,0:T(8,128)(2,1)S(1)}, u32[]{:S(2)}, u32[]{:S(2)}) collective-permute-start(bf16[160,384]{1,0:T(8,128)(2,1)S(1)} %get-tuple-element.56), channel_id=1, source_target_pairs={{0,2},{1,3},{2,0},{3,1},{4,6},{5,7},{6,4},{7,5},{8,10},{9,11},{10,... | collective-permute-start | bytes 368648 | tf_op jit(solution)/shard_map/ppermute | solution.py:21
  42.9 1.3 %collective-permute-start.14 = (f32[4,1,4,1536]{3,2,1,0:T(4,128)S(1)}, f32[4,1,4,1536]{3,2,1,0:T(4,128)S(1)}, u32[]{:S(2)}, u32[]{:S(2)}) collective-permute-start(f32[4,1,4,1536]{3,2,1,0:T(4,128)S(1)} %get-tuple-element.65), channel_id=1, source_target_pairs={{0,8},{4,12},{8,0},{12,4},{1,9},{5,13},{9,1},{13,5},{2,10},{6,14},... | collective-permute-start | bytes 294920 | tf_op jit(solution)/shard_map/ppermute | solution.py:21
  44.2 8.0 %collective-permute-done.14.y_ref = f32[4,1,4,1536]{3,2,1,0:T(4,128)S(1)} collective-permute-done((f32[4,1,4,1536]{3,2,1,0:T(4,128)S(1)}, f32[4,1,4,1536]{3,2,1,0:T(4,128)S(1)}, u32[]{:S(2)}, u32[]{:S(2)}) %collective-permute-start.14) | collective-permute-done | bytes 98336 | tf_op jit(solution)/shard_map/ppermute | solution.py:21
  52.2 0.6 collective-permute-start.12
  52.8 0.4 collective-permute-start.17
  53.3 0.7 collective-permute-done.18.refs_6_
  54.0 0.7 collective-permute-done.12.refs_2_
  54.7 0.7 collective-permute-done.19.refs_7_
  55.4 0.7 collective-permute-done.17.refs_3_
  56.1 2.0 %shard_map.167 = bf16[160,384]{1,0:T(8,128)(2,1)S(1)} custom-call(bf16[160,384]{1,0:T(8,128)(2,1)S(1)} %collective-permute-done.16.q_ref, bf16[640,384]{1,0:T(8,128)(2,1)S(1)} %shard_map.163.refs_0_, bf16[640,384]{1,0:T(8,128)(2,1)S(1)} %collective-permute-done.11.refs_1_, bf16[640,384]{1,0:T(8,128)(2,1)S(1)} %collective-permute-done.12.refs_2_, ...), custom_call_target="tpu_custom_call" | custom-call | tf_op jit(solution)/shard_map/pallas_call | solution.py:279
  58.1 0.2 collective-permute-start.21
  58.3 2.0 %shard_map.168 = bf16[160,384]{1,0:T(8,128)(2,1)S(1)} custom-call(bf16[160,384]{1,0:T(8,128)(2,1)S(1)} %collective-permute-done.15.q_ref, bf16[640,384]{1,0:T(8,128)(2,1)S(1)} %shard_map.163.refs_0_, bf16[640,384]{1,0:T(8,128)(2,1)S(1)} %collective-permute-done.11.refs_1_, bf16[640,384]{1,0:T(8,128)(2,1)S(1)} %collective-permute-done.12.refs_2_, ...), custom_call_target="tpu_custom_call" | custom-call | tf_op jit(solution)/shard_map/pallas_call | solution.py:279
  60.3 2.5 %collective-permute-start.22 = (bf16[160,384]{1,0:T(8,128)(2,1)S(1)}, bf16[160,384]{1,0:T(8,128)(2,1)S(1)}, u32[]{:S(2)}, u32[]{:S(2)}) collective-permute-start(bf16[160,384]{1,0:T(8,128)(2,1)S(1)} %shard_map.168), channel_id=1, source_target_pairs={{0,1},{1,0},{2,3},{3,2},{4,5},{5,4},{6,7},{7,6},{8,9},{9,8},{10,11... | collective-permute-start | bytes 368648 | tf_op jit(solution)/shard_map/ppermute | solution.py:21
  62.8 2.0 %shard_map.166 = bf16[160,384]{1,0:T(8,128)(2,1)S(1)} custom-call(bf16[160,384]{1,0:T(8,128)(2,1)S(1)} %collective-permute-done.5.q_ref, bf16[640,384]{1,0:T(8,128)(2,1)S(1)} %shard_map.163.refs_0_, bf16[640,384]{1,0:T(8,128)(2,1)S(1)} %collective-permute-done.11.refs_1_, bf16[640,384]{1,0:T(8,128)(2,1)S(1)} %collective-permute-done.12.refs_2_, ...), custom_call_target="tpu_custom_call" | custom-call | tf_op jit(solution)/shard_map/pallas_call | solution.py:279
  64.7 1.9 %collective-permute-start.20 = (bf16[160,384]{1,0:T(8,128)(2,1)S(1)}, bf16[160,384]{1,0:T(8,128)(2,1)S(1)}, u32[]{:S(2)}, u32[]{:S(2)}) collective-permute-start(bf16[160,384]{1,0:T(8,128)(2,1)S(1)} %shard_map.166), channel_id=1, source_target_pairs={{0,3},{1,2},{2,1},{3,0},{4,7},{5,6},{6,5},{7,4},{8,11},{9,10},{10,... | collective-permute-start | bytes 368648 | tf_op jit(solution)/shard_map/ppermute | solution.py:21
  66.8 2.0 %shard_map.169.refs_3_ = bf16[160,384]{1,0:T(8,128)(2,1)S(1)} custom-call(bf16[160,384]{1,0:T(8,128)(2,1)S(1)} %get-tuple-element.54.q_ref, bf16[640,384]{1,0:T(8,128)(2,1)S(1)} %shard_map.163.refs_0_, bf16[640,384]{1,0:T(8,128)(2,1)S(1)} %collective-permute-done.11.refs_1_, bf16[640,384]{1,0:T(8,128)(2,1)S(1)} %collective-permute-done.12.refs_2_, ...), custom_call_target="tpu_custom_call" | custom-call | tf_op jit(solution)/shard_map/pallas_call | solution.py:279
  68.8 3.7 %collective-permute-done.20.refs_0_ = bf16[160,384]{1,0:T(8,128)(2,1)S(1)} collective-permute-done((bf16[160,384]{1,0:T(8,128)(2,1)S(1)}, bf16[160,384]{1,0:T(8,128)(2,1)S(1)}, u32[]{:S(2)}, u32[]{:S(2)}) %collective-permute-start.20) | collective-permute-done | bytes 122912 | tf_op jit(solution)/shard_map/ppermute | solution.py:21
  72.6 0.8 %shard_map.170 = bf16[160,1536]{1,0:T(8,128)(2,1)} custom-call(bf16[160,384]{1,0:T(8,128)(2,1)S(1)} %collective-permute-done.20.refs_0_, bf16[160,384]{1,0:T(8,128)(2,1)S(1)} %collective-permute-done.21.refs_1_, bf16[160,384]{1,0:T(8,128)(2,1)S(1)} %collective-permute-done.22.refs_2_, bf16[160,384]{1,0:T(8,128)(2,1)S(1)} %shard_map.169.refs_3_), custom_call_target="tpu_custom_call" | custom-call | tf_op jit(solution)/shard_map/pallas_call | solution.py:101
  73.4 0.8 %shard_map.172 = (f32[4,3072]{1,0:T(4,128)}, f32[4,3072]{1,0:T(4,128)}) custom-call(bf16[4,3072]{1,0:T(4,128)(2,1)S(1)} %copy-done.4, f32[1,3072]{1,0:T(1,128)S(1)} %bitcast.12, f32[4,1,4,1536]{3,2,1,0:T(4,128)S(1)} %shard_map.171.first_ref, f32[4,1,4,1536]{3,2,1,0:T(4,128)S(1)} %collective-permute-done.24.second_ref), custom_call_target="tpu_custom_call" | custom-call | tf_op jit(solution)/shard_map/pallas_call | solution.py:170
  (59 shorter events, 0.8 us)
Async XLA Ops:
  0.6 1.0 %copy-start.2 = (bf16[160,1536]{1,0:T(8,128)(2,1)S(1)}, bf16[160,1536]{1,0:T(8,128)(2,1)}, u32[]{:S(2)}) copy-start(bf16[160,1536]{1,0:T(8,128)(2,1)} %x_ref.1) | copy-start | bytes 1474564
  1.7 7.3 %copy-start.4 = (bf16[4,3072]{1,0:T(4,128)(2,1)S(1)}, bf16[4,3072]{1,0:T(4,128)(2,1)}, u32[]{:S(2)}) copy-start(bf16[4,3072]{1,0:T(4,128)(2,1)} %k_ref.4) | copy-start | bytes 73732
  1.7 7.3 %copy-start.5 = (f32[3072]{0:T(1024)S(1)}, f32[3072]{0:T(1024)}, u32[]{:S(2)}) copy-start(f32[3072]{0:T(1024)} %param.21) | copy-start | bytes 36868
  1.7 7.3 %copy-start.6 = (bf16[4,3072]{1,0:T(4,128)(2,1)S(1)}, bf16[4,3072]{1,0:T(4,128)(2,1)}, u32[]{:S(2)}) copy-start(bf16[4,3072]{1,0:T(4,128)(2,1)} %v_ref.1) | copy-start | bytes 73732
  2.5 8.2 %copy-start = (bf16[160,1536]{1,0:T(8,128)(2,1)S(1)}, bf16[160,1536]{1,0:T(8,128)(2,1)}, u32[]{:S(2)}) copy-start(bf16[160,1536]{1,0:T(8,128)(2,1)} %refs_2_.4) | copy-start | bytes 1474564
  2.5 8.2 %copy-start.1 = (bf16[160,1536]{1,0:T(8,128)(2,1)S(1)}, bf16[160,1536]{1,0:T(8,128)(2,1)}, u32[]{:S(2)}) copy-start(bf16[160,1536]{1,0:T(8,128)(2,1)} %refs_2_.2) | copy-start | bytes 1474564
  2.5 20.2 %all-to-all-start = ((bf16[4,160,384]{2,1,0:T(8,128)(2,1)}), bf16[4,160,384]{2,1,0:T(8,128)(2,1)S(1)}, u32[]{:S(2)}, u32[]{:S(2)}) async-start(bf16[4,160,384]{2,1,0:T(8,128)(2,1)} %shard_map.156), calls=%async_computation | async-start | bytes 983040 | tf_op jit(solution)/shard_map/all_to_all | solution.py:354
  9.1 4.0 %collective-permute-start.1 = (bf16[2,4,1536]{2,1,0:T(4,128)(2,1)S(1)}, bf16[2,4,1536]{2,1,0:T(4,128)(2,1)S(1)}, u32[]{:S(2)}, u32[]{:S(2)}) collective-permute-start(bf16[2,4,1536]{2,1,0:T(4,128)(2,1)S(1)} %get-tuple-element.41), channel_id=1, source_target_pairs={{0,16},{16,0},{1,17},{17,1},{2,18},{18,2},{3,19},{19,3},{4,20},{20... | collective-permute-start | bytes 73736 | tf_op jit(solution)/shard_map/ppermute | solution.py:21
  10.6 0.9 %copy-start.9 = (s32[160,3]{0,1:T(4,128)S(1)}, s32[160,3]{0,1:T(4,128)}, u32[]{:S(2)}) copy-start(s32[160,3]{0,1:T(4,128)} %param.16) | copy-start | bytes 5764
  10.9 6.5 %collective-permute-start = (f32[160,2]{1,0:T(8,128)S(1)}, f32[160,2]{1,0:T(8,128)S(1)}, u32[]{:S(2)}, u32[]{:S(2)}) collective-permute-start(f32[160,2]{1,0:T(8,128)S(1)} %shard_map.158.refs_0_), channel_id=1, source_target_pairs={{0,16},{16,0},{1,17},{17,1},{2,18},{18,2},{3,19},{19,3},{4,20},{20... | collective-permute-start | bytes 3848 | tf_op jit(solution)/shard_map/ppermute | solution.py:21
  13.2 5.0 %collective-permute-start.4 = (bf16[2,8,1536]{2,1,0:T(8,128)(2,1)S(1)}, bf16[2,8,1536]{2,1,0:T(8,128)(2,1)S(1)}, u32[]{:S(2)}, u32[]{:S(2)}) collective-permute-start(bf16[2,8,1536]{2,1,0:T(8,128)(2,1)S(1)} %pad_maximum_fusion), channel_id=1, source_target_pairs={{0,12},{4,8},{8,4},{12,0},{1,13},{5,9},{9,5},{13,1},{2,14},{6,10},... | collective-permute-start | bytes 147464 | tf_op jit(solution)/shard_map/ppermute | solution.py:21
  13.2 4.9 %collective-permute-start.3 = (bf16[2,8,1536]{2,1,0:T(8,128)(2,1)S(1)}, bf16[2,8,1536]{2,1,0:T(8,128)(2,1)S(1)}, u32[]{:S(2)}, u32[]{:S(2)}) collective-permute-start(bf16[2,8,1536]{2,1,0:T(8,128)(2,1)S(1)} %pad_maximum_fusion), channel_id=1, source_target_pairs={{0,4},{4,0},{8,12},{12,8},{1,5},{5,1},{9,13},{13,9},{2,6},{6,2},{1... | collective-permute-start | bytes 147464 | tf_op jit(solution)/shard_map/ppermute | solution.py:21
  14.9 4.1 %collective-permute-start.2 = (bf16[2,8,1536]{2,1,0:T(8,128)(2,1)S(1)}, bf16[2,8,1536]{2,1,0:T(8,128)(2,1)S(1)}, u32[]{:S(2)}, u32[]{:S(2)}) collective-permute-start(bf16[2,8,1536]{2,1,0:T(8,128)(2,1)S(1)} %pad_maximum_fusion), channel_id=1, source_target_pairs={{0,8},{4,12},{8,0},{12,4},{1,9},{5,13},{9,1},{13,5},{2,10},{6,14},... | collective-permute-start | bytes 147464 | tf_op jit(solution)/shard_map/ppermute | solution.py:21
  15.4 0.7 copy-start.10
  15.4 0.7 copy-start.11
  15.4 0.7 copy-start.12
  16.1 0.7 copy-start.7
  16.8 0.7 copy-start.8
  17.5 1.5 %copy-start.3 = (bf16[160,1536]{1,0:T(8,128)(2,1)S(1)}, bf16[160,1536]{1,0:T(8,128)(2,1)}, u32[]{:S(2)}) copy-start(bf16[160,1536]{1,0:T(8,128)(2,1)} %refs_5_.1) | copy-start | bytes 1474564
  22.7 12.2 %collective-permute-start.7 = (bf16[640,384]{1,0:T(8,128)(2,1)S(1)}, bf16[640,384]{1,0:T(8,128)(2,1)S(1)}, u32[]{:S(2)}, u32[]{:S(2)}) collective-permute-start(bf16[640,384]{1,0:T(8,128)(2,1)S(1)} %bitcast.5), channel_id=1, source_target_pairs={{0,8},{4,12},{8,0},{12,4},{1,9},{5,13},{9,1},{13,5},{2,10},{6,14},... | collective-permute-start | bytes 1474568 | tf_op jit(solution)/shard_map/ppermute | solution.py:21
  24.3 5.9 %collective-permute-start.8 = (f32[2,4,4,1536]{3,2,1,0:T(4,128)S(1)}, f32[2,4,4,1536]{3,2,1,0:T(4,128)S(1)}, u32[]{:S(2)}, u32[]{:S(2)}) collective-permute-start(f32[2,4,4,1536]{3,2,1,0:T(4,128)S(1)} %get-tuple-element.52), channel_id=1, source_target_pairs={{0,16},{16,0},{1,17},{17,1},{2,18},{18,2},{3,19},{19,3},{4,20},{20... | collective-permute-start | bytes 589832 | tf_op jit(solution)/shard_map/ppermute | solution.py:21
  25.7 8.1 %collective-permute-start.10 = (bf16[160,384]{1,0:T(8,128)(2,1)S(1)}, bf16[160,384]{1,0:T(8,128)(2,1)S(1)}, u32[]{:S(2)}, u32[]{:S(2)}) collective-permute-start(bf16[160,384]{1,0:T(8,128)(2,1)S(1)} %get-tuple-element.60), channel_id=1, source_target_pairs={{0,3},{1,2},{2,1},{3,0},{4,7},{5,6},{6,5},{7,4},{8,11},{9,10},{10,... | collective-permute-start | bytes 368648 | tf_op jit(solution)/shard_map/ppermute | solution.py:21
  27.2 10.3 %collective-permute-start.9 = (bf16[160,384]{1,0:T(8,128)(2,1)S(1)}, bf16[160,384]{1,0:T(8,128)(2,1)S(1)}, u32[]{:S(2)}, u32[]{:S(2)}) collective-permute-start(bf16[160,384]{1,0:T(8,128)(2,1)S(1)} %get-tuple-element.58), channel_id=1, source_target_pairs={{0,2},{1,3},{2,0},{3,1},{4,6},{5,7},{6,4},{7,5},{8,10},{9,11},{10,... | collective-permute-start | bytes 368648 | tf_op jit(solution)/shard_map/ppermute | solution.py:21
  27.2 10.3 %collective-permute-start.6 = (bf16[160,384]{1,0:T(8,128)(2,1)S(1)}, bf16[160,384]{1,0:T(8,128)(2,1)S(1)}, u32[]{:S(2)}, u32[]{:S(2)}) collective-permute-start(bf16[160,384]{1,0:T(8,128)(2,1)S(1)} %get-tuple-element.51), channel_id=1, source_target_pairs={{0,1},{1,0},{2,3},{3,2},{4,5},{5,4},{6,7},{7,6},{8,9},{9,8},{10,11... | collective-permute-start | bytes 368648 | tf_op jit(solution)/shard_map/ppermute | solution.py:21
  37.6 15.2 %collective-permute-start.11 = (bf16[640,384]{1,0:T(8,128)(2,1)S(1)}, bf16[640,384]{1,0:T(8,128)(2,1)S(1)}, u32[]{:S(2)}, u32[]{:S(2)}) collective-permute-start(bf16[640,384]{1,0:T(8,128)(2,1)S(1)} %shard_map.163.refs_0_), channel_id=1, source_target_pairs={{0,8},{4,12},{8,0},{12,4},{1,9},{5,13},{9,1},{13,5},{2,10},{6,14},... | collective-permute-start | bytes 1474568 | tf_op jit(solution)/shard_map/ppermute | solution.py:21
  38.5 4.4 %collective-permute-start.13 = (f32[4,2,4,1536]{3,2,1,0:T(4,128)S(1)}, f32[4,2,4,1536]{3,2,1,0:T(4,128)S(1)}, u32[]{:S(2)}, u32[]{:S(2)}) collective-permute-start(f32[4,2,4,1536]{3,2,1,0:T(4,128)S(1)} %get-tuple-element.53), channel_id=1, source_target_pairs={{0,4},{4,0},{8,12},{12,8},{1,5},{5,1},{9,13},{13,9},{2,6},{6,2},{1... | collective-permute-start | bytes 589832 | tf_op jit(solution)/shard_map/ppermute | solution.py:21
  38.5 13.7 %collective-permute-start.5 = (bf16[160,384]{1,0:T(8,128)(2,1)S(1)}, bf16[160,384]{1,0:T(8,128)(2,1)S(1)}, u32[]{:S(2)}, u32[]{:S(2)}) collective-permute-start(bf16[160,384]{1,0:T(8,128)(2,1)S(1)} %get-tuple-element.50), channel_id=1, source_target_pairs={{0,3},{1,2},{2,1},{3,0},{4,7},{5,6},{6,5},{7,4},{8,11},{9,10},{10,... | collective-permute-start | bytes 368648 | tf_op jit(solution)/shard_map/ppermute | solution.py:21
  40.5 12.2 %collective-permute-start.15 = (bf16[160,384]{1,0:T(8,128)(2,1)S(1)}, bf16[160,384]{1,0:T(8,128)(2,1)S(1)}, u32[]{:S(2)}, u32[]{:S(2)}) collective-permute-start(bf16[160,384]{1,0:T(8,128)(2,1)S(1)} %get-tuple-element.55), channel_id=1, source_target_pairs={{0,1},{1,0},{2,3},{3,2},{4,5},{5,4},{6,7},{7,6},{8,9},{9,8},{10,11... | collective-permute-start | bytes 368648 | tf_op jit(solution)/shard_map/ppermute | solution.py:21
  40.5 12.3 %collective-permute-start.16 = (bf16[160,384]{1,0:T(8,128)(2,1)S(1)}, bf16[160,384]{1,0:T(8,128)(2,1)S(1)}, u32[]{:S(2)}, u32[]{:S(2)}) collective-permute-start(bf16[160,384]{1,0:T(8,128)(2,1)S(1)} %get-tuple-element.56), channel_id=1, source_target_pairs={{0,2},{1,3},{2,0},{3,1},{4,6},{5,7},{6,4},{7,5},{8,10},{9,11},{10,... | collective-permute-start | bytes 368648 | tf_op jit(solution)/shard_map/ppermute | solution.py:21
  42.9 9.2 %collective-permute-start.14 = (f32[4,1,4,1536]{3,2,1,0:T(4,128)S(1)}, f32[4,1,4,1536]{3,2,1,0:T(4,128)S(1)}, u32[]{:S(2)}, u32[]{:S(2)}) collective-permute-start(f32[4,1,4,1536]{3,2,1,0:T(4,128)S(1)} %get-tuple-element.65), channel_id=1, source_target_pairs={{0,8},{4,12},{8,0},{12,4},{1,9},{5,13},{9,1},{13,5},{2,10},{6,14},... | collective-permute-start | bytes 294920 | tf_op jit(solution)/shard_map/ppermute | solution.py:21
  52.1 1.9 %collective-permute-start.18 = (bf16[640,384]{1,0:T(8,128)(2,1)S(1)}, bf16[640,384]{1,0:T(8,128)(2,1)S(1)}, u32[]{:S(2)}, u32[]{:S(2)}) collective-permute-start(bf16[640,384]{1,0:T(8,128)(2,1)S(1)} %bitcast.6), channel_id=1, source_target_pairs={{0,4},{4,0},{8,12},{12,8},{1,5},{5,1},{9,13},{13,9},{2,6},{6,2},{1... | collective-permute-start | bytes 1474568 | tf_op jit(solution)/shard_map/ppermute | solution.py:21
  52.2 2.5 %collective-permute-start.12 = (bf16[640,384]{1,0:T(8,128)(2,1)S(1)}, bf16[640,384]{1,0:T(8,128)(2,1)S(1)}, u32[]{:S(2)}, u32[]{:S(2)}) collective-permute-start(bf16[640,384]{1,0:T(8,128)(2,1)S(1)} %shard_map.163.refs_0_), channel_id=1, source_target_pairs={{0,4},{4,0},{8,12},{12,8},{1,5},{5,1},{9,13},{13,9},{2,6},{6,2},{1... | collective-permute-start | bytes 1474568 | tf_op jit(solution)/shard_map/ppermute | solution.py:21
  52.7 2.7 %collective-permute-start.19 = (bf16[640,384]{1,0:T(8,128)(2,1)S(1)}, bf16[640,384]{1,0:T(8,128)(2,1)S(1)}, u32[]{:S(2)}, u32[]{:S(2)}) collective-permute-start(bf16[640,384]{1,0:T(8,128)(2,1)S(1)} %collective-permute-done.7.refs_5_), channel_id=1, source_target_pairs={{0,4},{4,0},{8,12},{12,8},{1,5},{5,1},{9,13},{13,9},{2,6},{6,2},{1... | collective-permute-start | bytes 1474568 | tf_op jit(solution)/shard_map/ppermute | solution.py:21
  52.8 3.3 %collective-permute-start.17 = (bf16[640,384]{1,0:T(8,128)(2,1)S(1)}, bf16[640,384]{1,0:T(8,128)(2,1)S(1)}, u32[]{:S(2)}, u32[]{:S(2)}) collective-permute-start(bf16[640,384]{1,0:T(8,128)(2,1)S(1)} %collective-permute-done.11.refs_1_), channel_id=1, source_target_pairs={{0,4},{4,0},{8,12},{12,8},{1,5},{5,1},{9,13},{13,9},{2,6},{6,2},{1... | collective-permute-start | bytes 1474568 | tf_op jit(solution)/shard_map/ppermute | solution.py:21
  53.3 13.4 %collective-permute-start.23 = (f32[4,1,4,1536]{3,2,1,0:T(4,128)S(1)}, f32[4,1,4,1536]{3,2,1,0:T(4,128)S(1)}, u32[]{:S(2)}, u32[]{:S(2)}) collective-permute-start(f32[4,1,4,1536]{3,2,1,0:T(4,128)S(1)} %shard_map.165.x_ref), channel_id=1, source_target_pairs={{0,2},{1,3},{2,0},{3,1},{4,6},{5,7},{6,4},{7,5},{8,10},{9,11},{10,... | collective-permute-start | bytes 294920 | tf_op jit(solution)/shard_map/ppermute | solution.py:21
  58.1 10.7 %collective-permute-start.21 = (bf16[160,384]{1,0:T(8,128)(2,1)S(1)}, bf16[160,384]{1,0:T(8,128)(2,1)S(1)}, u32[]{:S(2)}, u32[]{:S(2)}) collective-permute-start(bf16[160,384]{1,0:T(8,128)(2,1)S(1)} %shard_map.167), channel_id=1, source_target_pairs={{0,2},{1,3},{2,0},{3,1},{4,6},{5,7},{6,4},{7,5},{8,10},{9,11},{10,... | collective-permute-start | bytes 368648 | tf_op jit(solution)/shard_map/ppermute | solution.py:21
  60.3 8.5 %collective-permute-start.22 = (bf16[160,384]{1,0:T(8,128)(2,1)S(1)}, bf16[160,384]{1,0:T(8,128)(2,1)S(1)}, u32[]{:S(2)}, u32[]{:S(2)}) collective-permute-start(bf16[160,384]{1,0:T(8,128)(2,1)S(1)} %shard_map.168), channel_id=1, source_target_pairs={{0,1},{1,0},{2,3},{3,2},{4,5},{5,4},{6,7},{7,6},{8,9},{9,8},{10,11... | collective-permute-start | bytes 368648 | tf_op jit(solution)/shard_map/ppermute | solution.py:21
  64.7 7.8 %collective-permute-start.20 = (bf16[160,384]{1,0:T(8,128)(2,1)S(1)}, bf16[160,384]{1,0:T(8,128)(2,1)S(1)}, u32[]{:S(2)}, u32[]{:S(2)}) collective-permute-start(bf16[160,384]{1,0:T(8,128)(2,1)S(1)} %shard_map.166), channel_id=1, source_target_pairs={{0,3},{1,2},{2,1},{3,0},{4,7},{5,6},{6,5},{7,4},{8,11},{9,10},{10,... | collective-permute-start | bytes 368648 | tf_op jit(solution)/shard_map/ppermute | solution.py:21
  66.7 6.7 %collective-permute-start.24 = (f32[4,1,4,1536]{3,2,1,0:T(4,128)S(1)}, f32[4,1,4,1536]{3,2,1,0:T(4,128)S(1)}, u32[]{:S(2)}, u32[]{:S(2)}) collective-permute-start(f32[4,1,4,1536]{3,2,1,0:T(4,128)S(1)} %shard_map.171.first_ref), channel_id=1, source_target_pairs={{0,1},{1,0},{2,3},{3,2},{4,5},{5,4},{6,7},{7,6},{8,9},{9,8},{10,11... | collective-permute-start | bytes 294920 | tf_op jit(solution)/shard_map/ppermute | solution.py:21

commit v6 on v5

--- a/solution.py
+++ b/solution.py
@@ -77,9 +77,9 @@
     def body(*refs):
         for k in range(parts):
             start = (lax.axis_index(axis) ^ k) * rows if parts > 1 else 0
-            refs[parts][pl.ds(pl.multiple_of(start, math.gcd(rows, 32)), rows), :] = refs[k][...]
-
-    return kernel_call(body, jax.ShapeDtypeStruct((rows * parts, width), pieces[0].dtype))(*pieces)
+            refs[parts][pl.ds(pl.multiple_of(start, math.gcd(rows, 32)), rows), :] = refs[parts - 1 - k][...]
+
+    return kernel_call(body, jax.ShapeDtypeStruct((rows * parts, width), pieces[0].dtype))(*pieces[::-1])
 
 
 def join_columns(pieces, axis):
@@ -359,7 +359,7 @@
     own_count = context_keys.shape[0]
     context = context_shards(after(context_keys, value_split), context_values, context_gain, width, "enc", n_enc)
     context = [swap(x, "enc", n_enc, k) if k else x for k, x in enumerate(context)]
-    sums = square_sums(after(queries, context[0]), self_keys)
+    sums = square_sums(after(queries, value_split), self_keys)
     totals = [sums]
     bit = 1
     while bit < n_enc:
@@ -367,7 +367,7 @@
             totals = [totals[0] + totals[1]]
         totals = [totals[0], swap(totals[0], "enc", n_enc, bit)]
         bit *= 2
-    cosine, sine = rope_tables(after(positions, sums))
+    cosine, sine = rope_tables(after(positions, value_split))
     key_pieces = normed_turned(
         self_keys, 1, totals, key_gain, cosine, sine, full_width, "col", parts, True
     )
@@ -383,7 +383,7 @@
         queries, totals, query_gain, full_width, context, image_cotangent, own_count, n_enc
     )
 
-    values_here = after(values_here, grads[0]).reshape(parts * rows, width // parts)
+    values_here = after(values_here, context).reshape(parts * rows, width // parts)
     all_values = [values_here]
     if parts > 1:
         all_values += [swap(values_here, "row", n_row, row_bits[0])]
@@ -392,13 +392,14 @@
         after(queries, values_here), 0, totals, query_gain, cosine, sine, full_width, "col", parts, True
     )
     key_pieces = [
-        key_pieces[0], *(after(x, all_values[-1], sent, *query_here) for x in key_pieces[1:])
+        key_pieces[0], *(after(x, all_values[-1], *query_here) for x in key_pieces[1:])
     ]
     keys_here = join_rows(key_pieces, "col")
     got = keys_here
     if parts > 1:
         keys_there = swap(keys_here, "row", n_row, row_bits[0])
-        query_here = [swap(x, "col", n_col, k) if k else x for k, x in enumerate(query_here)]
+        moved = {k: swap(query_here[k], "col", n_col, k) for k in reversed(range(1, parts))}
+        query_here = [query_here[0]] + [moved[k] for k in range(1, parts)]
         all_values += [swap(x, "row", n_row, row_bits[1]) for x in all_values]
         all_keys = [keys_here, keys_there, swap(keys_here, "row", n_row, row_bits[1])]
     else:
@@ -413,6 +414,10 @@
     if parts > 1:
         keys_there = after(keys_there, grad, *query_here)
         all_keys += [swap(keys_there, "row", n_row, row_bits[1])]
+
+    if parts > 1:
+        all_keys = all_keys[::-1]
+        all_values = all_values[::-1]
 
     mixed = [None] * parts
     col_bits = [1 << i for i in reversed(range(n_col.bit_length() - 1))]

time: 74.5 us -> 72.2 us (0.969)
  waiting for transfers between devices: 25.2 us -> 22 us
  starting transfers between devices: 30.5 us -> 32.1 us
    ppermute x25, waiting for transfers between devices: 23.4 us -> 18.3 us  [swap(): return lax.ppermute(x, axis, [(i, i ^ k) for i in range(size)])]
    all_to_all x1, waiting for transfers between devices: 1.79 us -> 3.72 us  [relay(): return lax.all_to_all(x, 'col', split_axis=0, concat_axis=0, tiled=True)]
    ppermute x25, starting transfers between devices: 24 us -> 25.7 us  [swap(): return lax.ppermute(x, axis, [(i, i ^ k) for i in range(size)])]
  transfers between devices with their start and end apart: 26 -> 26, of which waited for: 12 -> 11; matrix products, arithmetic and copies ran while one was open for 1% -> 1% of each run, Pallas kernels for 17% -> 17%
where the time goes in v6:
time: 72.2 us; the launch traced here: 71.9 us
  starting transfers between devices  32.1 us (44%)
  waiting for transfers between devices  22 us (30%)
  Pallas kernels  14.1 us (20%)
  local copies, waits for them, and re-layouts  2.3 us (3%)
  between operations  0.87 us (1%)
    ppermute x25, starting transfers between devices, swap(): return lax.ppermute(x, axis, [(i, i ^ k) for i in range(size)])  25.7 us
    ppermute x25, waiting for transfers between devices, swap(): return lax.ppermute(x, axis, [(i, i ^ k) for i in range(size)])  18.3 us
    pallas_call x4, Pallas kernels, attention(): kernel_call(body, jax.ShapeDtypeStruct((rows, width), jnp.bfloat16))  7.95 us
    all_to_all x1, starting transfers between devices, relay(): return lax.all_to_all(x, 'col', split_axis=0, concat_axis=0, tiled=True)  6.45 us
    all_to_all x1, waiting for transfers between devices, relay(): return lax.all_to_all(x, 'col', split_axis=0, concat_axis=0, tiled=True)  3.72 us
    unnamed x26, local copies, waits for them, and re-layouts  2.02 us
    pallas_call x1, Pallas kernels, image_attention(): kernel_call(body, [jax.ShapeDtypeStruct((rows, width), jnp.bfloat16), *[j...  1.92 us
  transfers between devices with their start and end apart: 26, of which 11 were waited for; matrix products, arithmetic and copies ran while one was open for 1% of the time, Pallas kernels for 17%

profile of v6, /device:TPU:0, one launch (start us, length us, event | category | flops | bytes accessed | tf_op | source)
XLA Modules:
  0.0 71.9 jit_solution(3444040242893215972)
XLA Ops:
  0.6 1.0 %copy-done.2 = bf16[160,1536]{1,0:T(8,128)(2,1)S(1)} copy-done((bf16[160,1536]{1,0:T(8,128)(2,1)S(1)}, bf16[160,1536]{1,0:T(8,128)(2,1)}, u32[]{:S(2)}) %copy-start.2) | copy-done | bytes 491544
  1.7 0.8 %shard_map.156 = bf16[4,160,384]{2,1,0:T(8,128)(2,1)} custom-call(bf16[160,1536]{1,0:T(8,128)(2,1)S(1)} %copy-done.2), custom_call_target="tpu_custom_call" | custom-call | tf_op jit(solution)/shard_map/pallas_call | solution.py:70
  2.5 6.4 %all-to-all-start = ((bf16[4,160,384]{2,1,0:T(8,128)(2,1)}), bf16[4,160,384]{2,1,0:T(8,128)(2,1)S(1)}, u32[]{:S(2)}, u32[]{:S(2)}) async-start(bf16[4,160,384]{2,1,0:T(8,128)(2,1)} %shard_map.156), calls=%async_computation | async-start | bytes 983040 | tf_op jit(solution)/shard_map/all_to_all | solution.py:354
  9.0 0.1 shard_map.158
  9.1 1.6 %collective-permute-start.1 = (bf16[2,4,1536]{2,1,0:T(4,128)(2,1)S(1)}, bf16[2,4,1536]{2,1,0:T(4,128)(2,1)S(1)}, u32[]{:S(2)}, u32[]{:S(2)}) collective-permute-start(bf16[2,4,1536]{2,1,0:T(4,128)(2,1)S(1)} %get-tuple-element.41), channel_id=1, source_target_pairs={{0,16},{16,0},{1,17},{17,1},{2,18},{18,2},{3,19},{19,3},{4,20},{20... | collective-permute-start | bytes 73736 | tf_op jit(solution)/shard_map/ppermute | solution.py:21
  10.6 0.3 shard_map.157.refs_0_
  10.9 0.6 collective-permute-start
  11.7 0.1 mul.20
  11.8 1.3 %collective-permute-done.1 = bf16[2,4,1536]{2,1,0:T(4,128)(2,1)S(1)} collective-permute-done((bf16[2,4,1536]{2,1,0:T(4,128)(2,1)S(1)}, bf16[2,4,1536]{2,1,0:T(4,128)(2,1)S(1)}, u32[]{:S(2)}, u32[]{:S(2)}) %collective-permute-start.1) | collective-permute-done | bytes 24608 | tf_op jit(solution)/shard_map/ppermute | solution.py:21
  13.2 1.6 %collective-permute-start.3 = (bf16[2,8,1536]{2,1,0:T(8,128)(2,1)S(1)}, bf16[2,8,1536]{2,1,0:T(8,128)(2,1)S(1)}, u32[]{:S(2)}, u32[]{:S(2)}) collective-permute-start(bf16[2,8,1536]{2,1,0:T(8,128)(2,1)S(1)} %pad_maximum_fusion), channel_id=1, source_target_pairs={{0,4},{4,0},{8,12},{12,8},{1,5},{5,1},{9,13},{13,9},{2,6},{6,2},{1... | collective-permute-start | bytes 147464 | tf_op jit(solution)/shard_map/ppermute | solution.py:21
  14.9 0.5 collective-permute-start.2
  15.4 0.6 copy-done.10
  16.1 0.4 sine_multiply_fusion
  16.5 0.3 copy-done.7
  16.8 0.7 shard_map.159
  17.5 1.5 %collective-permute-done.2 = bf16[2,8,1536]{2,1,0:T(8,128)(2,1)S(1)} collective-permute-done((bf16[2,8,1536]{2,1,0:T(8,128)(2,1)S(1)}, bf16[2,8,1536]{2,1,0:T(8,128)(2,1)S(1)}, u32[]{:S(2)}, u32[]{:S(2)}) %collective-permute-start.2) | collective-permute-done | bytes 49184 | tf_op jit(solution)/shard_map/ppermute | solution.py:21
  19.0 3.7 %all-to-all-done = bf16[4,160,384]{2,1,0:T(8,128)(2,1)S(1)} async-done(((bf16[4,160,384]{2,1,0:T(8,128)(2,1)}), bf16[4,160,384]{2,1,0:T(8,128)(2,1)S(1)}, u32[]{:S(2)}, u32[]{:S(2)}) %all-to-all-start) | async-done | bytes 491552 | tf_op jit(solution)/shard_map/all_to_all | solution.py:354
  22.7 1.5 %collective-permute-start.7 = (bf16[640,384]{1,0:T(8,128)(2,1)S(1)}, bf16[640,384]{1,0:T(8,128)(2,1)S(1)}, u32[]{:S(2)}, u32[]{:S(2)}) collective-permute-start(bf16[640,384]{1,0:T(8,128)(2,1)S(1)} %bitcast.5), channel_id=1, source_target_pairs={{0,8},{4,12},{8,0},{12,4},{1,9},{5,13},{9,1},{13,5},{2,10},{6,14},... | collective-permute-start | bytes 1474568 | tf_op jit(solution)/shard_map/ppermute | solution.py:21
  24.3 2.0 %collective-permute-start.8 = (bf16[160,384]{1,0:T(8,128)(2,1)S(1)}, bf16[160,384]{1,0:T(8,128)(2,1)S(1)}, u32[]{:S(2)}, u32[]{:S(2)}) collective-permute-start(bf16[160,384]{1,0:T(8,128)(2,1)S(1)} %get-tuple-element.55), channel_id=1, source_target_pairs={{0,2},{1,3},{2,0},{3,1},{4,6},{5,7},{6,4},{7,5},{8,10},{9,11},{10,... | collective-permute-start | bytes 368648 | tf_op jit(solution)/shard_map/ppermute | solution.py:21
  26.3 2.4 %collective-permute-start.6 = (bf16[160,384]{1,0:T(8,128)(2,1)S(1)}, bf16[160,384]{1,0:T(8,128)(2,1)S(1)}, u32[]{:S(2)}, u32[]{:S(2)}) collective-permute-start(bf16[160,384]{1,0:T(8,128)(2,1)S(1)} %get-tuple-element.50), channel_id=1, source_target_pairs={{0,3},{1,2},{2,1},{3,0},{4,7},{5,6},{6,5},{7,4},{8,11},{9,10},{10,... | collective-permute-start | bytes 368648 | tf_op jit(solution)/shard_map/ppermute | solution.py:21
  28.7 1.9 %shard_map.162 = (bf16[160,1536]{1,0:T(8,128)(2,1)}, f32[2,4,4,1536]{3,2,1,0:T(4,128)S(1)}, f32[2,4,4,1536]{3,2,1,0:T(4,128)S(1)}) custom-call(f32[160,2]{1,0:T(8,128)S(1)} %shard_map.157.refs_0_, f32[160,2]{1,0:T(8,128)S(1)} %collective-permute-done.refs_1_, bf16[160,1536]{1,0:T(8,128)(2,1)S(1)} %copy-done, f32[1,1536]{1,0:T(1,128)S(1)} %broadcast_in_dim.64.refs_3_, ...), custom_call_target="tpu_custom_call" | custom-call | flops 1000 | bytes 1000 | tf_op jit(solution)/shard_map/pallas_call | solution.py:321
  30.6 1.5 %collective-permute-start.11 = (f32[2,4,4,1536]{3,2,1,0:T(4,128)S(1)}, f32[2,4,4,1536]{3,2,1,0:T(4,128)S(1)}, u32[]{:S(2)}, u32[]{:S(2)}) collective-permute-start(f32[2,4,4,1536]{3,2,1,0:T(4,128)S(1)} %get-tuple-element.60), channel_id=1, source_target_pairs={{0,16},{16,0},{1,17},{17,1},{2,18},{18,2},{3,19},{19,3},{4,20},{20... | collective-permute-start | bytes 589832 | tf_op jit(solution)/shard_map/ppermute | solution.py:21
  32.1 0.7 shard_map.160
  32.8 2.2 %collective-permute-done.7.refs_6_ = bf16[640,384]{1,0:T(8,128)(2,1)S(1)} collective-permute-done((bf16[640,384]{1,0:T(8,128)(2,1)S(1)}, bf16[640,384]{1,0:T(8,128)(2,1)S(1)}, u32[]{:S(2)}, u32[]{:S(2)}) %collective-permute-start.7) | collective-permute-done | bytes 491552 | tf_op jit(solution)/shard_map/ppermute | solution.py:21
  34.9 0.9 %collective-permute-done.8.refs_1_ = bf16[160,384]{1,0:T(8,128)(2,1)S(1)} collective-permute-done((bf16[160,384]{1,0:T(8,128)(2,1)S(1)}, bf16[160,384]{1,0:T(8,128)(2,1)S(1)}, u32[]{:S(2)}, u32[]{:S(2)}) %collective-permute-start.8) | collective-permute-done | bytes 122912 | tf_op jit(solution)/shard_map/ppermute | solution.py:21
  35.9 0.7 collective-permute-start.10
  36.7 1.3 %collective-permute-start.5 = (bf16[160,384]{1,0:T(8,128)(2,1)S(1)}, bf16[160,384]{1,0:T(8,128)(2,1)S(1)}, u32[]{:S(2)}, u32[]{:S(2)}) collective-permute-start(bf16[160,384]{1,0:T(8,128)(2,1)S(1)} %get-tuple-element.49), channel_id=1, source_target_pairs={{0,3},{1,2},{2,1},{3,0},{4,7},{5,6},{6,5},{7,4},{8,11},{9,10},{10,... | collective-permute-start | bytes 368648 | tf_op jit(solution)/shard_map/ppermute | solution.py:21
  38.0 1.0 %collective-permute-start.14 = (bf16[160,384]{1,0:T(8,128)(2,1)S(1)}, bf16[160,384]{1,0:T(8,128)(2,1)S(1)}, u32[]{:S(2)}, u32[]{:S(2)}) collective-permute-start(bf16[160,384]{1,0:T(8,128)(2,1)S(1)} %get-tuple-element.52), channel_id=1, source_target_pairs={{0,1},{1,0},{2,3},{3,2},{4,5},{5,4},{6,7},{7,6},{8,9},{9,8},{10,11... | collective-permute-start | bytes 368648 | tf_op jit(solution)/shard_map/ppermute | solution.py:21
  39.0 2.1 %collective-permute-start.15 = (bf16[160,384]{1,0:T(8,128)(2,1)S(1)}, bf16[160,384]{1,0:T(8,128)(2,1)S(1)}, u32[]{:S(2)}, u32[]{:S(2)}) collective-permute-start(bf16[160,384]{1,0:T(8,128)(2,1)S(1)} %get-tuple-element.53), channel_id=1, source_target_pairs={{0,2},{1,3},{2,0},{3,1},{4,6},{5,7},{6,4},{7,5},{8,10},{9,11},{10,... | collective-permute-start | bytes 368648 | tf_op jit(solution)/shard_map/ppermute | solution.py:21
  41.2 1.4 %collective-permute-start.13 = (f32[4,1,4,1536]{3,2,1,0:T(4,128)S(1)}, f32[4,1,4,1536]{3,2,1,0:T(4,128)S(1)}, u32[]{:S(2)}, u32[]{:S(2)}) collective-permute-start(f32[4,1,4,1536]{3,2,1,0:T(4,128)S(1)} %get-tuple-element.65), channel_id=1, source_target_pairs={{0,8},{4,12},{8,0},{12,4},{1,9},{5,13},{9,1},{13,5},{2,10},{6,14},... | collective-permute-start | bytes 294920 | tf_op jit(solution)/shard_map/ppermute | solution.py:21
  42.6 5.8 %collective-permute-done.13.y_ref = f32[4,1,4,1536]{3,2,1,0:T(4,128)S(1)} collective-permute-done((f32[4,1,4,1536]{3,2,1,0:T(4,128)S(1)}, f32[4,1,4,1536]{3,2,1,0:T(4,128)S(1)}, u32[]{:S(2)}, u32[]{:S(2)}) %collective-permute-start.13) | collective-permute-done | bytes 98336 | tf_op jit(solution)/shard_map/ppermute | solution.py:21
  48.5 0.6 collective-permute-start.17
  49.0 0.1 collective-permute-start.18
  49.1 2.4 %collective-permute-done.15.q_ref = bf16[160,384]{1,0:T(8,128)(2,1)S(1)} collective-permute-done((bf16[160,384]{1,0:T(8,128)(2,1)S(1)}, bf16[160,384]{1,0:T(8,128)(2,1)S(1)}, u32[]{:S(2)}, u32[]{:S(2)}) %collective-permute-start.15) | collective-permute-done | bytes 122912 | tf_op jit(solution)/shard_map/ppermute | solution.py:21
  51.5 1.1 %collective-permute-start.23 = (f32[4,1,4,1536]{3,2,1,0:T(4,128)S(1)}, f32[4,1,4,1536]{3,2,1,0:T(4,128)S(1)}, u32[]{:S(2)}, u32[]{:S(2)}) collective-permute-start(f32[4,1,4,1536]{3,2,1,0:T(4,128)S(1)} %shard_map.165.x_ref), channel_id=1, source_target_pairs={{0,2},{1,3},{2,0},{3,1},{4,6},{5,7},{6,4},{7,5},{8,10},{9,11},{10,... | collective-permute-start | bytes 294920 | tf_op jit(solution)/shard_map/ppermute | solution.py:21
  52.6 0.8 %collective-permute-done.16.refs_0_ = bf16[640,384]{1,0:T(8,128)(2,1)S(1)} collective-permute-done((bf16[640,384]{1,0:T(8,128)(2,1)S(1)}, bf16[640,384]{1,0:T(8,128)(2,1)S(1)}, u32[]{:S(2)}, u32[]{:S(2)}) %collective-permute-start.16) | collective-permute-done | bytes 491552 | tf_op jit(solution)/shard_map/ppermute | solution.py:21
  53.4 2.0 %shard_map.167 = bf16[160,384]{1,0:T(8,128)(2,1)S(1)} custom-call(bf16[160,384]{1,0:T(8,128)(2,1)S(1)} %collective-permute-done.15.q_ref, bf16[640,384]{1,0:T(8,128)(2,1)S(1)} %collective-permute-done.16.refs_0_, bf16[640,384]{1,0:T(8,128)(2,1)S(1)} %collective-permute-done.17.refs_1_, bf16[640,384]{1,0:T(8,128)(2,1)S(1)} %collective-permute-done.10.refs_2_, ...), custom_call_target="tpu_custom_call" | custom-call | tf_op jit(solution)/shard_map/pallas_call | solution.py:279
  55.3 2.1 %collective-permute-start.21 = (bf16[160,384]{1,0:T(8,128)(2,1)S(1)}, bf16[160,384]{1,0:T(8,128)(2,1)S(1)}, u32[]{:S(2)}, u32[]{:S(2)}) collective-permute-start(bf16[160,384]{1,0:T(8,128)(2,1)S(1)} %shard_map.167), channel_id=1, source_target_pairs={{0,2},{1,3},{2,0},{3,1},{4,6},{5,7},{6,4},{7,5},{8,10},{9,11},{10,... | collective-permute-start | bytes 368648 | tf_op jit(solution)/shard_map/ppermute | solution.py:21
  57.5 2.0 %shard_map.168 = bf16[160,384]{1,0:T(8,128)(2,1)S(1)} custom-call(bf16[160,384]{1,0:T(8,128)(2,1)S(1)} %collective-permute-done.14.q_ref, bf16[640,384]{1,0:T(8,128)(2,1)S(1)} %collective-permute-done.16.refs_0_, bf16[640,384]{1,0:T(8,128)(2,1)S(1)} %collective-permute-done.17.refs_1_, bf16[640,384]{1,0:T(8,128)(2,1)S(1)} %collective-permute-done.10.refs_2_, ...), custom_call_target="tpu_custom_call" | custom-call | tf_op jit(solution)/shard_map/pallas_call | solution.py:279
  59.5 2.0 %shard_map.166 = bf16[160,384]{1,0:T(8,128)(2,1)S(1)} custom-call(bf16[160,384]{1,0:T(8,128)(2,1)S(1)} %collective-permute-done.5.q_ref, bf16[640,384]{1,0:T(8,128)(2,1)S(1)} %collective-permute-done.16.refs_0_, bf16[640,384]{1,0:T(8,128)(2,1)S(1)} %collective-permute-done.17.refs_1_, bf16[640,384]{1,0:T(8,128)(2,1)S(1)} %collective-permute-done.10.refs_2_, ...), custom_call_target="tpu_custom_call" | custom-call | tf_op jit(solution)/shard_map/pallas_call | solution.py:279
  61.5 2.4 %collective-permute-start.20 = (bf16[160,384]{1,0:T(8,128)(2,1)S(1)}, bf16[160,384]{1,0:T(8,128)(2,1)S(1)}, u32[]{:S(2)}, u32[]{:S(2)}) collective-permute-start(bf16[160,384]{1,0:T(8,128)(2,1)S(1)} %shard_map.166), channel_id=1, source_target_pairs={{0,3},{1,2},{2,1},{3,0},{4,7},{5,6},{6,5},{7,4},{8,11},{9,10},{10,... | collective-permute-start | bytes 368648 | tf_op jit(solution)/shard_map/ppermute | solution.py:21
  63.9 1.0 %collective-permute-start.24 = (f32[4,1,4,1536]{3,2,1,0:T(4,128)S(1)}, f32[4,1,4,1536]{3,2,1,0:T(4,128)S(1)}, u32[]{:S(2)}, u32[]{:S(2)}) collective-permute-start(f32[4,1,4,1536]{3,2,1,0:T(4,128)S(1)} %shard_map.171.first_ref), channel_id=1, source_target_pairs={{0,1},{1,0},{2,3},{3,2},{4,5},{5,4},{6,7},{7,6},{8,9},{9,8},{10,11... | collective-permute-start | bytes 294920 | tf_op jit(solution)/shard_map/ppermute | solution.py:21
  64.9 2.0 %shard_map.169.refs_3_ = bf16[160,384]{1,0:T(8,128)(2,1)S(1)} custom-call(bf16[160,384]{1,0:T(8,128)(2,1)S(1)} %get-tuple-element.51.q_ref, bf16[640,384]{1,0:T(8,128)(2,1)S(1)} %collective-permute-done.16.refs_0_, bf16[640,384]{1,0:T(8,128)(2,1)S(1)} %collective-permute-done.17.refs_1_, bf16[640,384]{1,0:T(8,128)(2,1)S(1)} %collective-permute-done.10.refs_2_, ...), custom_call_target="tpu_custom_call" | custom-call | tf_op jit(solution)/shard_map/pallas_call | solution.py:279
  66.9 2.4 %collective-permute-done.22.refs_2_ = bf16[160,384]{1,0:T(8,128)(2,1)S(1)} collective-permute-done((bf16[160,384]{1,0:T(8,128)(2,1)S(1)}, bf16[160,384]{1,0:T(8,128)(2,1)S(1)}, u32[]{:S(2)}, u32[]{:S(2)}) %collective-permute-start.22) | collective-permute-done | bytes 122912 | tf_op jit(solution)/shard_map/ppermute | solution.py:21
  69.3 0.3 collective-permute-done.20.refs_0_
  69.6 0.8 %shard_map.170 = bf16[160,1536]{1,0:T(8,128)(2,1)} custom-call(bf16[160,384]{1,0:T(8,128)(2,1)S(1)} %collective-permute-done.20.refs_0_, bf16[160,384]{1,0:T(8,128)(2,1)S(1)} %collective-permute-done.21.refs_1_, bf16[160,384]{1,0:T(8,128)(2,1)S(1)} %collective-permute-done.22.refs_2_, bf16[160,384]{1,0:T(8,128)(2,1)S(1)} %shard_map.169.refs_3_), custom_call_target="tpu_custom_call" | custom-call | tf_op jit(solution)/shard_map/pallas_call | solution.py:101
  70.4 0.8 %collective-permute-done.24.second_ref = f32[4,1,4,1536]{3,2,1,0:T(4,128)S(1)} collective-permute-done((f32[4,1,4,1536]{3,2,1,0:T(4,128)S(1)}, f32[4,1,4,1536]{3,2,1,0:T(4,128)S(1)}, u32[]{:S(2)}, u32[]{:S(2)}) %collective-permute-start.24) | collective-permute-done | bytes 98336 | tf_op jit(solution)/shard_map/ppermute | solution.py:21
  71.2 0.8 %shard_map.172 = (f32[4,3072]{1,0:T(4,128)}, f32[4,3072]{1,0:T(4,128)}) custom-call(bf16[4,3072]{1,0:T(4,128)(2,1)S(1)} %copy-done.4, f32[1,3072]{1,0:T(1,128)S(1)} %bitcast.12, f32[4,1,4,1536]{3,2,1,0:T(4,128)S(1)} %shard_map.171.first_ref, f32[4,1,4,1536]{3,2,1,0:T(4,128)S(1)} %collective-permute-done.24.second_ref), custom_call_target="tpu_custom_call" | custom-call | tf_op jit(solution)/shard_map/pallas_call | solution.py:170
  (59 shorter events, 0.7 us)
Async XLA Ops:
  0.6 1.0 %copy-start.2 = (bf16[160,1536]{1,0:T(8,128)(2,1)S(1)}, bf16[160,1536]{1,0:T(8,128)(2,1)}, u32[]{:S(2)}) copy-start(bf16[160,1536]{1,0:T(8,128)(2,1)} %x_ref.1) | copy-start | bytes 1474564
  1.7 7.3 %copy-start.4 = (bf16[4,3072]{1,0:T(4,128)(2,1)S(1)}, bf16[4,3072]{1,0:T(4,128)(2,1)}, u32[]{:S(2)}) copy-start(bf16[4,3072]{1,0:T(4,128)(2,1)} %k_ref.4) | copy-start | bytes 73732
  1.7 7.3 %copy-start.5 = (f32[3072]{0:T(1024)S(1)}, f32[3072]{0:T(1024)}, u32[]{:S(2)}) copy-start(f32[3072]{0:T(1024)} %param.21) | copy-start | bytes 36868
  1.7 7.3 %copy-start.6 = (bf16[4,3072]{1,0:T(4,128)(2,1)S(1)}, bf16[4,3072]{1,0:T(4,128)(2,1)}, u32[]{:S(2)}) copy-start(bf16[4,3072]{1,0:T(4,128)(2,1)} %v_ref.1) | copy-start | bytes 73732
  2.5 8.2 %copy-start = (bf16[160,1536]{1,0:T(8,128)(2,1)S(1)}, bf16[160,1536]{1,0:T(8,128)(2,1)}, u32[]{:S(2)}) copy-start(bf16[160,1536]{1,0:T(8,128)(2,1)} %refs_2_.4) | copy-start | bytes 1474564
  2.5 8.2 %copy-start.1 = (bf16[160,1536]{1,0:T(8,128)(2,1)S(1)}, bf16[160,1536]{1,0:T(8,128)(2,1)}, u32[]{:S(2)}) copy-start(bf16[160,1536]{1,0:T(8,128)(2,1)} %refs_2_.2) | copy-start | bytes 1474564
  2.5 20.2 %all-to-all-start = ((bf16[4,160,384]{2,1,0:T(8,128)(2,1)}), bf16[4,160,384]{2,1,0:T(8,128)(2,1)S(1)}, u32[]{:S(2)}, u32[]{:S(2)}) async-start(bf16[4,160,384]{2,1,0:T(8,128)(2,1)} %shard_map.156), calls=%async_computation | async-start | bytes 983040 | tf_op jit(solution)/shard_map/all_to_all | solution.py:354
  9.1 4.0 %collective-permute-start.1 = (bf16[2,4,1536]{2,1,0:T(4,128)(2,1)S(1)}, bf16[2,4,1536]{2,1,0:T(4,128)(2,1)S(1)}, u32[]{:S(2)}, u32[]{:S(2)}) collective-permute-start(bf16[2,4,1536]{2,1,0:T(4,128)(2,1)S(1)} %get-tuple-element.41), channel_id=1, source_target_pairs={{0,16},{16,0},{1,17},{17,1},{2,18},{18,2},{3,19},{19,3},{4,20},{20... | collective-permute-start | bytes 73736 | tf_op jit(solution)/shard_map/ppermute | solution.py:21
  10.6 0.9 %copy-start.9 = (s32[160,3]{0,1:T(4,128)S(1)}, s32[160,3]{0,1:T(4,128)}, u32[]{:S(2)}) copy-start(s32[160,3]{0,1:T(4,128)} %param.16) | copy-start | bytes 5764
  10.9 5.8 %collective-permute-start = (f32[160,2]{1,0:T(8,128)S(1)}, f32[160,2]{1,0:T(8,128)S(1)}, u32[]{:S(2)}, u32[]{:S(2)}) collective-permute-start(f32[160,2]{1,0:T(8,128)S(1)} %shard_map.157.refs_0_), channel_id=1, source_target_pairs={{0,16},{16,0},{1,17},{17,1},{2,18},{18,2},{3,19},{19,3},{4,20},{20... | collective-permute-start | bytes 3848 | tf_op jit(solution)/shard_map/ppermute | solution.py:21
  13.2 4.3 %collective-permute-start.4 = (bf16[2,8,1536]{2,1,0:T(8,128)(2,1)S(1)}, bf16[2,8,1536]{2,1,0:T(8,128)(2,1)S(1)}, u32[]{:S(2)}, u32[]{:S(2)}) collective-permute-start(bf16[2,8,1536]{2,1,0:T(8,128)(2,1)S(1)} %pad_maximum_fusion), channel_id=1, source_target_pairs={{0,12},{4,8},{8,4},{12,0},{1,13},{5,9},{9,5},{13,1},{2,14},{6,10},... | collective-permute-start | bytes 147464 | tf_op jit(solution)/shard_map/ppermute | solution.py:21
  13.2 4.2 %collective-permute-start.3 = (bf16[2,8,1536]{2,1,0:T(8,128)(2,1)S(1)}, bf16[2,8,1536]{2,1,0:T(8,128)(2,1)S(1)}, u32[]{:S(2)}, u32[]{:S(2)}) collective-permute-start(bf16[2,8,1536]{2,1,0:T(8,128)(2,1)S(1)} %pad_maximum_fusion), channel_id=1, source_target_pairs={{0,4},{4,0},{8,12},{12,8},{1,5},{5,1},{9,13},{13,9},{2,6},{6,2},{1... | collective-permute-start | bytes 147464 | tf_op jit(solution)/shard_map/ppermute | solution.py:21
  14.9 4.1 %collective-permute-start.2 = (bf16[2,8,1536]{2,1,0:T(8,128)(2,1)S(1)}, bf16[2,8,1536]{2,1,0:T(8,128)(2,1)S(1)}, u32[]{:S(2)}, u32[]{:S(2)}) collective-permute-start(bf16[2,8,1536]{2,1,0:T(8,128)(2,1)S(1)} %pad_maximum_fusion), channel_id=1, source_target_pairs={{0,8},{4,12},{8,0},{12,4},{1,9},{5,13},{9,1},{13,5},{2,10},{6,14},... | collective-permute-start | bytes 147464 | tf_op jit(solution)/shard_map/ppermute | solution.py:21
  15.4 0.7 copy-start.10
  15.4 0.7 copy-start.11
  15.4 0.7 copy-start.12
  16.1 0.7 copy-start.7
  16.8 11.9 %copy-start.3 = (bf16[160,1536]{1,0:T(8,128)(2,1)S(1)}, bf16[160,1536]{1,0:T(8,128)(2,1)}, u32[]{:S(2)}) copy-start(bf16[160,1536]{1,0:T(8,128)(2,1)} %refs_5_.1) | copy-start | bytes 1474564
  19.0 9.7 %copy-start.8 = (f32[1536]{0:T(1024)S(1)}, f32[1536]{0:T(1024)}, u32[]{:S(2)}) copy-start(f32[1536]{0:T(1024)} %param.17) | copy-start | bytes 18436
  22.7 12.2 %collective-permute-start.7 = (bf16[640,384]{1,0:T(8,128)(2,1)S(1)}, bf16[640,384]{1,0:T(8,128)(2,1)S(1)}, u32[]{:S(2)}, u32[]{:S(2)}) collective-permute-start(bf16[640,384]{1,0:T(8,128)(2,1)S(1)} %bitcast.5), channel_id=1, source_target_pairs={{0,8},{4,12},{8,0},{12,4},{1,9},{5,13},{9,1},{13,5},{2,10},{6,14},... | collective-permute-start | bytes 1474568 | tf_op jit(solution)/shard_map/ppermute | solution.py:21
  24.3 8.5 %collective-permute-start.9 = (bf16[160,384]{1,0:T(8,128)(2,1)S(1)}, bf16[160,384]{1,0:T(8,128)(2,1)S(1)}, u32[]{:S(2)}, u32[]{:S(2)}) collective-permute-start(bf16[160,384]{1,0:T(8,128)(2,1)S(1)} %get-tuple-element.57), channel_id=1, source_target_pairs={{0,1},{1,0},{2,3},{3,2},{4,5},{5,4},{6,7},{7,6},{8,9},{9,8},{10,11... | collective-permute-start | bytes 368648 | tf_op jit(solution)/shard_map/ppermute | solution.py:21
  24.3 11.5 %collective-permute-start.8 = (bf16[160,384]{1,0:T(8,128)(2,1)S(1)}, bf16[160,384]{1,0:T(8,128)(2,1)S(1)}, u32[]{:S(2)}, u32[]{:S(2)}) collective-permute-start(bf16[160,384]{1,0:T(8,128)(2,1)S(1)} %get-tuple-element.55), channel_id=1, source_target_pairs={{0,2},{1,3},{2,0},{3,1},{4,6},{5,7},{6,4},{7,5},{8,10},{9,11},{10,... | collective-permute-start | bytes 368648 | tf_op jit(solution)/shard_map/ppermute | solution.py:21
  26.3 9.5 %collective-permute-start.6 = (bf16[160,384]{1,0:T(8,128)(2,1)S(1)}, bf16[160,384]{1,0:T(8,128)(2,1)S(1)}, u32[]{:S(2)}, u32[]{:S(2)}) collective-permute-start(bf16[160,384]{1,0:T(8,128)(2,1)S(1)} %get-tuple-element.50), channel_id=1, source_target_pairs={{0,3},{1,2},{2,1},{3,0},{4,7},{5,6},{6,5},{7,4},{8,11},{9,10},{10,... | collective-permute-start | bytes 368648 | tf_op jit(solution)/shard_map/ppermute | solution.py:21
  30.6 6.0 %collective-permute-start.11 = (f32[2,4,4,1536]{3,2,1,0:T(4,128)S(1)}, f32[2,4,4,1536]{3,2,1,0:T(4,128)S(1)}, u32[]{:S(2)}, u32[]{:S(2)}) collective-permute-start(f32[2,4,4,1536]{3,2,1,0:T(4,128)S(1)} %get-tuple-element.60), channel_id=1, source_target_pairs={{0,16},{16,0},{1,17},{17,1},{2,18},{18,2},{3,19},{19,3},{4,20},{20... | collective-permute-start | bytes 589832 | tf_op jit(solution)/shard_map/ppermute | solution.py:21
  35.9 15.6 %collective-permute-start.10 = (bf16[640,384]{1,0:T(8,128)(2,1)S(1)}, bf16[640,384]{1,0:T(8,128)(2,1)S(1)}, u32[]{:S(2)}, u32[]{:S(2)}) collective-permute-start(bf16[640,384]{1,0:T(8,128)(2,1)S(1)} %shard_map.161.refs_3_), channel_id=1, source_target_pairs={{0,8},{4,12},{8,0},{12,4},{1,9},{5,13},{9,1},{13,5},{2,10},{6,14},... | collective-permute-start | bytes 1474568 | tf_op jit(solution)/shard_map/ppermute | solution.py:21
  36.6 4.5 %collective-permute-start.12 = (f32[4,2,4,1536]{3,2,1,0:T(4,128)S(1)}, f32[4,2,4,1536]{3,2,1,0:T(4,128)S(1)}, u32[]{:S(2)}, u32[]{:S(2)}) collective-permute-start(f32[4,2,4,1536]{3,2,1,0:T(4,128)S(1)} %get-tuple-element.62), channel_id=1, source_target_pairs={{0,4},{4,0},{8,12},{12,8},{1,5},{5,1},{9,13},{13,9},{2,6},{6,2},{1... | collective-permute-start | bytes 589832 | tf_op jit(solution)/shard_map/ppermute | solution.py:21
  36.7 11.8 %collective-permute-start.5 = (bf16[160,384]{1,0:T(8,128)(2,1)S(1)}, bf16[160,384]{1,0:T(8,128)(2,1)S(1)}, u32[]{:S(2)}, u32[]{:S(2)}) collective-permute-start(bf16[160,384]{1,0:T(8,128)(2,1)S(1)} %get-tuple-element.49), channel_id=1, source_target_pairs={{0,3},{1,2},{2,1},{3,0},{4,7},{5,6},{6,5},{7,4},{8,11},{9,10},{10,... | collective-permute-start | bytes 368648 | tf_op jit(solution)/shard_map/ppermute | solution.py:21
  38.0 11.0 %collective-permute-start.14 = (bf16[160,384]{1,0:T(8,128)(2,1)S(1)}, bf16[160,384]{1,0:T(8,128)(2,1)S(1)}, u32[]{:S(2)}, u32[]{:S(2)}) collective-permute-start(bf16[160,384]{1,0:T(8,128)(2,1)S(1)} %get-tuple-element.52), channel_id=1, source_target_pairs={{0,1},{1,0},{2,3},{3,2},{4,5},{5,4},{6,7},{7,6},{8,9},{9,8},{10,11... | collective-permute-start | bytes 368648 | tf_op jit(solution)/shard_map/ppermute | solution.py:21
  39.0 12.5 %collective-permute-start.15 = (bf16[160,384]{1,0:T(8,128)(2,1)S(1)}, bf16[160,384]{1,0:T(8,128)(2,1)S(1)}, u32[]{:S(2)}, u32[]{:S(2)}) collective-permute-start(bf16[160,384]{1,0:T(8,128)(2,1)S(1)} %get-tuple-element.53), channel_id=1, source_target_pairs={{0,2},{1,3},{2,0},{3,1},{4,6},{5,7},{6,4},{7,5},{8,10},{9,11},{10,... | collective-permute-start | bytes 368648 | tf_op jit(solution)/shard_map/ppermute | solution.py:21
  41.2 7.3 %collective-permute-start.13 = (f32[4,1,4,1536]{3,2,1,0:T(4,128)S(1)}, f32[4,1,4,1536]{3,2,1,0:T(4,128)S(1)}, u32[]{:S(2)}, u32[]{:S(2)}) collective-permute-start(f32[4,1,4,1536]{3,2,1,0:T(4,128)S(1)} %get-tuple-element.65), channel_id=1, source_target_pairs={{0,8},{4,12},{8,0},{12,4},{1,9},{5,13},{9,1},{13,5},{2,10},{6,14},... | collective-permute-start | bytes 294920 | tf_op jit(solution)/shard_map/ppermute | solution.py:21
  48.4 4.2 %collective-permute-start.19 = (bf16[640,384]{1,0:T(8,128)(2,1)S(1)}, bf16[640,384]{1,0:T(8,128)(2,1)S(1)}, u32[]{:S(2)}, u32[]{:S(2)}) collective-permute-start(bf16[640,384]{1,0:T(8,128)(2,1)S(1)} %bitcast.6), channel_id=1, source_target_pairs={{0,4},{4,0},{8,12},{12,8},{1,5},{5,1},{9,13},{13,9},{2,6},{6,2},{1... | collective-permute-start | bytes 1474568 | tf_op jit(solution)/shard_map/ppermute | solution.py:21
  48.5 4.1 %collective-permute-start.17 = (bf16[640,384]{1,0:T(8,128)(2,1)S(1)}, bf16[640,384]{1,0:T(8,128)(2,1)S(1)}, u32[]{:S(2)}, u32[]{:S(2)}) collective-permute-start(bf16[640,384]{1,0:T(8,128)(2,1)S(1)} %shard_map.161.refs_3_), channel_id=1, source_target_pairs={{0,4},{4,0},{8,12},{12,8},{1,5},{5,1},{9,13},{13,9},{2,6},{6,2},{1... | collective-permute-start | bytes 1474568 | tf_op jit(solution)/shard_map/ppermute | solution.py:21
  49.0 3.6 %collective-permute-start.18 = (bf16[640,384]{1,0:T(8,128)(2,1)S(1)}, bf16[640,384]{1,0:T(8,128)(2,1)S(1)}, u32[]{:S(2)}, u32[]{:S(2)}) collective-permute-start(bf16[640,384]{1,0:T(8,128)(2,1)S(1)} %collective-permute-done.7.refs_6_), channel_id=1, source_target_pairs={{0,4},{4,0},{8,12},{12,8},{1,5},{5,1},{9,13},{13,9},{2,6},{6,2},{1... | collective-permute-start | bytes 1474568 | tf_op jit(solution)/shard_map/ppermute | solution.py:21
  51.5 1.9 %collective-permute-start.16 = (bf16[640,384]{1,0:T(8,128)(2,1)S(1)}, bf16[640,384]{1,0:T(8,128)(2,1)S(1)}, u32[]{:S(2)}, u32[]{:S(2)}) collective-permute-start(bf16[640,384]{1,0:T(8,128)(2,1)S(1)} %collective-permute-done.10.refs_2_), channel_id=1, source_target_pairs={{0,4},{4,0},{8,12},{12,8},{1,5},{5,1},{9,13},{13,9},{2,6},{6,2},{1... | collective-permute-start | bytes 1474568 | tf_op jit(solution)/shard_map/ppermute | solution.py:21
  51.5 12.4 %collective-permute-start.23 = (f32[4,1,4,1536]{3,2,1,0:T(4,128)S(1)}, f32[4,1,4,1536]{3,2,1,0:T(4,128)S(1)}, u32[]{:S(2)}, u32[]{:S(2)}) collective-permute-start(f32[4,1,4,1536]{3,2,1,0:T(4,128)S(1)} %shard_map.165.x_ref), channel_id=1, source_target_pairs={{0,2},{1,3},{2,0},{3,1},{4,6},{5,7},{6,4},{7,5},{8,10},{9,11},{10,... | collective-permute-start | bytes 294920 | tf_op jit(solution)/shard_map/ppermute | solution.py:21
  55.3 11.6 %collective-permute-start.21 = (bf16[160,384]{1,0:T(8,128)(2,1)S(1)}, bf16[160,384]{1,0:T(8,128)(2,1)S(1)}, u32[]{:S(2)}, u32[]{:S(2)}) collective-permute-start(bf16[160,384]{1,0:T(8,128)(2,1)S(1)} %shard_map.167), channel_id=1, source_target_pairs={{0,2},{1,3},{2,0},{3,1},{4,6},{5,7},{6,4},{7,5},{8,10},{9,11},{10,... | collective-permute-start | bytes 368648 | tf_op jit(solution)/shard_map/ppermute | solution.py:21
  59.5 9.9 %collective-permute-start.22 = (bf16[160,384]{1,0:T(8,128)(2,1)S(1)}, bf16[160,384]{1,0:T(8,128)(2,1)S(1)}, u32[]{:S(2)}, u32[]{:S(2)}) collective-permute-start(bf16[160,384]{1,0:T(8,128)(2,1)S(1)} %shard_map.168), channel_id=1, source_target_pairs={{0,1},{1,0},{2,3},{3,2},{4,5},{5,4},{6,7},{7,6},{8,9},{9,8},{10,11... | collective-permute-start | bytes 368648 | tf_op jit(solution)/shard_map/ppermute | solution.py:21
  61.5 8.1 %collective-permute-start.20 = (bf16[160,384]{1,0:T(8,128)(2,1)S(1)}, bf16[160,384]{1,0:T(8,128)(2,1)S(1)}, u32[]{:S(2)}, u32[]{:S(2)}) collective-permute-start(bf16[160,384]{1,0:T(8,128)(2,1)S(1)} %shard_map.166), channel_id=1, source_target_pairs={{0,3},{1,2},{2,1},{3,0},{4,7},{5,6},{6,5},{7,4},{8,11},{9,10},{10,... | collective-permute-start | bytes 368648 | tf_op jit(solution)/shard_map/ppermute | solution.py:21
  63.9 7.2 %collective-permute-start.24 = (f32[4,1,4,1536]{3,2,1,0:T(4,128)S(1)}, f32[4,1,4,1536]{3,2,1,0:T(4,128)S(1)}, u32[]{:S(2)}, u32[]{:S(2)}) collective-permute-start(f32[4,1,4,1536]{3,2,1,0:T(4,128)S(1)} %shard_map.171.first_ref), channel_id=1, source_target_pairs={{0,1},{1,0},{2,3},{3,2},{4,5},{5,4},{6,7},{7,6},{8,9},{9,8},{10,11... | collective-permute-start | bytes 294920 | tf_op jit(solution)/shard_map/ppermute | solution.py:21

commit v7 on v6

--- a/solution.py
+++ b/solution.py
@@ -261,18 +261,13 @@
             current = following
             if j + 1 < len(heads):
                 following = scores(heads[j + 1])
-            peak = functools.reduce(
-                jnp.maximum, [jnp.max(s, axis=1, keepdims=True) for s in current]
-            )
-            weight_sum = 0.0
+            peak = jnp.max(functools.reduce(jnp.maximum, current), axis=1, keepdims=True)
+            weights = [jnp.exp2((s - peak) * factor) for s in current]
+            weight_sum = jnp.sum(sum(weights[1:], weights[0]), axis=1, keepdims=True)
             mixed = 0.0
-            for s, place in zip(current, places[len(keys) :]):
-                weights = jnp.exp2((s - peak) * factor)
-                weight_sum = weight_sum + jnp.sum(weights, axis=1, keepdims=True)
+            for w, place in zip(weights, places[len(keys) :]):
                 mixed = mixed + jnp.dot(
-                    weights.astype(jnp.bfloat16),
-                    part(place, cols),
-                    preferred_element_type=jnp.float32,
+                    w.astype(jnp.bfloat16), part(place, cols), preferred_element_type=jnp.float32
                 )
             refs[-1][:, cols] = (mixed / weight_sum).astype(jnp.bfloat16)
 

time: 72.2 us -> 72.1 us (level)
  transfers between devices with their start and end apart: 26 -> 26, of which waited for: 11 -> 10; matrix products, arithmetic and copies ran while one was open for 1% -> 1% of each run, Pallas kernels for 17% -> 17%
where the time goes in v7:
time: 72.1 us; the launch traced here: 71.9 us
  starting transfers between devices  32.1 us (45%)
  waiting for transfers between devices  22.2 us (31%)
  Pallas kernels  13.9 us (19%)
  local copies, waits for them, and re-layouts  2.3 us (3%)
  between operations  0.87 us (1%)
    ppermute x25, starting transfers between devices, swap(): return lax.ppermute(x, axis, [(i, i ^ k) for i in range(size)])  25.7 us
    ppermute x25, waiting for transfers between devices, swap(): return lax.ppermute(x, axis, [(i, i ^ k) for i in range(size)])  18.4 us
    pallas_call x4, Pallas kernels, attention(): kernel_call(body, jax.ShapeDtypeStruct((rows, width), jnp.bfloat16))  7.7 us
    all_to_all x1, starting transfers between devices, relay(): return lax.all_to_all(x, 'col', split_axis=0, concat_axis=0, tiled=True)  6.45 us
    all_to_all x1, waiting for transfers between devices, relay(): return lax.all_to_all(x, 'col', split_axis=0, concat_axis=0, tiled=True)  3.72 us
    unnamed x26, local copies, waits for them, and re-layouts  2.02 us
    pallas_call x1, Pallas kernels, image_attention(): kernel_call(body, [jax.ShapeDtypeStruct((rows, width), jnp.bfloat16), *[j...  1.92 us
  transfers between devices with their start and end apart: 26, of which 10 were waited for; matrix products, arithmetic and copies ran while one was open for 1% of the time, Pallas kernels for 17%

profile of v7, /device:TPU:0, one launch (start us, length us, event | category | flops | bytes accessed | tf_op | source)
XLA Modules:
  0.0 71.9 jit_solution(12999372097103432170)
XLA Ops:
  0.6 1.0 %copy-done.2 = bf16[160,1536]{1,0:T(8,128)(2,1)S(1)} copy-done((bf16[160,1536]{1,0:T(8,128)(2,1)S(1)}, bf16[160,1536]{1,0:T(8,128)(2,1)}, u32[]{:S(2)}) %copy-start.2) | copy-done | bytes 491544
  1.7 0.8 %shard_map.156 = bf16[4,160,384]{2,1,0:T(8,128)(2,1)} custom-call(bf16[160,1536]{1,0:T(8,128)(2,1)S(1)} %copy-done.2), custom_call_target="tpu_custom_call" | custom-call | tf_op jit(solution)/shard_map/pallas_call | solution.py:70
  2.5 6.4 %all-to-all-start = ((bf16[4,160,384]{2,1,0:T(8,128)(2,1)}), bf16[4,160,384]{2,1,0:T(8,128)(2,1)S(1)}, u32[]{:S(2)}, u32[]{:S(2)}) async-start(bf16[4,160,384]{2,1,0:T(8,128)(2,1)} %shard_map.156), calls=%async_computation | async-start | bytes 983040 | tf_op jit(solution)/shard_map/all_to_all | solution.py:349
  9.0 0.1 shard_map.158
  9.1 1.6 %collective-permute-start.1 = (bf16[2,4,1536]{2,1,0:T(4,128)(2,1)S(1)}, bf16[2,4,1536]{2,1,0:T(4,128)(2,1)S(1)}, u32[]{:S(2)}, u32[]{:S(2)}) collective-permute-start(bf16[2,4,1536]{2,1,0:T(4,128)(2,1)S(1)} %get-tuple-element.41), channel_id=1, source_target_pairs={{0,16},{16,0},{1,17},{17,1},{2,18},{18,2},{3,19},{19,3},{4,20},{20... | collective-permute-start | bytes 73736 | tf_op jit(solution)/shard_map/ppermute | solution.py:21
  10.6 0.3 shard_map.157.refs_0_
  10.9 0.6 collective-permute-start
  11.5 0.1 pad_maximum_fusion.1
  11.7 0.1 mul.20
  11.8 1.3 %collective-permute-done.1 = bf16[2,4,1536]{2,1,0:T(4,128)(2,1)S(1)} collective-permute-done((bf16[2,4,1536]{2,1,0:T(4,128)(2,1)S(1)}, bf16[2,4,1536]{2,1,0:T(4,128)(2,1)S(1)}, u32[]{:S(2)}, u32[]{:S(2)}) %collective-permute-start.1) | collective-permute-done | bytes 24608 | tf_op jit(solution)/shard_map/ppermute | solution.py:21
  13.2 1.6 %collective-permute-start.3 = (bf16[2,8,1536]{2,1,0:T(8,128)(2,1)S(1)}, bf16[2,8,1536]{2,1,0:T(8,128)(2,1)S(1)}, u32[]{:S(2)}, u32[]{:S(2)}) collective-permute-start(bf16[2,8,1536]{2,1,0:T(8,128)(2,1)S(1)} %pad_maximum_fusion), channel_id=1, source_target_pairs={{0,4},{4,0},{8,12},{12,8},{1,5},{5,1},{9,13},{13,9},{2,6},{6,2},{1... | collective-permute-start | bytes 147464 | tf_op jit(solution)/shard_map/ppermute | solution.py:21
  14.9 0.5 collective-permute-start.2
  15.4 0.6 copy-done.10
  16.1 0.4 sine_multiply_fusion
  16.5 0.3 copy-done.7
  16.8 0.7 shard_map.159
  17.5 1.5 %collective-permute-done.2 = bf16[2,8,1536]{2,1,0:T(8,128)(2,1)S(1)} collective-permute-done((bf16[2,8,1536]{2,1,0:T(8,128)(2,1)S(1)}, bf16[2,8,1536]{2,1,0:T(8,128)(2,1)S(1)}, u32[]{:S(2)}, u32[]{:S(2)}) %collective-permute-start.2) | collective-permute-done | bytes 49184 | tf_op jit(solution)/shard_map/ppermute | solution.py:21
  19.0 3.7 %all-to-all-done = bf16[4,160,384]{2,1,0:T(8,128)(2,1)S(1)} async-done(((bf16[4,160,384]{2,1,0:T(8,128)(2,1)}), bf16[4,160,384]{2,1,0:T(8,128)(2,1)S(1)}, u32[]{:S(2)}, u32[]{:S(2)}) %all-to-all-start) | async-done | bytes 491552 | tf_op jit(solution)/shard_map/all_to_all | solution.py:349
  22.7 1.5 %collective-permute-start.7 = (bf16[640,384]{1,0:T(8,128)(2,1)S(1)}, bf16[640,384]{1,0:T(8,128)(2,1)S(1)}, u32[]{:S(2)}, u32[]{:S(2)}) collective-permute-start(bf16[640,384]{1,0:T(8,128)(2,1)S(1)} %bitcast.5), channel_id=1, source_target_pairs={{0,8},{4,12},{8,0},{12,4},{1,9},{5,13},{9,1},{13,5},{2,10},{6,14},... | collective-permute-start | bytes 1474568 | tf_op jit(solution)/shard_map/ppermute | solution.py:21
  24.3 2.0 %collective-permute-start.8 = (bf16[160,384]{1,0:T(8,128)(2,1)S(1)}, bf16[160,384]{1,0:T(8,128)(2,1)S(1)}, u32[]{:S(2)}, u32[]{:S(2)}) collective-permute-start(bf16[160,384]{1,0:T(8,128)(2,1)S(1)} %get-tuple-element.55), channel_id=1, source_target_pairs={{0,2},{1,3},{2,0},{3,1},{4,6},{5,7},{6,4},{7,5},{8,10},{9,11},{10,... | collective-permute-start | bytes 368648 | tf_op jit(solution)/shard_map/ppermute | solution.py:21
  26.3 2.4 %collective-permute-start.6 = (bf16[160,384]{1,0:T(8,128)(2,1)S(1)}, bf16[160,384]{1,0:T(8,128)(2,1)S(1)}, u32[]{:S(2)}, u32[]{:S(2)}) collective-permute-start(bf16[160,384]{1,0:T(8,128)(2,1)S(1)} %get-tuple-element.50), channel_id=1, source_target_pairs={{0,3},{1,2},{2,1},{3,0},{4,7},{5,6},{6,5},{7,4},{8,11},{9,10},{10,... | collective-permute-start | bytes 368648 | tf_op jit(solution)/shard_map/ppermute | solution.py:21
  28.7 1.9 %shard_map.162 = (bf16[160,1536]{1,0:T(8,128)(2,1)}, f32[2,4,4,1536]{3,2,1,0:T(4,128)S(1)}, f32[2,4,4,1536]{3,2,1,0:T(4,128)S(1)}) custom-call(f32[160,2]{1,0:T(8,128)S(1)} %shard_map.157.refs_0_, f32[160,2]{1,0:T(8,128)S(1)} %collective-permute-done.refs_1_, bf16[160,1536]{1,0:T(8,128)(2,1)S(1)} %copy-done, f32[1,1536]{1,0:T(1,128)S(1)} %broadcast_in_dim.64.refs_3_, ...), custom_call_target="tpu_custom_call" | custom-call | flops 1000 | bytes 1000 | tf_op jit(solution)/shard_map/pallas_call | solution.py:316
  30.6 1.5 %collective-permute-start.11 = (f32[2,4,4,1536]{3,2,1,0:T(4,128)S(1)}, f32[2,4,4,1536]{3,2,1,0:T(4,128)S(1)}, u32[]{:S(2)}, u32[]{:S(2)}) collective-permute-start(f32[2,4,4,1536]{3,2,1,0:T(4,128)S(1)} %get-tuple-element.60), channel_id=1, source_target_pairs={{0,16},{16,0},{1,17},{17,1},{2,18},{18,2},{3,19},{19,3},{4,20},{20... | collective-permute-start | bytes 589832 | tf_op jit(solution)/shard_map/ppermute | solution.py:21
  32.1 0.7 shard_map.160
  32.8 2.2 %collective-permute-done.7.refs_6_ = bf16[640,384]{1,0:T(8,128)(2,1)S(1)} collective-permute-done((bf16[640,384]{1,0:T(8,128)(2,1)S(1)}, bf16[640,384]{1,0:T(8,128)(2,1)S(1)}, u32[]{:S(2)}, u32[]{:S(2)}) %collective-permute-start.7) | collective-permute-done | bytes 491552 | tf_op jit(solution)/shard_map/ppermute | solution.py:21
  34.9 0.9 %collective-permute-done.8.refs_1_ = bf16[160,384]{1,0:T(8,128)(2,1)S(1)} collective-permute-done((bf16[160,384]{1,0:T(8,128)(2,1)S(1)}, bf16[160,384]{1,0:T(8,128)(2,1)S(1)}, u32[]{:S(2)}, u32[]{:S(2)}) %collective-permute-start.8) | collective-permute-done | bytes 122912 | tf_op jit(solution)/shard_map/ppermute | solution.py:21
  35.9 0.7 collective-permute-start.10
  36.7 1.3 %collective-permute-start.5 = (bf16[160,384]{1,0:T(8,128)(2,1)S(1)}, bf16[160,384]{1,0:T(8,128)(2,1)S(1)}, u32[]{:S(2)}, u32[]{:S(2)}) collective-permute-start(bf16[160,384]{1,0:T(8,128)(2,1)S(1)} %get-tuple-element.49), channel_id=1, source_target_pairs={{0,3},{1,2},{2,1},{3,0},{4,7},{5,6},{6,5},{7,4},{8,11},{9,10},{10,... | collective-permute-start | bytes 368648 | tf_op jit(solution)/shard_map/ppermute | solution.py:21
  38.0 1.0 %collective-permute-start.14 = (bf16[160,384]{1,0:T(8,128)(2,1)S(1)}, bf16[160,384]{1,0:T(8,128)(2,1)S(1)}, u32[]{:S(2)}, u32[]{:S(2)}) collective-permute-start(bf16[160,384]{1,0:T(8,128)(2,1)S(1)} %get-tuple-element.52), channel_id=1, source_target_pairs={{0,1},{1,0},{2,3},{3,2},{4,5},{5,4},{6,7},{7,6},{8,9},{9,8},{10,11... | collective-permute-start | bytes 368648 | tf_op jit(solution)/shard_map/ppermute | solution.py:21
  39.0 2.1 %collective-permute-start.15 = (bf16[160,384]{1,0:T(8,128)(2,1)S(1)}, bf16[160,384]{1,0:T(8,128)(2,1)S(1)}, u32[]{:S(2)}, u32[]{:S(2)}) collective-permute-start(bf16[160,384]{1,0:T(8,128)(2,1)S(1)} %get-tuple-element.53), channel_id=1, source_target_pairs={{0,2},{1,3},{2,0},{3,1},{4,6},{5,7},{6,4},{7,5},{8,10},{9,11},{10,... | collective-permute-start | bytes 368648 | tf_op jit(solution)/shard_map/ppermute | solution.py:21
  41.2 1.4 %collective-permute-start.13 = (f32[4,1,4,1536]{3,2,1,0:T(4,128)S(1)}, f32[4,1,4,1536]{3,2,1,0:T(4,128)S(1)}, u32[]{:S(2)}, u32[]{:S(2)}) collective-permute-start(f32[4,1,4,1536]{3,2,1,0:T(4,128)S(1)} %get-tuple-element.65), channel_id=1, source_target_pairs={{0,8},{4,12},{8,0},{12,4},{1,9},{5,13},{9,1},{13,5},{2,10},{6,14},... | collective-permute-start | bytes 294920 | tf_op jit(solution)/shard_map/ppermute | solution.py:21
  42.6 5.8 %collective-permute-done.13.y_ref = f32[4,1,4,1536]{3,2,1,0:T(4,128)S(1)} collective-permute-done((f32[4,1,4,1536]{3,2,1,0:T(4,128)S(1)}, f32[4,1,4,1536]{3,2,1,0:T(4,128)S(1)}, u32[]{:S(2)}, u32[]{:S(2)}) %collective-permute-start.13) | collective-permute-done | bytes 98336 | tf_op jit(solution)/shard_map/ppermute | solution.py:21
  48.5 0.6 collective-permute-start.17
  49.0 0.1 collective-permute-start.18
  49.1 2.4 %collective-permute-done.15.q_ref = bf16[160,384]{1,0:T(8,128)(2,1)S(1)} collective-permute-done((bf16[160,384]{1,0:T(8,128)(2,1)S(1)}, bf16[160,384]{1,0:T(8,128)(2,1)S(1)}, u32[]{:S(2)}, u32[]{:S(2)}) %collective-permute-start.15) | collective-permute-done | bytes 122912 | tf_op jit(solution)/shard_map/ppermute | solution.py:21
  51.5 1.1 %collective-permute-start.23 = (f32[4,1,4,1536]{3,2,1,0:T(4,128)S(1)}, f32[4,1,4,1536]{3,2,1,0:T(4,128)S(1)}, u32[]{:S(2)}, u32[]{:S(2)}) collective-permute-start(f32[4,1,4,1536]{3,2,1,0:T(4,128)S(1)} %shard_map.165.x_ref), channel_id=1, source_target_pairs={{0,2},{1,3},{2,0},{3,1},{4,6},{5,7},{6,4},{7,5},{8,10},{9,11},{10,... | collective-permute-start | bytes 294920 | tf_op jit(solution)/shard_map/ppermute | solution.py:21
  52.6 0.8 %collective-permute-done.16.refs_0_ = bf16[640,384]{1,0:T(8,128)(2,1)S(1)} collective-permute-done((bf16[640,384]{1,0:T(8,128)(2,1)S(1)}, bf16[640,384]{1,0:T(8,128)(2,1)S(1)}, u32[]{:S(2)}, u32[]{:S(2)}) %collective-permute-start.16) | collective-permute-done | bytes 491552 | tf_op jit(solution)/shard_map/ppermute | solution.py:21
  53.4 1.9 %shard_map.167 = bf16[160,384]{1,0:T(8,128)(2,1)S(1)} custom-call(bf16[160,384]{1,0:T(8,128)(2,1)S(1)} %collective-permute-done.15.q_ref, bf16[640,384]{1,0:T(8,128)(2,1)S(1)} %collective-permute-done.16.refs_0_, bf16[640,384]{1,0:T(8,128)(2,1)S(1)} %collective-permute-done.17.refs_1_, bf16[640,384]{1,0:T(8,128)(2,1)S(1)} %collective-permute-done.10.refs_2_, ...), custom_call_target="tpu_custom_call" | custom-call | tf_op jit(solution)/shard_map/pallas_call | solution.py:274
  55.3 2.1 %collective-permute-start.21 = (bf16[160,384]{1,0:T(8,128)(2,1)S(1)}, bf16[160,384]{1,0:T(8,128)(2,1)S(1)}, u32[]{:S(2)}, u32[]{:S(2)}) collective-permute-start(bf16[160,384]{1,0:T(8,128)(2,1)S(1)} %shard_map.167), channel_id=1, source_target_pairs={{0,2},{1,3},{2,0},{3,1},{4,6},{5,7},{6,4},{7,5},{8,10},{9,11},{10,... | collective-permute-start | bytes 368648 | tf_op jit(solution)/shard_map/ppermute | solution.py:21
  57.4 1.9 %shard_map.168 = bf16[160,384]{1,0:T(8,128)(2,1)S(1)} custom-call(bf16[160,384]{1,0:T(8,128)(2,1)S(1)} %collective-permute-done.14.q_ref, bf16[640,384]{1,0:T(8,128)(2,1)S(1)} %collective-permute-done.16.refs_0_, bf16[640,384]{1,0:T(8,128)(2,1)S(1)} %collective-permute-done.17.refs_1_, bf16[640,384]{1,0:T(8,128)(2,1)S(1)} %collective-permute-done.10.refs_2_, ...), custom_call_target="tpu_custom_call" | custom-call | tf_op jit(solution)/shard_map/pallas_call | solution.py:274
  59.4 1.9 %shard_map.166 = bf16[160,384]{1,0:T(8,128)(2,1)S(1)} custom-call(bf16[160,384]{1,0:T(8,128)(2,1)S(1)} %collective-permute-done.5.q_ref, bf16[640,384]{1,0:T(8,128)(2,1)S(1)} %collective-permute-done.16.refs_0_, bf16[640,384]{1,0:T(8,128)(2,1)S(1)} %collective-permute-done.17.refs_1_, bf16[640,384]{1,0:T(8,128)(2,1)S(1)} %collective-permute-done.10.refs_2_, ...), custom_call_target="tpu_custom_call" | custom-call | tf_op jit(solution)/shard_map/pallas_call | solution.py:274
  61.4 2.4 %collective-permute-start.20 = (bf16[160,384]{1,0:T(8,128)(2,1)S(1)}, bf16[160,384]{1,0:T(8,128)(2,1)S(1)}, u32[]{:S(2)}, u32[]{:S(2)}) collective-permute-start(bf16[160,384]{1,0:T(8,128)(2,1)S(1)} %shard_map.166), channel_id=1, source_target_pairs={{0,3},{1,2},{2,1},{3,0},{4,7},{5,6},{6,5},{7,4},{8,11},{9,10},{10,... | collective-permute-start | bytes 368648 | tf_op jit(solution)/shard_map/ppermute | solution.py:21
  63.7 1.0 %collective-permute-start.24 = (f32[4,1,4,1536]{3,2,1,0:T(4,128)S(1)}, f32[4,1,4,1536]{3,2,1,0:T(4,128)S(1)}, u32[]{:S(2)}, u32[]{:S(2)}) collective-permute-start(f32[4,1,4,1536]{3,2,1,0:T(4,128)S(1)} %shard_map.171.first_ref), channel_id=1, source_target_pairs={{0,1},{1,0},{2,3},{3,2},{4,5},{5,4},{6,7},{7,6},{8,9},{9,8},{10,11... | collective-permute-start | bytes 294920 | tf_op jit(solution)/shard_map/ppermute | solution.py:21
  64.7 1.9 %shard_map.169.refs_3_ = bf16[160,384]{1,0:T(8,128)(2,1)S(1)} custom-call(bf16[160,384]{1,0:T(8,128)(2,1)S(1)} %get-tuple-element.51.q_ref, bf16[640,384]{1,0:T(8,128)(2,1)S(1)} %collective-permute-done.16.refs_0_, bf16[640,384]{1,0:T(8,128)(2,1)S(1)} %collective-permute-done.17.refs_1_, bf16[640,384]{1,0:T(8,128)(2,1)S(1)} %collective-permute-done.10.refs_2_, ...), custom_call_target="tpu_custom_call" | custom-call | tf_op jit(solution)/shard_map/pallas_call | solution.py:274
  66.6 2.9 %collective-permute-done.22.refs_2_ = bf16[160,384]{1,0:T(8,128)(2,1)S(1)} collective-permute-done((bf16[160,384]{1,0:T(8,128)(2,1)S(1)}, bf16[160,384]{1,0:T(8,128)(2,1)S(1)}, u32[]{:S(2)}, u32[]{:S(2)}) %collective-permute-start.22) | collective-permute-done | bytes 122912 | tf_op jit(solution)/shard_map/ppermute | solution.py:21
  69.5 0.8 %shard_map.170 = bf16[160,1536]{1,0:T(8,128)(2,1)} custom-call(bf16[160,384]{1,0:T(8,128)(2,1)S(1)} %collective-permute-done.20.refs_0_, bf16[160,384]{1,0:T(8,128)(2,1)S(1)} %collective-permute-done.21.refs_1_, bf16[160,384]{1,0:T(8,128)(2,1)S(1)} %collective-permute-done.22.refs_2_, bf16[160,384]{1,0:T(8,128)(2,1)S(1)} %shard_map.169.refs_3_), custom_call_target="tpu_custom_call" | custom-call | tf_op jit(solution)/shard_map/pallas_call | solution.py:101
  70.3 0.8 %collective-permute-done.24.second_ref = f32[4,1,4,1536]{3,2,1,0:T(4,128)S(1)} collective-permute-done((f32[4,1,4,1536]{3,2,1,0:T(4,128)S(1)}, f32[4,1,4,1536]{3,2,1,0:T(4,128)S(1)}, u32[]{:S(2)}, u32[]{:S(2)}) %collective-permute-start.24) | collective-permute-done | bytes 98336 | tf_op jit(solution)/shard_map/ppermute | solution.py:21
  71.1 0.8 %shard_map.172 = (f32[4,3072]{1,0:T(4,128)}, f32[4,3072]{1,0:T(4,128)}) custom-call(bf16[4,3072]{1,0:T(4,128)(2,1)S(1)} %copy-done.4, f32[1,3072]{1,0:T(1,128)S(1)} %bitcast.12, f32[4,1,4,1536]{3,2,1,0:T(4,128)S(1)} %shard_map.171.first_ref, f32[4,1,4,1536]{3,2,1,0:T(4,128)S(1)} %collective-permute-done.24.second_ref), custom_call_target="tpu_custom_call" | custom-call | tf_op jit(solution)/shard_map/pallas_call | solution.py:170
  (59 shorter events, 0.7 us)
Async XLA Ops:
  0.6 1.0 %copy-start.2 = (bf16[160,1536]{1,0:T(8,128)(2,1)S(1)}, bf16[160,1536]{1,0:T(8,128)(2,1)}, u32[]{:S(2)}) copy-start(bf16[160,1536]{1,0:T(8,128)(2,1)} %x_ref.1) | copy-start | bytes 1474564
  1.7 7.3 %copy-start.4 = (bf16[4,3072]{1,0:T(4,128)(2,1)S(1)}, bf16[4,3072]{1,0:T(4,128)(2,1)}, u32[]{:S(2)}) copy-start(bf16[4,3072]{1,0:T(4,128)(2,1)} %k_ref.4) | copy-start | bytes 73732
  1.7 7.3 %copy-start.5 = (f32[3072]{0:T(1024)S(1)}, f32[3072]{0:T(1024)}, u32[]{:S(2)}) copy-start(f32[3072]{0:T(1024)} %param.21) | copy-start | bytes 36868
  1.7 7.3 %copy-start.6 = (bf16[4,3072]{1,0:T(4,128)(2,1)S(1)}, bf16[4,3072]{1,0:T(4,128)(2,1)}, u32[]{:S(2)}) copy-start(bf16[4,3072]{1,0:T(4,128)(2,1)} %v_ref.1) | copy-start | bytes 73732
  2.5 8.2 %copy-start = (bf16[160,1536]{1,0:T(8,128)(2,1)S(1)}, bf16[160,1536]{1,0:T(8,128)(2,1)}, u32[]{:S(2)}) copy-start(bf16[160,1536]{1,0:T(8,128)(2,1)} %refs_2_.4) | copy-start | bytes 1474564
  2.5 8.2 %copy-start.1 = (bf16[160,1536]{1,0:T(8,128)(2,1)S(1)}, bf16[160,1536]{1,0:T(8,128)(2,1)}, u32[]{:S(2)}) copy-start(bf16[160,1536]{1,0:T(8,128)(2,1)} %refs_2_.2) | copy-start | bytes 1474564
  2.5 20.2 %all-to-all-start = ((bf16[4,160,384]{2,1,0:T(8,128)(2,1)}), bf16[4,160,384]{2,1,0:T(8,128)(2,1)S(1)}, u32[]{:S(2)}, u32[]{:S(2)}) async-start(bf16[4,160,384]{2,1,0:T(8,128)(2,1)} %shard_map.156), calls=%async_computation | async-start | bytes 983040 | tf_op jit(solution)/shard_map/all_to_all | solution.py:349
  9.1 4.0 %collective-permute-start.1 = (bf16[2,4,1536]{2,1,0:T(4,128)(2,1)S(1)}, bf16[2,4,1536]{2,1,0:T(4,128)(2,1)S(1)}, u32[]{:S(2)}, u32[]{:S(2)}) collective-permute-start(bf16[2,4,1536]{2,1,0:T(4,128)(2,1)S(1)} %get-tuple-element.41), channel_id=1, source_target_pairs={{0,16},{16,0},{1,17},{17,1},{2,18},{18,2},{3,19},{19,3},{4,20},{20... | collective-permute-start | bytes 73736 | tf_op jit(solution)/shard_map/ppermute | solution.py:21
  10.6 0.9 %copy-start.9 = (s32[160,3]{0,1:T(4,128)S(1)}, s32[160,3]{0,1:T(4,128)}, u32[]{:S(2)}) copy-start(s32[160,3]{0,1:T(4,128)} %param.16) | copy-start | bytes 5764
  10.9 5.8 %collective-permute-start = (f32[160,2]{1,0:T(8,128)S(1)}, f32[160,2]{1,0:T(8,128)S(1)}, u32[]{:S(2)}, u32[]{:S(2)}) collective-permute-start(f32[160,2]{1,0:T(8,128)S(1)} %shard_map.157.refs_0_), channel_id=1, source_target_pairs={{0,16},{16,0},{1,17},{17,1},{2,18},{18,2},{3,19},{19,3},{4,20},{20... | collective-permute-start | bytes 3848 | tf_op jit(solution)/shard_map/ppermute | solution.py:21
  13.2 4.3 %collective-permute-start.4 = (bf16[2,8,1536]{2,1,0:T(8,128)(2,1)S(1)}, bf16[2,8,1536]{2,1,0:T(8,128)(2,1)S(1)}, u32[]{:S(2)}, u32[]{:S(2)}) collective-permute-start(bf16[2,8,1536]{2,1,0:T(8,128)(2,1)S(1)} %pad_maximum_fusion), channel_id=1, source_target_pairs={{0,12},{4,8},{8,4},{12,0},{1,13},{5,9},{9,5},{13,1},{2,14},{6,10},... | collective-permute-start | bytes 147464 | tf_op jit(solution)/shard_map/ppermute | solution.py:21
  13.2 4.2 %collective-permute-start.3 = (bf16[2,8,1536]{2,1,0:T(8,128)(2,1)S(1)}, bf16[2,8,1536]{2,1,0:T(8,128)(2,1)S(1)}, u32[]{:S(2)}, u32[]{:S(2)}) collective-permute-start(bf16[2,8,1536]{2,1,0:T(8,128)(2,1)S(1)} %pad_maximum_fusion), channel_id=1, source_target_pairs={{0,4},{4,0},{8,12},{12,8},{1,5},{5,1},{9,13},{13,9},{2,6},{6,2},{1... | collective-permute-start | bytes 147464 | tf_op jit(solution)/shard_map/ppermute | solution.py:21
  14.9 4.1 %collective-permute-start.2 = (bf16[2,8,1536]{2,1,0:T(8,128)(2,1)S(1)}, bf16[2,8,1536]{2,1,0:T(8,128)(2,1)S(1)}, u32[]{:S(2)}, u32[]{:S(2)}) collective-permute-start(bf16[2,8,1536]{2,1,0:T(8,128)(2,1)S(1)} %pad_maximum_fusion), channel_id=1, source_target_pairs={{0,8},{4,12},{8,0},{12,4},{1,9},{5,13},{9,1},{13,5},{2,10},{6,14},... | collective-permute-start | bytes 147464 | tf_op jit(solution)/shard_map/ppermute | solution.py:21
  15.4 0.7 copy-start.10
  15.4 0.7 copy-start.11
  15.4 0.7 copy-start.12
  16.1 0.7 copy-start.7
  16.8 11.9 %copy-start.3 = (bf16[160,1536]{1,0:T(8,128)(2,1)S(1)}, bf16[160,1536]{1,0:T(8,128)(2,1)}, u32[]{:S(2)}) copy-start(bf16[160,1536]{1,0:T(8,128)(2,1)} %refs_5_.1) | copy-start | bytes 1474564
  19.0 9.7 %copy-start.8 = (f32[1536]{0:T(1024)S(1)}, f32[1536]{0:T(1024)}, u32[]{:S(2)}) copy-start(f32[1536]{0:T(1024)} %param.17) | copy-start | bytes 18436
  22.7 12.2 %collective-permute-start.7 = (bf16[640,384]{1,0:T(8,128)(2,1)S(1)}, bf16[640,384]{1,0:T(8,128)(2,1)S(1)}, u32[]{:S(2)}, u32[]{:S(2)}) collective-permute-start(bf16[640,384]{1,0:T(8,128)(2,1)S(1)} %bitcast.5), channel_id=1, source_target_pairs={{0,8},{4,12},{8,0},{12,4},{1,9},{5,13},{9,1},{13,5},{2,10},{6,14},... | collective-permute-start | bytes 1474568 | tf_op jit(solution)/shard_map/ppermute | solution.py:21
  24.3 8.5 %collective-permute-start.9 = (bf16[160,384]{1,0:T(8,128)(2,1)S(1)}, bf16[160,384]{1,0:T(8,128)(2,1)S(1)}, u32[]{:S(2)}, u32[]{:S(2)}) collective-permute-start(bf16[160,384]{1,0:T(8,128)(2,1)S(1)} %get-tuple-element.57), channel_id=1, source_target_pairs={{0,1},{1,0},{2,3},{3,2},{4,5},{5,4},{6,7},{7,6},{8,9},{9,8},{10,11... | collective-permute-start | bytes 368648 | tf_op jit(solution)/shard_map/ppermute | solution.py:21
  24.3 11.5 %collective-permute-start.8 = (bf16[160,384]{1,0:T(8,128)(2,1)S(1)}, bf16[160,384]{1,0:T(8,128)(2,1)S(1)}, u32[]{:S(2)}, u32[]{:S(2)}) collective-permute-start(bf16[160,384]{1,0:T(8,128)(2,1)S(1)} %get-tuple-element.55), channel_id=1, source_target_pairs={{0,2},{1,3},{2,0},{3,1},{4,6},{5,7},{6,4},{7,5},{8,10},{9,11},{10,... | collective-permute-start | bytes 368648 | tf_op jit(solution)/shard_map/ppermute | solution.py:21
  26.3 9.5 %collective-permute-start.6 = (bf16[160,384]{1,0:T(8,128)(2,1)S(1)}, bf16[160,384]{1,0:T(8,128)(2,1)S(1)}, u32[]{:S(2)}, u32[]{:S(2)}) collective-permute-start(bf16[160,384]{1,0:T(8,128)(2,1)S(1)} %get-tuple-element.50), channel_id=1, source_target_pairs={{0,3},{1,2},{2,1},{3,0},{4,7},{5,6},{6,5},{7,4},{8,11},{9,10},{10,... | collective-permute-start | bytes 368648 | tf_op jit(solution)/shard_map/ppermute | solution.py:21
  30.6 6.0 %collective-permute-start.11 = (f32[2,4,4,1536]{3,2,1,0:T(4,128)S(1)}, f32[2,4,4,1536]{3,2,1,0:T(4,128)S(1)}, u32[]{:S(2)}, u32[]{:S(2)}) collective-permute-start(f32[2,4,4,1536]{3,2,1,0:T(4,128)S(1)} %get-tuple-element.60), channel_id=1, source_target_pairs={{0,16},{16,0},{1,17},{17,1},{2,18},{18,2},{3,19},{19,3},{4,20},{20... | collective-permute-start | bytes 589832 | tf_op jit(solution)/shard_map/ppermute | solution.py:21
  35.9 15.6 %collective-permute-start.10 = (bf16[640,384]{1,0:T(8,128)(2,1)S(1)}, bf16[640,384]{1,0:T(8,128)(2,1)S(1)}, u32[]{:S(2)}, u32[]{:S(2)}) collective-permute-start(bf16[640,384]{1,0:T(8,128)(2,1)S(1)} %shard_map.161.refs_3_), channel_id=1, source_target_pairs={{0,8},{4,12},{8,0},{12,4},{1,9},{5,13},{9,1},{13,5},{2,10},{6,14},... | collective-permute-start | bytes 1474568 | tf_op jit(solution)/shard_map/ppermute | solution.py:21
  36.6 4.5 %collective-permute-start.12 = (f32[4,2,4,1536]{3,2,1,0:T(4,128)S(1)}, f32[4,2,4,1536]{3,2,1,0:T(4,128)S(1)}, u32[]{:S(2)}, u32[]{:S(2)}) collective-permute-start(f32[4,2,4,1536]{3,2,1,0:T(4,128)S(1)} %get-tuple-element.62), channel_id=1, source_target_pairs={{0,4},{4,0},{8,12},{12,8},{1,5},{5,1},{9,13},{13,9},{2,6},{6,2},{1... | collective-permute-start | bytes 589832 | tf_op jit(solution)/shard_map/ppermute | solution.py:21
  36.7 11.8 %collective-permute-start.5 = (bf16[160,384]{1,0:T(8,128)(2,1)S(1)}, bf16[160,384]{1,0:T(8,128)(2,1)S(1)}, u32[]{:S(2)}, u32[]{:S(2)}) collective-permute-start(bf16[160,384]{1,0:T(8,128)(2,1)S(1)} %get-tuple-element.49), channel_id=1, source_target_pairs={{0,3},{1,2},{2,1},{3,0},{4,7},{5,6},{6,5},{7,4},{8,11},{9,10},{10,... | collective-permute-start | bytes 368648 | tf_op jit(solution)/shard_map/ppermute | solution.py:21
  38.0 11.0 %collective-permute-start.14 = (bf16[160,384]{1,0:T(8,128)(2,1)S(1)}, bf16[160,384]{1,0:T(8,128)(2,1)S(1)}, u32[]{:S(2)}, u32[]{:S(2)}) collective-permute-start(bf16[160,384]{1,0:T(8,128)(2,1)S(1)} %get-tuple-element.52), channel_id=1, source_target_pairs={{0,1},{1,0},{2,3},{3,2},{4,5},{5,4},{6,7},{7,6},{8,9},{9,8},{10,11... | collective-permute-start | bytes 368648 | tf_op jit(solution)/shard_map/ppermute | solution.py:21
  39.0 12.5 %collective-permute-start.15 = (bf16[160,384]{1,0:T(8,128)(2,1)S(1)}, bf16[160,384]{1,0:T(8,128)(2,1)S(1)}, u32[]{:S(2)}, u32[]{:S(2)}) collective-permute-start(bf16[160,384]{1,0:T(8,128)(2,1)S(1)} %get-tuple-element.53), channel_id=1, source_target_pairs={{0,2},{1,3},{2,0},{3,1},{4,6},{5,7},{6,4},{7,5},{8,10},{9,11},{10,... | collective-permute-start | bytes 368648 | tf_op jit(solution)/shard_map/ppermute | solution.py:21
  41.2 7.3 %collective-permute-start.13 = (f32[4,1,4,1536]{3,2,1,0:T(4,128)S(1)}, f32[4,1,4,1536]{3,2,1,0:T(4,128)S(1)}, u32[]{:S(2)}, u32[]{:S(2)}) collective-permute-start(f32[4,1,4,1536]{3,2,1,0:T(4,128)S(1)} %get-tuple-element.65), channel_id=1, source_target_pairs={{0,8},{4,12},{8,0},{12,4},{1,9},{5,13},{9,1},{13,5},{2,10},{6,14},... | collective-permute-start | bytes 294920 | tf_op jit(solution)/shard_map/ppermute | solution.py:21
  48.4 4.2 %collective-permute-start.19 = (bf16[640,384]{1,0:T(8,128)(2,1)S(1)}, bf16[640,384]{1,0:T(8,128)(2,1)S(1)}, u32[]{:S(2)}, u32[]{:S(2)}) collective-permute-start(bf16[640,384]{1,0:T(8,128)(2,1)S(1)} %bitcast.6), channel_id=1, source_target_pairs={{0,4},{4,0},{8,12},{12,8},{1,5},{5,1},{9,13},{13,9},{2,6},{6,2},{1... | collective-permute-start | bytes 1474568 | tf_op jit(solution)/shard_map/ppermute | solution.py:21
  48.5 4.1 %collective-permute-start.17 = (bf16[640,384]{1,0:T(8,128)(2,1)S(1)}, bf16[640,384]{1,0:T(8,128)(2,1)S(1)}, u32[]{:S(2)}, u32[]{:S(2)}) collective-permute-start(bf16[640,384]{1,0:T(8,128)(2,1)S(1)} %shard_map.161.refs_3_), channel_id=1, source_target_pairs={{0,4},{4,0},{8,12},{12,8},{1,5},{5,1},{9,13},{13,9},{2,6},{6,2},{1... | collective-permute-start | bytes 1474568 | tf_op jit(solution)/shard_map/ppermute | solution.py:21
  49.0 3.6 %collective-permute-start.18 = (bf16[640,384]{1,0:T(8,128)(2,1)S(1)}, bf16[640,384]{1,0:T(8,128)(2,1)S(1)}, u32[]{:S(2)}, u32[]{:S(2)}) collective-permute-start(bf16[640,384]{1,0:T(8,128)(2,1)S(1)} %collective-permute-done.7.refs_6_), channel_id=1, source_target_pairs={{0,4},{4,0},{8,12},{12,8},{1,5},{5,1},{9,13},{13,9},{2,6},{6,2},{1... | collective-permute-start | bytes 1474568 | tf_op jit(solution)/shard_map/ppermute | solution.py:21
  51.5 1.9 %collective-permute-start.16 = (bf16[640,384]{1,0:T(8,128)(2,1)S(1)}, bf16[640,384]{1,0:T(8,128)(2,1)S(1)}, u32[]{:S(2)}, u32[]{:S(2)}) collective-permute-start(bf16[640,384]{1,0:T(8,128)(2,1)S(1)} %collective-permute-done.10.refs_2_), channel_id=1, source_target_pairs={{0,4},{4,0},{8,12},{12,8},{1,5},{5,1},{9,13},{13,9},{2,6},{6,2},{1... | collective-permute-start | bytes 1474568 | tf_op jit(solution)/shard_map/ppermute | solution.py:21
  51.5 12.2 %collective-permute-start.23 = (f32[4,1,4,1536]{3,2,1,0:T(4,128)S(1)}, f32[4,1,4,1536]{3,2,1,0:T(4,128)S(1)}, u32[]{:S(2)}, u32[]{:S(2)}) collective-permute-start(f32[4,1,4,1536]{3,2,1,0:T(4,128)S(1)} %shard_map.165.x_ref), channel_id=1, source_target_pairs={{0,2},{1,3},{2,0},{3,1},{4,6},{5,7},{6,4},{7,5},{8,10},{9,11},{10,... | collective-permute-start | bytes 294920 | tf_op jit(solution)/shard_map/ppermute | solution.py:21
  55.3 11.4 %collective-permute-start.21 = (bf16[160,384]{1,0:T(8,128)(2,1)S(1)}, bf16[160,384]{1,0:T(8,128)(2,1)S(1)}, u32[]{:S(2)}, u32[]{:S(2)}) collective-permute-start(bf16[160,384]{1,0:T(8,128)(2,1)S(1)} %shard_map.167), channel_id=1, source_target_pairs={{0,2},{1,3},{2,0},{3,1},{4,6},{5,7},{6,4},{7,5},{8,10},{9,11},{10,... | collective-permute-start | bytes 368648 | tf_op jit(solution)/shard_map/ppermute | solution.py:21
  59.3 10.2 %collective-permute-start.22 = (bf16[160,384]{1,0:T(8,128)(2,1)S(1)}, bf16[160,384]{1,0:T(8,128)(2,1)S(1)}, u32[]{:S(2)}, u32[]{:S(2)}) collective-permute-start(bf16[160,384]{1,0:T(8,128)(2,1)S(1)} %shard_map.168), channel_id=1, source_target_pairs={{0,1},{1,0},{2,3},{3,2},{4,5},{5,4},{6,7},{7,6},{8,9},{9,8},{10,11... | collective-permute-start | bytes 368648 | tf_op jit(solution)/shard_map/ppermute | solution.py:21
  61.4 8.2 %collective-permute-start.20 = (bf16[160,384]{1,0:T(8,128)(2,1)S(1)}, bf16[160,384]{1,0:T(8,128)(2,1)S(1)}, u32[]{:S(2)}, u32[]{:S(2)}) collective-permute-start(bf16[160,384]{1,0:T(8,128)(2,1)S(1)} %shard_map.166), channel_id=1, source_target_pairs={{0,3},{1,2},{2,1},{3,0},{4,7},{5,6},{6,5},{7,4},{8,11},{9,10},{10,... | collective-permute-start | bytes 368648 | tf_op jit(solution)/shard_map/ppermute | solution.py:21
  63.7 7.4 %collective-permute-start.24 = (f32[4,1,4,1536]{3,2,1,0:T(4,128)S(1)}, f32[4,1,4,1536]{3,2,1,0:T(4,128)S(1)}, u32[]{:S(2)}, u32[]{:S(2)}) collective-permute-start(f32[4,1,4,1536]{3,2,1,0:T(4,128)S(1)} %shard_map.171.first_ref), channel_id=1, source_target_pairs={{0,1},{1,0},{2,3},{3,2},{4,5},{5,4},{6,7},{7,6},{8,9},{9,8},{10,11... | collective-permute-start | bytes 294920 | tf_op jit(solution)/shard_map/ppermute | solution.py:21
